TPU v7x, 32 devices: a whole 2x2x4 slice. The times are simulated.
32 devices in a mesh: shard: 4 (over y, x), rep: 8 (over z, core).
Axes of the slice: x: 2, y: 2, z: 4, core: 2. Of those that a mesh axis runs over, the one named last changes fastest.
Arguments:
- tokens: bfloat16 [32768, 1024], P(('shard', 'rep')), may hold values from -6 to 6
- doc_ids: int32 [32, 1024], P(('shard', 'rep')), may hold values from 0 to 3, never falling along the last dimension, each value on 1 to 512 neighbouring positions
- w_query: bfloat16 [1024, 1024], P('shard'), may hold values from -0.1875 to 0.1875
- w_key: bfloat16 [1024, 512], P('shard'), may hold values from -0.1875 to 0.1875
- w_value: bfloat16 [1024, 512], P('shard'), may hold values from -0.1875 to 0.1875
- w_out: bfloat16 [1024, 1024], P('shard'), may hold values from -1.5 to 1.5
- w_gate: bfloat16 [1024, 4608], P('shard'), may hold values from -0.1875 to 0.1875
- w_up: bfloat16 [1024, 4608], P('shard'), may hold values from -0.1875 to 0.1875
- w_down: bfloat16 [4608, 1024], P('shard'), may hold values from -0.09375 to 0.09375
- attn_gain: bfloat16 [1024], P('shard'), may hold values from 0.25 to 1.75
- ffn_gain: bfloat16 [1024], P('shard'), may hold values from 0.25 to 1.75
- query_gain: bfloat16 [64], P('shard'), may hold values from 0.25 to 1.75
- key_gain: bfloat16 [64], P('shard'), may hold values from 0.25 to 1.75
- cotangent: bfloat16 [32768, 1024], P(('shard', 'rep')), may hold values from -6 to 6
Outputs:
- output: bfloat16 [32768, 1024], P(('shard', 'rep'))
- grad_tokens: float32 [32768, 1024], P(('shard', 'rep'))
- grad_w_query: float32 [1024, 1024], P('shard')
- grad_w_key: float32 [1024, 512], P('shard')
- grad_w_value: float32 [1024, 512], P('shard')
- grad_w_out: float32 [1024, 1024], P('shard')
- grad_w_gate: float32 [1024, 4608], P('shard')
- grad_w_up: float32 [1024, 4608], P('shard')
- grad_w_down: float32 [4608, 1024], P('shard')
- grad_attn_gain: float32 [1024], P('shard')
- grad_ffn_gain: float32 [1024], P('shard')
- grad_query_gain: float32 [64], P('shard')
- grad_key_gain: float32 [64], P('shard')
Inputs may be any that keep to these rules, and one draw needn't show every extreme that they name: `doc_ids`: within each row of 1024 positions the document numbers never fall; each document covers 1 to 512 positions.
All inputs are finite; a program needn't handle non-finite values.
Results may differ from a plain program's by a relative error of at most 0.03.
Values may be sent and summed in bfloat16 or wider, within the bound.
No kernel may reach another device: no remote copies, remote signals or barrier semaphores. Data moves between devices by JAX's collectives and lax.ppermute only.
A program may use at most 320 MiB of HBM per device.

v0:
```python
import jax
import jax.numpy as jnp
from jax import lax
from jax.sharding import PartitionSpec as P

HQ = 16
HK = 8
DH = 64
DOCS = 4


EPS = 1e-05
ROPE_BASE = 1000000.0


def outer_sum(first_op, second_op):
    return lax.dot_general(
        first_op, second_op, (((0,), (0,)), ((), ())), preferred_element_type=jnp.float32
    )


def back_dot(grad_rows, weight):
    return lax.dot_general(
        grad_rows, weight, (((1,), (1,)), ((), ())), preferred_element_type=jnp.float32
    )


def inverse_rms(values):
    return lax.rsqrt(jnp.mean(values * values, axis=-1, keepdims=True) + EPS)


def norm_back(grad_in, normed, inverse):
    return inverse * (grad_in - normed * jnp.mean(grad_in * normed, axis=-1, keepdims=True))


def doc_positions(doc_rows):
    kinds = jnp.arange(DOCS, dtype=jnp.int32)
    onehot = (doc_rows[:, :, None] == kinds[None, None, :]).astype(jnp.int32)
    counts = jnp.sum(onehot, axis=1)
    before = jnp.cumsum(counts, axis=1) - counts
    starts = jnp.sum(onehot * before[:, None, :], axis=2)
    return jnp.arange(doc_rows.shape[1], dtype=jnp.int32)[None, :] - starts


def rotate(values, cosine, sine):
    half = values.shape[-1] // 2
    first_half = values[..., :half]
    second_half = values[..., half:]
    return jnp.concatenate(
        [first_half * cosine - second_half * sine, second_half * cosine + first_half * sine],
        axis=-1,
    )


def unrotate(values, cosine, sine):
    half = values.shape[-1] // 2
    first_half = values[..., :half]
    second_half = values[..., half:]
    return jnp.concatenate(
        [first_half * cosine + second_half * sine, second_half * cosine - first_half * sine],
        axis=-1,
    )


def block_mask(doc_row, row_start, row_count):
    row_end = row_start + row_count
    query_ids = row_start + jnp.arange(row_count)[:, None]
    key_ids = jnp.arange(row_end)[None, :]
    same_doc = doc_row[row_start:row_end, None] == doc_row[None, :row_end]
    return (key_ids <= query_ids) & same_doc


def block_forward(query_blk, key_rows, value_rows, allowed):
    scores = jnp.einsum("qkgd,pkd->kgqp", query_blk, key_rows, preferred_element_type=jnp.float32)
    logits = jnp.where(allowed, scores * DH ** (-0.5), -1e30)
    row_max = jnp.max(logits, axis=-1, keepdims=True)
    exp_terms = jnp.exp(logits - row_max)
    totals = jnp.sum(exp_terms, axis=-1, keepdims=True)
    prob_low = (exp_terms / totals).astype(jnp.bfloat16)
    mixed = jnp.einsum("kgqp,pkd->qkgd", prob_low, value_rows, preferred_element_type=jnp.float32)
    return (mixed, row_max + jnp.log(totals))


def block_backward(query_blk, key_rows, value_rows, allowed, log_total, grad_mix):
    scores = jnp.einsum("qkgd,pkd->kgqp", query_blk, key_rows, preferred_element_type=jnp.float32)
    logits = jnp.where(allowed, scores * DH ** (-0.5), -1e30)
    attn_probs = jnp.exp(logits - log_total)
    prob_low = attn_probs.astype(jnp.bfloat16)
    grad_probs = jnp.einsum(
        "qkgd,pkd->kgqp", grad_mix, value_rows, preferred_element_type=jnp.float32
    )
    inner = jnp.sum(grad_probs * attn_probs, axis=-1, keepdims=True)
    grad_scores = (attn_probs * (grad_probs - inner) * DH ** (-0.5)).astype(jnp.bfloat16)
    grad_query = jnp.einsum(
        "kgqp,pkd->qkgd", grad_scores, key_rows, preferred_element_type=jnp.float32
    )
    grad_key = jnp.einsum(
        "kgqp,qkgd->pkd", grad_scores, query_blk, preferred_element_type=jnp.float32
    )
    grad_value = jnp.einsum(
        "kgqp,qkgd->pkd", prob_low, grad_mix, preferred_element_type=jnp.float32
    )
    return (grad_query, grad_key, grad_value)


def per_device(
    tokens,
    doc_ids,
    w_query,
    w_key,
    w_value,
    w_out,
    w_gate,
    w_up,
    w_down,
    attn_gain,
    ffn_gain,
    query_gain,
    key_gain,
    cotangent,
):
    full_set = (
        lax.all_gather(w_query, "shard", axis=0, tiled=True),
        lax.all_gather(w_key, "shard", axis=0, tiled=True),
        lax.all_gather(w_value, "shard", axis=0, tiled=True),
        lax.all_gather(w_out, "shard", axis=0, tiled=True),
        lax.all_gather(w_gate, "shard", axis=0, tiled=True),
        lax.all_gather(w_up, "shard", axis=0, tiled=True),
        lax.all_gather(w_down, "shard", axis=0, tiled=True),
        lax.all_gather(attn_gain, "shard", axis=0, tiled=True),
        lax.all_gather(ffn_gain, "shard", axis=0, tiled=True),
        lax.all_gather(query_gain, "shard", axis=0, tiled=True),
        lax.all_gather(key_gain, "shard", axis=0, tiled=True),
    )
    wq_full, wk_full, wv_full, wo_full, gate_full, up_full, down_full = (
        full_set[0],
        full_set[1],
        full_set[2],
        full_set[3],
        full_set[4],
        full_set[5],
        full_set[6],
    )
    gain_attn = full_set[7].astype(jnp.float32)
    gain_ffn = full_set[8].astype(jnp.float32)
    gain_query = full_set[9].astype(jnp.float32)
    gain_key = full_set[10].astype(jnp.float32)
    tok_count = tokens.shape[0]
    seq_len = doc_ids.shape[1]
    block_rows = min(512, seq_len)
    groups = HQ // HK
    x_in = tokens.astype(jnp.float32)
    inv_one = inverse_rms(x_in)
    x_hat = x_in * inv_one
    attn_in = (x_hat * gain_attn).astype(jnp.bfloat16)
    q_heads = jnp.dot(attn_in, wq_full, preferred_element_type=jnp.float32).reshape(
        tok_count, HQ, DH
    )
    k_heads = jnp.dot(attn_in, wk_full, preferred_element_type=jnp.float32).reshape(
        tok_count, HK, DH
    )
    v_low = jnp.dot(attn_in, wv_full, preferred_element_type=jnp.float32).astype(jnp.bfloat16)
    q_inv = inverse_rms(q_heads)
    q_hat = q_heads * q_inv
    k_inv = inverse_rms(k_heads)
    k_hat = k_heads * k_inv
    positions = doc_positions(doc_ids).reshape(tok_count)
    freqs = jnp.power(ROPE_BASE, -2.0 * jnp.arange(DH // 2, dtype=jnp.float32) / DH)
    angles = positions.astype(jnp.float32)[:, None] * freqs
    cosine = jnp.cos(angles)[:, None, :]
    sine = jnp.sin(angles)[:, None, :]
    q_rot = rotate(q_hat * gain_query, cosine, sine).astype(jnp.bfloat16)
    k_rot = rotate(k_hat * gain_key, cosine, sine).astype(jnp.bfloat16)
    q_group = q_rot.reshape(tok_count, HK, groups, DH)
    v_heads = v_low.reshape(tok_count, HK, DH)
    mixed_parts = []
    log_totals = []
    number = 0
    seq_base = number * seq_len
    for row_start in range(0, seq_len, block_rows):
        row_end = row_start + block_rows
        allowed = block_mask(doc_ids[number], row_start, block_rows)
        mixed, log_total = block_forward(
            q_group[seq_base + row_start : seq_base + row_end],
            k_rot[seq_base : seq_base + row_end],
            v_heads[seq_base : seq_base + row_end],
            allowed,
        )
        mixed_parts.append(mixed)
        log_totals.append(log_total)
    mix_low = jnp.concatenate(mixed_parts, axis=0).reshape(tok_count, HQ * DH).astype(jnp.bfloat16)
    resid = x_in + jnp.dot(mix_low, wo_full, preferred_element_type=jnp.float32)
    inv_two = inverse_rms(resid)
    resid_hat = resid * inv_two
    ffn_in = (resid_hat * gain_ffn).astype(jnp.bfloat16)
    gate = jnp.dot(ffn_in, gate_full, preferred_element_type=jnp.float32)
    upper = jnp.dot(ffn_in, up_full, preferred_element_type=jnp.float32)
    sigmoid_gate = jax.nn.sigmoid(gate)
    silu_gate = gate * sigmoid_gate
    hidden = (silu_gate * upper).astype(jnp.bfloat16)
    result = (resid + jnp.dot(hidden, down_full, preferred_element_type=jnp.float32)).astype(
        jnp.bfloat16
    )
    again = (
        lax.all_gather(w_query, "shard", axis=0, tiled=True),
        lax.all_gather(w_key, "shard", axis=0, tiled=True),
        lax.all_gather(w_value, "shard", axis=0, tiled=True),
        lax.all_gather(w_out, "shard", axis=0, tiled=True),
        lax.all_gather(w_gate, "shard", axis=0, tiled=True),
        lax.all_gather(w_up, "shard", axis=0, tiled=True),
        lax.all_gather(w_down, "shard", axis=0, tiled=True),
    )
    wq_back, wk_back, wv_back, wo_back, gate_back, up_back, down_back = (
        again[0],
        again[1],
        again[2],
        again[3],
        again[4],
        again[5],
        again[6],
    )
    grad_out = cotangent.astype(jnp.float32)
    grad_down = outer_sum(hidden, cotangent)
    grad_hidden = back_dot(cotangent, down_back)
    grad_gate_low = (
        grad_hidden * upper * sigmoid_gate * (1.0 + gate * (1.0 - sigmoid_gate))
    ).astype(jnp.bfloat16)
    grad_up_low = (grad_hidden * silu_gate).astype(jnp.bfloat16)
    grad_gate_w = outer_sum(ffn_in, grad_gate_low)
    grad_up_w = outer_sum(ffn_in, grad_up_low)
    grad_ffn_in = back_dot(grad_gate_low, gate_back) + back_dot(grad_up_low, up_back)
    grad_gain_ffn = jnp.sum(grad_ffn_in * resid_hat, axis=0)
    grad_resid = grad_out + norm_back(grad_ffn_in * gain_ffn, resid_hat, inv_two)
    grad_resid_low = grad_resid.astype(jnp.bfloat16)
    grad_out_w = outer_sum(mix_low, grad_resid_low)
    grad_mix_low = (
        back_dot(grad_resid_low, wo_back).astype(jnp.bfloat16).reshape(tok_count, HK, groups, DH)
    )
    grad_q_parts = []
    place = 0
    number = 0
    seq_base = number * seq_len
    key_total = jnp.zeros((seq_len, HK, DH), jnp.float32)
    value_total = jnp.zeros((seq_len, HK, DH), jnp.float32)
    for row_start in range(0, seq_len, block_rows):
        row_end = row_start + block_rows
        allowed = block_mask(doc_ids[number], row_start, block_rows)
        grad_query, grad_key, grad_value = block_backward(
            q_group[seq_base + row_start : seq_base + row_end],
            k_rot[seq_base : seq_base + row_end],
            v_heads[seq_base : seq_base + row_end],
            allowed,
            log_totals[place],
            grad_mix_low[seq_base + row_start : seq_base + row_end],
        )
        place = place + 1
        padding = ((0, seq_len - row_end), (0, 0), (0, 0))
        key_total = key_total + jnp.pad(grad_key, padding)
        value_total = value_total + jnp.pad(grad_value, padding)
        grad_q_parts.append(grad_query)
    grad_q_rot = jnp.concatenate(grad_q_parts, axis=0).reshape(tok_count, HQ, DH)
    grad_v_low = value_total.reshape(tok_count, HK * DH).astype(jnp.bfloat16)
    grad_q_norm = unrotate(grad_q_rot, cosine, sine)
    grad_k_norm = unrotate(key_total, cosine, sine)
    grad_gain_query = jnp.sum(grad_q_norm * q_hat, axis=(0, 1))
    grad_gain_key = jnp.sum(grad_k_norm * k_hat, axis=(0, 1))
    grad_q_low = (
        norm_back(grad_q_norm * gain_query, q_hat, q_inv)
        .reshape(tok_count, HQ * DH)
        .astype(jnp.bfloat16)
    )
    grad_k_low = (
        norm_back(grad_k_norm * gain_key, k_hat, k_inv)
        .reshape(tok_count, HK * DH)
        .astype(jnp.bfloat16)
    )
    grad_query_w = outer_sum(attn_in, grad_q_low)
    grad_key_w = outer_sum(attn_in, grad_k_low)
    grad_value_w = outer_sum(attn_in, grad_v_low)
    grad_attn_in = (
        back_dot(grad_q_low, wq_back)
        + back_dot(grad_k_low, wk_back)
        + back_dot(grad_v_low, wv_back)
    )
    grad_gain_attn = jnp.sum(grad_attn_in * x_hat, axis=0)
    grad_input = grad_resid + norm_back(grad_attn_in * gain_attn, x_hat, inv_one)
    owned = (
        lax.psum_scatter(
            grad_query_w.astype(jnp.bfloat16), "shard", scatter_dimension=0, tiled=True
        ).astype(jnp.float32),
        lax.psum_scatter(
            grad_key_w.astype(jnp.bfloat16), "shard", scatter_dimension=0, tiled=True
        ).astype(jnp.float32),
        lax.psum_scatter(
            grad_value_w.astype(jnp.bfloat16), "shard", scatter_dimension=0, tiled=True
        ).astype(jnp.float32),
        lax.psum_scatter(
            grad_out_w.astype(jnp.bfloat16), "shard", scatter_dimension=0, tiled=True
        ).astype(jnp.float32),
        lax.psum_scatter(
            grad_gate_w.astype(jnp.bfloat16), "shard", scatter_dimension=0, tiled=True
        ).astype(jnp.float32),
        lax.psum_scatter(
            grad_up_w.astype(jnp.bfloat16), "shard", scatter_dimension=0, tiled=True
        ).astype(jnp.float32),
        lax.psum_scatter(
            grad_down.astype(jnp.bfloat16), "shard", scatter_dimension=0, tiled=True
        ).astype(jnp.float32),
        lax.psum_scatter(
            grad_gain_attn.astype(jnp.bfloat16), "shard", scatter_dimension=0, tiled=True
        ).astype(jnp.float32),
        lax.psum_scatter(
            grad_gain_ffn.astype(jnp.bfloat16), "shard", scatter_dimension=0, tiled=True
        ).astype(jnp.float32),
        lax.psum_scatter(
            grad_gain_query.astype(jnp.bfloat16), "shard", scatter_dimension=0, tiled=True
        ).astype(jnp.float32),
        lax.psum_scatter(
            grad_gain_key.astype(jnp.bfloat16), "shard", scatter_dimension=0, tiled=True
        ).astype(jnp.float32),
    )
    totals = (
        lax.psum(owned[0].astype(jnp.bfloat16), "rep").astype(jnp.float32),
        lax.psum(owned[1].astype(jnp.bfloat16), "rep").astype(jnp.float32),
        lax.psum(owned[2].astype(jnp.bfloat16), "rep").astype(jnp.float32),
        lax.psum(owned[3].astype(jnp.bfloat16), "rep").astype(jnp.float32),
        lax.psum(owned[4].astype(jnp.bfloat16), "rep").astype(jnp.float32),
        lax.psum(owned[5].astype(jnp.bfloat16), "rep").astype(jnp.float32),
        lax.psum(owned[6].astype(jnp.bfloat16), "rep").astype(jnp.float32),
        lax.psum(owned[7].astype(jnp.bfloat16), "rep").astype(jnp.float32),
        lax.psum(owned[8].astype(jnp.bfloat16), "rep").astype(jnp.float32),
        lax.psum(owned[9].astype(jnp.bfloat16), "rep").astype(jnp.float32),
        lax.psum(owned[10].astype(jnp.bfloat16), "rep").astype(jnp.float32),
    )
    return (
        result,
        grad_input,
        totals[0],
        totals[1],
        totals[2],
        totals[3],
        totals[4],
        totals[5],
        totals[6],
        totals[7],
        totals[8],
        totals[9],
        totals[10],
    )


def solution(mesh):
    in_specs = (
        P(("shard", "rep"), None),
        P(("shard", "rep"), None),
        P("shard", None),
        P("shard", None),
        P("shard", None),
        P("shard", None),
        P("shard", None),
        P("shard", None),
        P("shard", None),
        P("shard"),
        P("shard"),
        P("shard"),
        P("shard"),
        P(("shard", "rep"), None),
    )
    out_specs = (
        P(("shard", "rep"), None),
        P(("shard", "rep"), None),
        P("shard", None),
        P("shard", None),
        P("shard", None),
        P("shard", None),
        P("shard", None),
        P("shard", None),
        P("shard", None),
        P("shard"),
        P("shard"),
        P("shard"),
        P("shard"),
    )
    return jax.shard_map(
        per_device, mesh=mesh, in_specs=in_specs, out_specs=out_specs, check_vma=False
    )
```

profile of v0, /device:TPU:0, one launch (start us, length us, event | category | flops | bytes accessed | tf_op | source)
XLA Modules:
  0.0 1284.2 jit_solution(8816345716559144776)
XLA Ops:
  15.4 9.5 all-gather
  26.8 9.0 all-reduce.11
  37.2 8.2 all-gather.1
  45.3 3.9 copy.67
  52.5 3.9 multiply_reduce_fusion.6
  56.4 11.4 all-gather.10.cloned.1.call-done
  72.3 32.7 %all-gather.14.cloned.1.call-done = bf16[1024,1024]{1,0:T(8,128)(2,1)} async-done(((bf16[256,1024]{1,0:T(8,128)(2,1)}), bf16[1024,1024]{1,0:T(8,128)(2,1)}) %all-gather.14.cloned.1.call-update) | async-done | bytes 2097168 | tf_op jit(solution)/shard_map/all_gather | solution.py:123
  105.0 4.2 multiply_reduce_fusion.4
  112.4 7.4 fusion.93
  119.8 8.2 fusion.15
  128.1 7.6 fusion.57
  135.8 13.6 %fusion.92 = (f32[8,2,512]{2,1,0:T(2,128)S(1)}, f32[8,2,512,1024]{2,3,1,0:T(8,128)}) fusion(bf16[512,8,2,64]{0,3,2,1:T(8,128)(2,1)S(1)} %bitcast.248, bf16[1024,8,32]{0,2,1:T(8,128)(2,1)S(1)} %get-tuple-element.89, bf16[1024,8,32]{0,2,1:T(8,128)(2,1)S(1)} %get-tuple-element.88, pred[512,1024]{0,1:T(8,128)(4,1)S(1)} %copy-done.18), kind=kOutput, calls=%fused_computation.169 | convolution fusion | flops 1100996608 | bytes 36208640 | tf_op jit(solution)/shard_map/qkgd,pkd->kgqp/dot_general | solution.py:74
  149.3 15.0 %fusion.5 = f32[8,2,512]{2,1,0:T(2,128)S(1)} fusion(f32[8,2,512,1024]{2,3,1,0:T(8,128)} %get-tuple-element.107, f32[8,2,512]{2,1,0:T(2,128)S(1)} %get-tuple-element.106), kind=kLoop, calls=%fused_computation.11 | loop fusion | flops 16769024 | bytes 33619968 | tf_op jit(solution)/shard_map/reduce_sum | solution.py:78
  164.4 14.0 %fusion.56 = bf16[512,8,2,64]{0,3,2,1:T(8,128)(2,1)S(1)} fusion(bf16[1024,8,64,1]{0,2,3,1:T(8,128)(2,1)S(1)} %bitcast.252, f32[8,2,512,1024]{2,3,1,0:T(8,128)} %get-tuple-element.107, f32[8,2,512]{2,1,0:T(2,128)S(1)} %fusion.5, f32[8,2,512]{2,1,0:T(2,128)S(1)} %get-tuple-element.106), kind=kOutput, calls=%fused_computation.115 | convolution fusion | flops 1099431936 | bytes 35717120 | tf_op jit(solution)/shard_map/kgqp,pkd->qkgd/dot_general | solution.py:80
  180.0 4.8 multiply_reduce_fusion.3
  187.2 52.8 %all-gather.18.cloned.1.call-done = bf16[1024,4608]{1,0:T(8,128)(2,1)} async-done(((bf16[256,4608]{1,0:T(8,128)(2,1)}), bf16[1024,4608]{1,0:T(8,128)(2,1)}) %all-gather.18.cloned.1.call-update) | async-done | bytes 9437200 | tf_op jit(solution)/shard_map/all_gather | solution.py:127
  240.1 16.2 %fusion.94 = f32[1024,4608]{1,0:T(8,128)} fusion(bf16[1024,1024]{0,1:T(8,128)(2,1)S(1)} %multiply_convert_fusion.3, bf16[1024,4608]{1,0:T(8,128)(2,1)} %all-gather.18.cloned.1.call-done), kind=kOutput, calls=%fused_computation.171 | convolution fusion | flops 9663676416 | bytes 30408704 | tf_op jit(solution)/shard_map/dot_general | solution.py:196
  256.3 81.8 %all-gather.20.cloned.1.call-done = bf16[1024,4608]{1,0:T(8,128)(2,1)} async-done(((bf16[256,4608]{1,0:T(8,128)(2,1)}), bf16[1024,4608]{1,0:T(8,128)(2,1)}) %all-gather.20.cloned.1.call-update) | async-done | bytes 9437200 | tf_op jit(solution)/shard_map/all_gather | solution.py:128
  338.1 17.2 %fusion.95 = f32[1024,4608]{1,0:T(8,128)} fusion(bf16[1024,1024]{0,1:T(8,128)(2,1)} %copy-done.34, bf16[1024,4608]{1,0:T(8,128)(2,1)} %all-gather.20.cloned.1.call-done), kind=kOutput, calls=%fused_computation.172 | convolution fusion | flops 9663676416 | bytes 30408704 | tf_op jit(solution)/shard_map/dot_general | solution.py:197
  355.3 81.1 %all-gather.22.cloned.1.call-done = bf16[4608,1024]{1,0:T(8,128)(2,1)} async-done(((bf16[1152,1024]{1,0:T(8,128)(2,1)}), bf16[4608,1024]{1,0:T(8,128)(2,1)}) %all-gather.22.cloned.1.call-update) | async-done | bytes 9437200 | tf_op jit(solution)/shard_map/all_gather | solution.py:129
  436.3 30.6 %multiply_convert_fusion = (bf16[1024,4608]{1,0:T(8,128)(2,1)}, bf16[1024,4608]{1,0:T(8,128)(2,1)}, bf16[1024,4608]{1,0:T(8,128)(2,1)}) fusion(f32[1024,4608]{1,0:T(8,128)} %fusion.94, f32[1024,4608]{1,0:T(8,128)} %fusion.95, bf16[1024,1024]{1,0:T(8,128)(2,1)S(1)} %copy-done.33, bf16[4608,1024]{1,0:T(8,128)(2,1)} %all-gather.22.cloned.1.call-done), kind=kOutput, calls=%fused_computation.13 | convolution fusion | flops 9734455296 | bytes 77594624 | tf_op jit(solution)/shard_map/dot_general | solution.py:23
  467.0 14.2 %fusion.96 = f32[1024,1024]{0,1:T(8,128)S(1)} fusion(bf16[1024,4608]{1,0:T(8,128)(2,1)} %get-tuple-element.74, bf16[1024,4608]{1,0:T(8,128)(2,1)} %all-gather.18.cloned.1.call-done), kind=kOutput, calls=%fused_computation.173 | convolution fusion | flops 9663676416 | bytes 23068672 | tf_op jit(solution)/shard_map/dot_general | solution.py:23
  481.2 17.0 %multiply_reduce_fusion = (bf16[1024]{0:T(1024)(128)(2,1)}, f32[1024]{0:T(1024)S(1)}, f32[1024,1024]{0,1:T(8,128)S(1)}) fusion(f32[1024,1024]{0,1:T(8,128)S(1)} %copy-done.7, f32[1024]{0:T(1024)S(1)} %add_rsqrt_fusion.2, f32[1024]{0:T(1024)S(1)} %bitcast.278, f32[1024,1024]{0,1:T(8,128)S(1)} %fusion.96, bf16[1024,4608]{1,0:T(8,128)(2,1)} %get-tuple-element.73, ...), kind=kOutput, calls=%fused_computation.68 | convolution fusion | flops 9671014400 | bytes 31471616 | tf_op jit(solution)/shard_map/dot_general | solution.py:23
  504.0 8.2 fusion.97
  515.9 23.8 %fusion.52 = f32[512,8,64]{0,2,1:T(8,128)} fusion(bf16[512,8,2,64]{0,3,2,1:T(8,128)(2,1)} %bitcast.245, f32[8,512,512,2]{2,1,3,0:T(8,128)} %fusion.97, f32[8,2,512,512]{2,3,1,0:T(8,128)} %get-tuple-element.109, f32[8,2,512]{2,1,0:T(2,128)S(1)} %bitcast.262), kind=kOutput, calls=%fused_computation.113 | convolution fusion | flops 566239744 | bytes 35684352 | tf_op jit(solution)/shard_map/kgqp,qkgd->pkd/dot_general | solution.py:97
  539.7 13.3 %fusion.98 = f32[8,1024,512,2]{2,1,3,0:T(8,128)} fusion(bf16[1024,8,64,1]{0,2,3,1:T(8,128)(2,1)S(1)} %bitcast.253, bf16[512,8,2,64]{0,3,2,1:T(8,128)(2,1)S(1)} %bitcast.242), kind=kOutput, calls=%fused_computation.175 | convolution fusion | flops 1073741824 | bytes 35651584 | tf_op jit(solution)/shard_map/qkgd,pkd->kgqp/dot_general | solution.py:89
  553.1 43.5 %fusion.47 = f32[512,8,2,64]{0,3,2,1:T(8,128)} fusion(f32[8,1024,512,2]{2,1,3,0:T(8,128)} %fusion.98, f32[8,2,512,1024]{2,3,1,0:T(8,128)} %get-tuple-element.107, f32[8,2,512]{2,1,0:T(2,128)S(1)} %bitcast.258, bf16[1024,8,32]{0,2,1:T(8,128)(2,1)S(1)} %copy-done.16, bf16[1024,8,32]{0,2,1:T(8,128)(2,1)S(1)} %copy-done.13), kind=kOutput, calls=%fused_computation.107 | convolution fusion | flops 1134568448 | bytes 70287360 | tf_op jit(solution)/shard_map/kgqp,pkd->qkgd/dot_general | solution.py:94
  596.6 43.9 %bitcast_add_fusion.1 = f32[1024,8,64]{0,2,1:T(8,128)} fusion(f32[512,8,64]{0,2,1:T(8,128)} %fusion.52, bf16[512,8,2,64]{0,3,2,1:T(8,128)(2,1)S(1)} %bitcast.249, f32[8,1024,512,2]{2,1,3,0:T(8,128)} %fusion.98, f32[8,2,512,1024]{2,3,1,0:T(8,128)} %get-tuple-element.107, f32[8,2,512]{2,1,0:T(2,128)S(1)} %bitcast.259), kind=kOutput, calls=%fused_computation.87 | convolution fusion | flops 1132995584 | bytes 71335936 | tf_op jit(solution)/shard_map/kgqp,qkgd->pkd/dot_general | solution.py:97
  647.6 14.9 %fusion.42 = bf16[1024,8,64]{0,2,1:T(8,128)(2,1)} fusion(f32[512,8,64]{0,2,1:T(8,128)} %fusion.53, bf16[512,8,2,64]{0,3,2,1:T(8,128)(2,1)S(1)} %bitcast.243, f32[8,2,512,1024]{2,3,1,0:T(8,128)} %get-tuple-element.107, f32[8,2,512]{2,1,0:T(2,128)S(1)} %bitcast.260), kind=kOutput, calls=%fused_computation.86 | convolution fusion | flops 1091567616 | bytes 36732928 | tf_op jit(solution)/shard_map/kgqp,qkgd->pkd/dot_general | solution.py:100
  666.1 28.9 %fusion.46 = f32[512,8,2,64]{0,3,2,1:T(8,128)} fusion(f32[8,512,512,2]{2,1,3,0:T(8,128)} %fusion.97, f32[8,2,512,512]{2,3,1,0:T(8,128)} %get-tuple-element.109, f32[8,2,512]{2,1,0:T(2,128)S(1)} %bitcast.263, bf16[1024,8,32]{0,2,1:T(8,128)(2,1)S(1)} %copy-done.14, bf16[1024,8,32]{0,2,1:T(8,128)(2,1)S(1)} %copy-done.17), kind=kOutput, calls=%fused_computation.106 | convolution fusion | flops 567288320 | bytes 70320128 | tf_op jit(solution)/shard_map/kgqp,pkd->qkgd/dot_general | solution.py:94
  707.8 6.5 convolution_convert_fusion.4
  714.3 17.0 %convolution_convert_fusion.1 = bf16[1024,4608]{1,0:T(8,128)(2,1)} fusion(bf16[1024,1024]{0,1:T(8,128)(2,1)} %copy-done.34, bf16[1024,4608]{1,0:T(8,128)(2,1)} %get-tuple-element.74), kind=kOutput, calls=%fused_computation.36 | convolution fusion | flops 9668395008 | bytes 20971520 | tf_op jit(solution)/shard_map/dot_general | solution.py:17
  731.5 16.3 %convolution_convert_fusion = bf16[1024,4608]{1,0:T(8,128)(2,1)} fusion(bf16[1024,1024]{0,1:T(8,128)(2,1)} %copy-done.34, bf16[1024,4608]{1,0:T(8,128)(2,1)} %get-tuple-element.73), kind=kOutput, calls=%fused_computation.35 | convolution fusion | flops 9668395008 | bytes 20971520 | tf_op jit(solution)/shard_map/dot_general | solution.py:17
  747.8 16.5 %convolution_convert_fusion.2 = bf16[4608,1024]{1,0:T(8,128)(2,1)} fusion(bf16[1024,4608]{1,0:T(8,128)(2,1)} %get-tuple-element.75, bf16[1024,1024]{1,0:T(8,128)(2,1)} %param.27), kind=kOutput, calls=%fused_computation.37 | convolution fusion | flops 9668395008 | bytes 20971520 | tf_op jit(solution)/shard_map/dot_general | solution.py:17
  765.8 6.6 fusion.99
  772.4 11.0 reduce-scatter.14.cloned.1.call-done
  783.4 98.0 %reduce-scatter.16.cloned.1.call-done = bf16[256,4608]{1,0:T(8,128)(2,1)} async-done(((bf16[1024,4608]{1,0:T(8,128)(2,1)}), bf16[256,4608]{1,0:T(8,128)(2,1)}) %reduce-scatter.16.cloned.1.call-update) | async-done | bytes 2359312 | tf_op jit(solution)/shard_map/reduce_scatter | solution.py:300
  881.5 98.2 %reduce-scatter.18.cloned.1.call-done = bf16[256,4608]{1,0:T(8,128)(2,1)} async-done(((bf16[1024,4608]{1,0:T(8,128)(2,1)}), bf16[256,4608]{1,0:T(8,128)(2,1)}) %reduce-scatter.18.cloned.1.call-update) | async-done | bytes 2359312 | tf_op jit(solution)/shard_map/reduce_scatter | solution.py:303
  979.6 98.0 %reduce-scatter.20.cloned.1.call-done = bf16[1152,1024]{1,0:T(8,128)(2,1)} async-done(((bf16[4608,1024]{1,0:T(8,128)(2,1)}), bf16[1152,1024]{1,0:T(8,128)(2,1)}) %reduce-scatter.20.cloned.1.call-update) | async-done | bytes 2359312 | tf_op jit(solution)/shard_map/reduce_scatter | solution.py:306
  1077.7 4.9 fusion.100
  1082.8 8.2 fusion.36
  1091.0 8.5 all-reduce.10
  1099.8 15.6 %all-reduce.8 = (bf16[256]{0:T(256)(128)(2,1)S(1)}, bf16[256]{0:T(256)(128)(2,1)S(1)}, bf16[16]{0:T(256)(128)(2,1)S(1)}, bf16[16]{0:T(256)(128)(2,1)S(1)}) all-reduce(bf16[256]{0:T(256)(128)(2,1)S(1)} %dynamic-slice.3, bf16[256]{0:T(256)(128)(2,1)S(1)} %dynamic-slice.5, ...), channel_id=1, replica_groups=mesh['shard'=4,'rep'=8] {'rep'}, use_global_device_ids=true, to_apply=%region_33.34 | all-reduce | flops 544 | bytes 2176 | tf_op jit(solution)/shard_map/psum | solution.py:330
  1117.5 6.6 fusion.35
  1124.1 5.4 copy.80
  1129.5 16.1 %add_convert_fusion = bf16[1024,1024]{0,1:T(8,128)(2,1)S(1)} fusion(f32[1024,1024]{0,1:T(8,128)} %copy-done.6, bf16[1024,4608]{1,0:T(8,128)(2,1)} %get-tuple-element.75, bf16[4608,1024]{1,0:T(8,128)(2,1)} %all-gather.22.cloned.1.call-done), kind=kOutput, calls=%fused_computation.73 | convolution fusion | flops 9665773568 | bytes 25165824 | tf_op jit(solution)/shard_map/dot_general | solution.py:201
  1148.2 115.3 %all-reduce.14.cloned.1.call-done = (bf16[256,1024]{1,0:T(8,128)(2,1)}, bf16[256,512]{1,0:T(8,128)(2,1)}, bf16[256,512]{1,0:T(8,128)(2,1)}, bf16[256,1024]{1,0:T...) async-done(((bf16[256,1024]{1,0:T(8,128)(2,1)}, bf16[256,512]{1,0:T(8,128)(2,1)}, bf16[256,512]{1,0:T(8,128)(2,1)}, ...) | async-done | bytes 8650768 | tf_op jit(solution)/shard_map/psum | solution.py:323
  1263.5 4.6 convert_element_type.227
  (252 shorter events, 73.1 us)
Async XLA Ops:
  7.2 45.3 %all-gather.12.cloned.1.call-start = ((), (), s32[]{:S(2)}) async-start(), calls=%async_computation.8 | async-start | bytes 1310720 | tf_op jit(solution)/shard_map/all_gather | solution.py:124
  7.9 59.9 %all-gather.10.cloned.1.call-start = ((), (), s32[]{:S(2)}) async-start(), calls=%async_computation.7 | async-start | bytes 1310720 | tf_op jit(solution)/shard_map/all_gather | solution.py:125
  8.7 96.3 %all-gather.14.cloned.1.call-start = ((), (), s32[]{:S(2)}) async-start(), calls=%async_computation.9 | async-start | bytes 2621440 | tf_op jit(solution)/shard_map/all_gather | solution.py:123
  9.4 170.6 %all-gather.16.cloned.1.call-start = ((), (), s32[]{:S(2)}) async-start(), calls=%async_computation.10 | async-start | bytes 2621440 | tf_op jit(solution)/shard_map/all_gather | solution.py:126
  10.0 230.1 %all-gather.18.cloned.1.call-start = ((), (), s32[]{:S(2)}) async-start(), calls=%async_computation.11 | async-start | bytes 11796480 | tf_op jit(solution)/shard_map/all_gather | solution.py:127
  10.6 327.6 %all-gather.20.cloned.1.call-start = ((), (), s32[]{:S(2)}) async-start(), calls=%async_computation.12 | async-start | bytes 11796480 | tf_op jit(solution)/shard_map/all_gather | solution.py:128
  11.1 13.8 %copy-start.57 = (u32[32]{0:T(128)S(1)}, u32[32]{0:T(128)}, u32[]{:S(2)}) copy-start(u32[32]{0:T(128)} %constant.51) | copy-start | bytes 388
  11.2 15.1 %copy-start.61 = (bf16[16]{0:T(256)(128)(2,1)S(1)}, bf16[16]{0:T(256)(128)(2,1)}, u32[]{:S(2)}) copy-start(bf16[16]{0:T(256)(128)(2,1)} %param.26) | copy-start | bytes 100
  11.2 15.3 %copy-start.62 = (bf16[16]{0:T(256)(128)(2,1)S(1)}, bf16[16]{0:T(256)(128)(2,1)}, u32[]{:S(2)}) copy-start(bf16[16]{0:T(256)(128)(2,1)} %param.25) | copy-start | bytes 100
  11.2 24.6 %copy-start.46 = (s32[1,1024]{1,0:T(1,128)S(1)}, s32[1,1024]{1,0:T(1,128)}, u32[]{:S(2)}) copy-start(s32[1,1024]{1,0:T(1,128)} %param.15) | copy-start | bytes 12292
  11.2 26.0 %copy-start.63 = (bf16[256]{0:T(256)(128)(2,1)S(1)}, bf16[256]{0:T(256)(128)(2,1)}, u32[]{:S(2)}) copy-start(bf16[256]{0:T(256)(128)(2,1)} %param.24) | copy-start | bytes 1540
  11.2 425.1 %all-gather.22.cloned.1.call-start = ((), (), s32[]{:S(2)}) async-start(), calls=%async_computation.13 | async-start | bytes 11796480 | tf_op jit(solution)/shard_map/all_gather | solution.py:129
  11.9 760.5 %reduce-scatter.10.cloned.1.call-start = ((), (), s32[]{:S(2)}) async-start(), calls=%async_computation.15 | async-start | bytes 1310720 | tf_op jit(solution)/shard_map/reduce_scatter | solution.py:291
  14.9 165.1 %copy-start.2 = (bf16[1024,1024]{0,1:T(8,128)(2,1)}, bf16[1024,1024]{0,1:T(8,128)(2,1)S(1)}, u32[]{:S(2)}) copy-start(bf16[1024,1024]{0,1:T(8,128)(2,1)S(1)} %copy.63) | copy-start | bytes 6291460
  15.4 89.5 %copy-start.47 = (f32[1024]{0:T(1024)}, f32[1024]{0:T(1024)S(1)}, u32[]{:S(2)}) copy-start(f32[1024]{0:T(1024)S(1)} %add_rsqrt_fusion.3) | copy-start | bytes 12292
  25.0 80.0 %copy-start.49 = (f32[4,1,256]{2,1,0:T(1,128)}, f32[4,1,256]{2,1,0:T(1,128)S(1)}, u32[]{:S(2)}) copy-start(f32[4,1,256]{2,1,0:T(1,128)S(1)} %convert_element_type.240) | copy-start | bytes 12292
  35.8 73.4 %copy-start.53 = (f32[64]{0:T(128)}, f32[64]{0:T(128)S(1)}, u32[]{:S(2)}) copy-start(f32[64]{0:T(128)S(1)} %convert_element_type.197) | copy-start | bytes 772
  36.2 35.2 %copy-start.55 = (f32[64]{0:T(128)}, f32[64]{0:T(128)S(1)}, u32[]{:S(2)}) copy-start(f32[64]{0:T(128)S(1)} %convert_element_type.194) | copy-start | bytes 772
  51.2 59.1 %copy-start.21 = (f32[1024,32]{0,1:T(8,128)}, f32[1024,32]{0,1:T(8,128)S(1)}, u32[]{:S(2)}) copy-start(f32[1024,32]{0,1:T(8,128)S(1)} %get-tuple-element.96) | copy-start | bytes 393220
  51.2 59.1 %copy-start.23 = (f32[1024,32]{0,1:T(8,128)}, f32[1024,32]{0,1:T(8,128)S(1)}, u32[]{:S(2)}) copy-start(f32[1024,32]{0,1:T(8,128)S(1)} %get-tuple-element.97) | copy-start | bytes 393220
  56.4 15.0 %copy-start.39 = (f32[1024,8]{0,1:T(8,128)}, f32[1024,8]{0,1:T(8,128)S(1)}, u32[]{:S(2)}) copy-start(f32[1024,8]{0,1:T(8,128)S(1)} %add_rsqrt_fusion.1) | copy-start | bytes 98308
  72.3 63.5 %copy-start.12 = (bf16[1024,8,32]{0,2,1:T(8,128)(2,1)}, bf16[1024,8,32]{0,2,1:T(8,128)(2,1)S(1)}, u32[]{:S(2)}) copy-start(bf16[1024,8,32]{0,2,1:T(8,128)(2,1)S(1)} %get-tuple-element.88) | copy-start | bytes 1572868
  72.3 63.5 %copy-start.15 = (bf16[1024,8,32]{0,2,1:T(8,128)(2,1)}, bf16[1024,8,32]{0,2,1:T(8,128)(2,1)S(1)}, u32[]{:S(2)}) copy-start(bf16[1024,8,32]{0,2,1:T(8,128)(2,1)S(1)} %get-tuple-element.89) | copy-start | bytes 1572868
  112.3 23.4 %copy-start.19 = (bf16[512,16,64]{0,2,1:T(8,128)(2,1)}, bf16[512,16,64]{0,2,1:T(8,128)(2,1)S(1)}, u32[]{:S(2)}) copy-start(bf16[512,16,64]{0,2,1:T(8,128)(2,1)S(1)} %get-tuple-element.95) | copy-start | bytes 3145732
  119.8 8.3 copy-start.25
  149.3 15.0 %copy-start.31 = (bf16[1024,512]{0,1:T(8,128)(2,1)S(1)}, bf16[1024,512]{0,1:T(8,128)(2,1)}, u32[]{:S(2)}) copy-start(bf16[1024,512]{0,1:T(8,128)(2,1)} %copy-done.30) | copy-start | bytes 3145732
  187.2 52.8 %copy-start.34 = (bf16[1024,1024]{0,1:T(8,128)(2,1)}, bf16[1024,1024]{0,1:T(8,128)(2,1)S(1)}, u32[]{:S(2)}) copy-start(bf16[1024,1024]{0,1:T(8,128)(2,1)S(1)} %multiply_convert_fusion.3) | copy-start | bytes 6291460
  256.3 180.0 %copy-start.33 = (bf16[1024,1024]{1,0:T(8,128)(2,1)S(1)}, bf16[1024,1024]{1,0:T(8,128)(2,1)}, u32[]{:S(2)}) copy-start(bf16[1024,1024]{1,0:T(8,128)(2,1)} %param.27) | copy-start | bytes 6291460
  467.0 14.2 %copy-start.7 = (f32[1024,1024]{0,1:T(8,128)S(1)}, f32[1024,1024]{0,1:T(8,128)}, u32[]{:S(2)}) copy-start(f32[1024,1024]{0,1:T(8,128)} %copy-done.6) | copy-start | bytes 12582916
  481.2 17.0 %copy-start.9 = (bf16[1024,1024]{0,1:T(8,128)(2,1)S(1)}, bf16[1024,1024]{0,1:T(8,128)(2,1)}, u32[]{:S(2)}) copy-start(bf16[1024,1024]{0,1:T(8,128)(2,1)} %copy.67) | copy-start | bytes 6291460
  499.8 12.4 slice-start
  499.8 12.4 slice-start.1
  504.0 8.2 slice-start.3
  515.9 23.8 %copy-start.32 = (bf16[1024,512]{0,1:T(8,128)(2,1)S(1)}, bf16[1024,512]{0,1:T(8,128)(2,1)}, u32[]{:S(2)}) copy-start(bf16[1024,512]{0,1:T(8,128)(2,1)} %copy-done.30) | copy-start | bytes 3145732
  539.7 13.3 %copy-start.13 = (bf16[1024,8,32]{0,2,1:T(8,128)(2,1)S(1)}, bf16[1024,8,32]{0,2,1:T(8,128)(2,1)}, u32[]{:S(2)}) copy-start(bf16[1024,8,32]{0,2,1:T(8,128)(2,1)} %copy-done.12) | copy-start | bytes 1572868
  539.7 13.3 %copy-start.16 = (bf16[1024,8,32]{0,2,1:T(8,128)(2,1)S(1)}, bf16[1024,8,32]{0,2,1:T(8,128)(2,1)}, u32[]{:S(2)}) copy-start(bf16[1024,8,32]{0,2,1:T(8,128)(2,1)} %copy-done.15) | copy-start | bytes 1572868
  539.7 13.3 %copy-start.45 = (f32[2,8,512]{2,1,0:T(8,128)S(1)}, f32[2,8,512]{2,1,0:T(8,128)}, u32[]{:S(2)}) copy-start(f32[2,8,512]{2,1,0:T(8,128)} %log_add_fusion) | copy-start | bytes 98308
  553.0 43.6 %copy-start.20 = (bf16[512,16,64]{0,2,1:T(8,128)(2,1)S(1)}, bf16[512,16,64]{0,2,1:T(8,128)(2,1)}, u32[]{:S(2)}) copy-start(bf16[512,16,64]{0,2,1:T(8,128)(2,1)} %copy-done.19) | copy-start | bytes 3145732
  596.6 43.9 %copy-start.22 = (f32[1024,32]{0,1:T(8,128)S(1)}, f32[1024,32]{0,1:T(8,128)}, u32[]{:S(2)}) copy-start(f32[1024,32]{0,1:T(8,128)} %copy-done.21) | copy-start | bytes 393220
  596.6 43.9 %copy-start.24 = (f32[1024,32]{0,1:T(8,128)S(1)}, f32[1024,32]{0,1:T(8,128)}, u32[]{:S(2)}) copy-start(f32[1024,32]{0,1:T(8,128)} %copy-done.23) | copy-start | bytes 393220
  647.5 124.9 %reduce-scatter.12.cloned.1.call-start = ((), (), s32[]{:S(2)}) async-start(), calls=%async_computation.16 | async-start | bytes 1310720 | tf_op jit(solution)/shard_map/reduce_scatter | solution.py:294
  666.1 106.4 %reduce-scatter.8.cloned.1.call-start = ((), (), s32[]{:S(2)}) async-start(), calls=%async_computation.14 | async-start | bytes 2621440 | tf_op jit(solution)/shard_map/reduce_scatter | solution.py:288
  707.7 75.7 %reduce-scatter.14.cloned.1.call-start = ((), (), s32[]{:S(2)}) async-start(), calls=%async_computation.17 | async-start | bytes 2621440 | tf_op jit(solution)/shard_map/reduce_scatter | solution.py:297
  714.3 167.2 %reduce-scatter.16.cloned.1.call-start = ((), (), s32[]{:S(2)}) async-start(), calls=%async_computation.18 | async-start | bytes 11796480 | tf_op jit(solution)/shard_map/reduce_scatter | solution.py:300
  731.4 248.2 %reduce-scatter.18.cloned.1.call-start = ((), (), s32[]{:S(2)}) async-start(), calls=%async_computation.19 | async-start | bytes 11796480 | tf_op jit(solution)/shard_map/reduce_scatter | solution.py:303
  747.7 329.9 %reduce-scatter.20.cloned.1.call-start = ((), (), s32[]{:S(2)}) async-start(), calls=%async_computation.20 | async-start | bytes 11796480 | tf_op jit(solution)/shard_map/reduce_scatter | solution.py:306
  764.3 499.2 %all-reduce.14.cloned.1.call-start = ((), (), s32[]{:S(2)}) async-start(), calls=%async_computation.21 | async-start | bytes 17301504 | tf_op jit(solution)/shard_map/psum | solution.py:323
  1082.8 8.2 copy-start.58
  (35 other events, 106.1 us)
Sparse Core Ops, SparseCore 0:
  9.9 29.3 all-gather.11
  41.1 26.5 all-gather.9
  69.6 35.2 all-gather.13
  106.7 35.2 all-gather.15
  143.7 96.3 all-gather.17
  241.7 96.3 all-gather.19
  340.0 96.3 all-gather.21
  647.6 27.7 reduce-scatter.9
  679.1 27.7 reduce-scatter.11
  709.7 35.1 reduce-scatter.7
  748.2 35.1 reduce-scatter.13
  786.4 95.0 reduce-scatter.15
  884.6 95.0 reduce-scatter.17
  982.6 95.0 reduce-scatter.19
  1080.5 182.9 all-reduce.13
where the time goes:
time: 1290 us; the launch traced here: 1280 us
  waiting for transfers between devices  685 us (53%)
  matrix products  438 us (34%)
  other arithmetic  65.6 us (5%)
  blocking collectives  50.7 us (4%)
  local copies, waits for them, and re-layouts  27.7 us (2%)
  between operations  17 us (1%)
    psum x1, waiting for transfers between devices, per_device(): lax.psum(owned[0].astype(jnp.bfloat16), 'rep').astype(jnp.float32)  115 us
    reduce_scatter x1, waiting for transfers between devices, per_device(): lax.psum_scatter(grad_up_w.astype(jnp.bfloat16), 'shard', scatter_dimensi...  98.2 us
    reduce_scatter x1, waiting for transfers between devices, per_device(): lax.psum_scatter(grad_gate_w.astype(jnp.bfloat16), 'shard', scatter_dimen...  98 us
    reduce_scatter x1, waiting for transfers between devices, per_device(): lax.psum_scatter(grad_down.astype(jnp.bfloat16), 'shard', scatter_dimensi...  98 us
    dot_general x7, matrix products, back_dot(): lax.dot_general(grad_rows, weight, (((1,), (1,)), ((), ())), preferred_el...  83.9 us
    all_gather x1, waiting for transfers between devices, per_device(): lax.all_gather(w_up, 'shard', axis=0, tiled=True)  81.8 us
    all_gather x1, waiting for transfers between devices, per_device(): lax.all_gather(w_down, 'shard', axis=0, tiled=True)  81.1 us
    dot_general x2, matrix products, block_backward(): jnp.einsum('kgqp,pkd->qkgd', grad_scores, key_rows, preferred_element_typ...  72.4 us
  transfers between devices with their start and end apart: 15, of which 10 were waited for; matrix products, arithmetic and copies ran while one was open for 23% of the time, Pallas kernels for 0%

commit v1 on v0

v1 whole, which is shorter than its diff:
```python
import functools

import jax
import jax.numpy as jnp
from jax import lax
from jax.experimental import pallas as pl
from jax.experimental.pallas import tpu as pltpu
from jax.sharding import PartitionSpec as P

HQ = 16
HK = 8
DH = 64
DOCS = 4
DOC_MAX = 512
EPS = 1e-05
ROPE_BASE = 1000000.0
AXES = ("shard", "rep")
PIECES = 3
GAIN_ROWS = 16
LOW = jnp.bfloat16
FULL = jnp.float32


def dot(first, second, first_dim, second_dim):
    return lax.dot_general(
        first, second, (((first_dim,), (second_dim,)), ((), ())), preferred_element_type=FULL
    )


def inverse_rms(values, axis):
    return lax.rsqrt(jnp.mean(values * values, axis=axis, keepdims=True) + EPS)


def norm_back(grad_in, normed, inverse, axis):
    return inverse * (grad_in - normed * jnp.mean(grad_in * normed, axis=axis, keepdims=True))


def doc_positions(doc_rows):
    kinds = jnp.arange(DOCS, dtype=jnp.int32)
    onehot = (doc_rows[:, :, None] == kinds[None, None, :]).astype(jnp.int32)
    counts = jnp.sum(onehot, axis=1)
    before = jnp.cumsum(counts, axis=1) - counts
    starts = jnp.sum(onehot * before[:, None, :], axis=2)
    return jnp.arange(doc_rows.shape[1], dtype=jnp.int32)[None, :] - starts


def rotate(values, cosine, sine):
    half = DH // 2
    first, second = values[:, :half], values[:, half:]
    return jnp.concatenate(
        [first * cosine - second * sine, second * cosine + first * sine], axis=1
    )


def unrotate(values, cosine, sine):
    half = DH // 2
    first, second = values[:, :half], values[:, half:]
    return jnp.concatenate(
        [first * cosine + second * sine, second * cosine - first * sine], axis=1
    )


class Links:
    def __init__(self, mesh):
        self.shards = mesh.shape["shard"]
        self.reps = mesh.shape["rep"]
        self.shard_bits = self.shards.bit_length() - 1
        self.rep_bits = self.reps.bit_length() - 1
        self.paired = self.shards == 4 and self.reps >= 4

    def here(self):
        return lax.axis_index("shard"), lax.axis_index("rep")

    def move(self, value, partner):
        pairs = []
        for shard in range(self.shards):
            for rep in range(self.reps):
                to_shard, to_rep = partner(shard, rep)
                pairs.append((shard * self.reps + rep, to_shard * self.reps + to_rep))
        return lax.ppermute(value, AXES, pairs)

    def shard_swap(self, value, bit):
        return self.move(value, lambda s, r: (s ^ (1 << bit), r))

    def rep_swap(self, value, bit):
        return self.move(value, lambda s, r: (s, r ^ (1 << bit)))

    def core_swap(self, value):
        return self.rep_swap(value, 0)

    def gather(self, value):
        shard, rep = self.here()
        if self.paired:
            first = self.move(value, lambda s, r: (s ^ (2 if r & 2 else 1), r))
            other = self.rep_swap(first, 1)
            last = self.move(first, lambda s, r: (s ^ (1 if r & 2 else 2), r))
            near = jnp.where((rep & 2) == 0, 1, 2)
            ids = jnp.stack([shard, shard ^ near, shard ^ (3 - near), shard ^ 3, shard])
            return [value, first, other, last], ids.astype(jnp.int32)
        whole = value[None]
        for bit in range(self.shard_bits):
            came = self.shard_swap(whole, bit)
            mine = (shard >> bit) & 1
            whole = jnp.where(
                mine == 0,
                jnp.concatenate([whole, came], axis=0),
                jnp.concatenate([came, whole], axis=0),
            )
        ids = jnp.concatenate([jnp.arange(self.shards), shard[None]])
        return [whole[block] for block in range(self.shards)], ids.astype(jnp.int32)

    def by_mark(self, blocks):
        shard, _ = self.here()
        wide = blocks.shape[2] // 2
        sides = []
        for stream, (_, leave, stay) in enumerate(block_orders(self.shard_bits)):
            part = blocks[:, :, stream * wide : (stream + 1) * wide]
            for marks in (leave, stay):
                sides.append(
                    jnp.stack(
                        [
                            lax.dynamic_index_in_dim(part, shard ^ mark, 0, keepdims=False)
                            for mark in marks
                        ]
                    )
                )
        return sides

    def total(self, sides, axis, tail):
        _, rep = self.here()
        streams = []
        for stream, (order, _, _) in enumerate(block_orders(self.shard_bits)):
            streams.append([order, sides[2 * stream], sides[2 * stream + 1]])
        for turn in range(self.shard_bits):
            came = [self.shard_swap(send, order[turn]) for order, send, _ in streams]
            token = yield [send for _, send, _ in streams]
            came = hold(came, token)
            for entry, arrived in zip(streams, came, strict=True):
                stay = entry[2]
                half = stay.shape[0] // 2
                if half:
                    entry[1] = add_low(stay[half:], arrived[half:])
                    entry[2] = add_low(stay[:half], arrived[:half])
                else:
                    entry[2] = add_low(stay, arrived)
        value = jnp.concatenate([entry[2][0] for entry in streams], axis=axis)
        if self.rep_bits != 3:
            for bit in range(1, self.rep_bits):
                value = add_low(value, self.rep_swap(value, bit))
        elif tail:
            quarter = value.shape[0] // 4
            place = rep >> 1
            pick = lambda at: lax.dynamic_slice_in_dim(value, at * quarter, quarter, 0)
            sends = [pick(place ^ mark) for mark in (1, 2, 3)]
            came = [self.rep_move(send, mark) for send, mark in zip(sends, (1, 2, 3), strict=True)]
            token = yield sends
            came = hold(came, token)
            mine = pick(place).astype(FULL)
            for arrived in came:
                mine = mine + arrived.astype(FULL)
            mine = mine.astype(LOW)
            came = [self.rep_move(mine, mark) for mark in (1, 2, 3)]
            token = yield [mine]
            value = jnp.zeros_like(value)
            for mark, part in enumerate([mine] + hold(came, token)):
                value = lax.dynamic_update_slice_in_dim(
                    value, part, (place ^ mark) * quarter, 0
                )
        else:
            came = self.rep_line(value, {0: 1, 3: 2})
            token = yield [value]
            value = add_low(value, hold([came], token)[0])
            came = self.rep_line(value, {1: 2, 2: 1})
            token = yield [value]
            value = add_low(value, hold([came], token)[0])
            came = self.rep_line(value, {1: 0, 2: 3})
            token = yield [value]
            middle = ((rep >> 1) == 1) | ((rep >> 1) == 2)
            value = jnp.where(middle, value, hold([came], token)[0])
        yield value

    def rep_move(self, value, mark):
        return self.move(value, lambda s, r: (s, r ^ (mark << 1)))

    def rep_line(self, value, targets):
        pairs = []
        for shard in range(self.shards):
            for rep in range(self.reps):
                if rep >> 1 in targets:
                    to = targets[rep >> 1] * 2 + (rep & 1)
                    pairs.append((shard * self.reps + rep, shard * self.reps + to))
        return lax.ppermute(value, AXES, pairs)


def add_low(first, second):
    return (first.astype(FULL) + second.astype(FULL)).astype(LOW)


def hold(values, token):
    if token is None:
        return list(values)
    return list(lax.optimization_barrier(tuple(values) + (token,))[:-1])


def block_orders(bits):
    for order in (list(range(bits)), list(range(bits))[::-1]):
        stay = [0]
        for bit in reversed(order[1:]):
            stay = stay + [m | (1 << bit) for m in stay]
        yield order, [m | (1 << order[0]) for m in stay], stay


def ffn_kernel(ids_ref, ffn_ref, cot_ref, *refs, shards, fresh):
    blocks = refs[:shards]
    refs = refs[shards:]
    if not fresh:
        out_in, back_in = refs[:2]
        refs = refs[2:]
    out_ref, back_ref = refs[:2]
    sides = refs[2:6]
    w_in, w_down, g_in, g_down, stage, sem, out_sem = refs[6:]
    model = ffn_ref.shape[1]
    own = model // shards
    wide = w_down.shape[0]
    step = wide // shards
    at_row = pl.program_id(0)
    parts = []
    for part in range(2 * wide // 256):
        parts.append((part * own, own, part * 256, True))
    for part in range(model // 256):
        parts.append((2 * wide // 256 * own + part * step, step, part * 256, False))

    @pl.when(at_row == 0)
    def _():
        copies = []
        for place, block in enumerate(blocks):
            shard = ids_ref[place]
            for start, count, column, first in parts:
                target = w_in if first else w_down
                row = pl.multiple_of(shard * count, count)
                copies.append(
                    pltpu.make_async_copy(
                        block.at[pl.ds(start, count)],
                        target.at[pl.ds(row, count), pl.ds(column, 256)],
                        sem,
                    )
                )
        for copy in copies:
            copy.start()
        g_in[...] = jnp.zeros_like(g_in)
        g_down[...] = jnp.zeros_like(g_down)
        for copy in copies:
            copy.wait()

    ffn = ffn_ref[...]
    cot = cot_ref[...]
    both = dot(ffn, w_in[...], 1, 0)
    grad_hidden = dot(cot, w_down[...], 1, 1)
    gate, upper = both[:, :wide], both[:, wide:]
    sigmoid = 1.0 / (1.0 + jnp.exp(-gate))
    silu = gate * sigmoid
    hidden = (silu * upper).astype(LOW)
    d_gate = (grad_hidden * upper * sigmoid * (1.0 + gate * (1.0 - sigmoid))).astype(LOW)
    d_up = (grad_hidden * silu).astype(LOW)
    d_both = jnp.concatenate([d_gate, d_up], axis=1)
    term = dot(hidden, w_down[...], 1, 0)
    out_ref[...] = term if fresh else out_in[...] + term
    term = dot(d_both, w_in[...], 1, 1)
    back_ref[...] = term if fresh else back_in[...] + term
    g_down[...] += dot(hidden, cot, 0, 0)
    g_in[...] += dot(ffn, d_both, 0, 0)

    @pl.when(at_row == pl.num_programs(0) - 1)
    def _():
        shard = ids_ref[shards]
        for mark in range(shards):
            block = lax.bitwise_xor(shard, jnp.int32(mark))
            for start, count, column, first in parts:
                source = g_in if first else g_down
                row = pl.multiple_of(block * count, count)
                stage[mark, start : start + count] = source[
                    pl.ds(row, count), column : column + 256
                ].astype(LOW)
        half = stage.shape[1] // 2
        copies = []
        for stream, (_, leave, stay) in enumerate(block_orders(shards.bit_length() - 1)):
            for side, marks in enumerate((leave, stay)):
                for slot, mark in enumerate(marks):
                    copies.append(
                        pltpu.make_async_copy(
                            stage.at[mark, pl.ds(stream * half, half)],
                            sides[2 * stream + side].at[slot],
                            out_sem,
                        )
                    )
        for copy in copies:
            copy.start()
        for copy in copies:
            copy.wait()


def ffn_piece(ids, ffn_pair, cot_pair, blocks, sums, tile=512):
    shards = len(blocks)
    rows = blocks[0].shape[0]
    count, model = ffn_pair.shape
    own = model // shards
    wide = shards * rows * 256 // (3 * model)
    fresh = sums is None
    tall = pl.BlockSpec((tile, model), lambda i, ids: (i, 0))
    where = pl.BlockSpec(memory_space=pl.ANY)
    sums = () if fresh else tuple(sums)
    side = jax.ShapeDtypeStruct((shards // 2, rows // 2, 256), LOW)
    total = jax.ShapeDtypeStruct((count, model), FULL)
    flops = 18 * count * model * wide
    return pl.pallas_call(
        functools.partial(ffn_kernel, shards=shards, fresh=fresh),
        grid_spec=pltpu.PrefetchScalarGridSpec(
            num_scalar_prefetch=1,
            grid=(count // tile,),
            in_specs=[tall, tall] + [where] * shards + [tall] * len(sums),
            out_specs=[tall, tall] + [where] * 4,
            scratch_shapes=[
                pltpu.VMEM((model, 2 * wide), LOW),
                pltpu.VMEM((wide, model), LOW),
                pltpu.VMEM((model, 2 * wide), FULL),
                pltpu.VMEM((wide, model), FULL),
                pltpu.VMEM((shards, rows, 256), LOW),
                pltpu.SemaphoreType.DMA,
                pltpu.SemaphoreType.DMA,
            ],
        ),
        out_shape=[total, total] + [side] * 4,
        input_output_aliases={} if fresh else {3 + shards: 0, 4 + shards: 1},
        compiler_params=pltpu.CompilerParams(vmem_limit_bytes=60 * 1024 * 1024),
        cost_estimate=pl.CostEstimate(flops=flops, bytes_accessed=40_000_000, transcendentals=0),
        name="ffn_piece",
    )(ids, ffn_pair, cot_pair, *blocks, *sums)


def query_blocks(length):
    size = min(256, length)
    for start in range(0, length, size):
        low = max(0, start - DOC_MAX)
        yield start, start + size, low


def attend_kernel(q_ref, k_ref, v_ref, mask_ref, o_ref, log_ref):
    length = q_ref.shape[1]
    value = jnp.concatenate([v_ref[...], jnp.ones((16, length), LOW)], axis=0)
    for group in range(HQ // HK):
        head = slice(group * DH, (group + 1) * DH)
        for start, end, low in query_blocks(length):
            scores = dot(k_ref[:, low:end], q_ref[head, start:end], 0, 0)
            terms = jnp.exp(scores).astype(LOW) * mask_ref[low:end, start:end]
            mixed = dot(value[:, low:end], terms, 1, 0)
            total = mixed[DH : DH + 1]
            o_ref[head, start:end] = (mixed[:DH] * (1.0 / total)).astype(LOW)
            log_ref[0, group : group + 1, start:end] = jnp.log(total)


def attend(q_low, k_low, v_low, mask):
    length = q_low.shape[1]
    wide = HQ // HK * DH
    return pl.pallas_call(
        attend_kernel,
        grid=(HK,),
        in_specs=[
            pl.BlockSpec((wide, length), lambda c: (c, 0)),
            pl.BlockSpec((DH, length), lambda c: (c, 0)),
            pl.BlockSpec((DH, length), lambda c: (c, 0)),
            pl.BlockSpec((length, length), lambda c: (0, 0)),
        ],
        out_specs=[
            pl.BlockSpec((wide, length), lambda c: (c, 0)),
            pl.BlockSpec((1, HQ // HK, length), lambda c: (c, 0, 0)),
        ],
        out_shape=[
            jax.ShapeDtypeStruct((HQ * DH, length), LOW),
            jax.ShapeDtypeStruct((HK, HQ // HK, length), FULL),
        ],
        compiler_params=pltpu.CompilerParams(vmem_limit_bytes=40 * 1024 * 1024),
        cost_estimate=pl.CostEstimate(
            flops=16_000_000_000, bytes_accessed=8_000_000, transcendentals=10_000_000
        ),
        name="attend",
    )(q_low, k_low, v_low, mask)


def row_pair(row, count):
    high = row.astype(LOW).astype(FULL)
    place = lax.broadcasted_iota(jnp.int32, (count, row.shape[1]), 0)
    return jnp.where(place == 0, high, jnp.where(place == 1, row - high, 0.0)).astype(LOW)


def attend_back_kernel(
    q_ref, k_ref, v_ref, o_ref, do_ref, log_ref, mask_ref, dq_ref, dk_ref, dv_ref, value_sum
):
    length = q_ref.shape[1]
    place = lax.broadcasted_iota(jnp.int32, (16, length), 0)
    twos = jnp.where(place < 2, 1.0, 0.0).astype(LOW)
    key = jnp.concatenate([k_ref[...], twos], axis=0)
    value = jnp.concatenate([v_ref[...], twos], axis=0)
    dk_ref[...] = jnp.zeros_like(dk_ref)
    value_sum[...] = jnp.zeros_like(value_sum)
    for group in range(HQ // HK):
        head = slice(group * DH, (group + 1) * DH)
        for start, end, low in query_blocks(length):
            q_blk = q_ref[head, start:end]
            do_blk = do_ref[head, start:end]
            inner = jnp.sum(
                do_blk.astype(FULL) * o_ref[head, start:end].astype(FULL), axis=0, keepdims=True
            )
            log_row = log_ref[0, group : group + 1, start:end]
            q_more = jnp.concatenate([q_blk, row_pair(-log_row, 16)], axis=0)
            do_more = jnp.concatenate([do_blk, row_pair(-inner, 16)], axis=0)
            mask = mask_ref[low:end, start:end]
            probs = jnp.exp(dot(key[:, low:end], q_more, 0, 0))
            grads = dot(value[:, low:end], do_more, 0, 0)
            probs_low = probs.astype(LOW) * mask
            grads_low = (probs * grads).astype(LOW) * mask
            dq_ref[head, start:end] = dot(k_ref[:, low:end], grads_low, 1, 0) * DH ** (-0.5)
            dk_ref[:, low:end] += dot(q_blk, grads_low, 1, 1)
            value_sum[:, low:end] += dot(do_blk, probs_low, 1, 1)
    dv_ref[...] = value_sum[...].astype(LOW)


def attend_back(q_low, k_low, v_low, o_low, do_low, log_total, mask):
    length = q_low.shape[1]
    wide = HQ // HK * DH
    two = pl.BlockSpec((wide, length), lambda c: (c, 0))
    one = pl.BlockSpec((DH, length), lambda c: (c, 0))
    return pl.pallas_call(
        attend_back_kernel,
        grid=(HK,),
        in_specs=[
            two,
            one,
            one,
            two,
            two,
            pl.BlockSpec((1, HQ // HK, length), lambda c: (c, 0, 0)),
            pl.BlockSpec((length, length), lambda c: (0, 0)),
        ],
        out_specs=[two, one, one],
        out_shape=[
            jax.ShapeDtypeStruct((HQ * DH, length), FULL),
            jax.ShapeDtypeStruct((HK * DH, length), FULL),
            jax.ShapeDtypeStruct((HK * DH, length), LOW),
        ],
        scratch_shapes=[pltpu.VMEM((DH, length), FULL)],
        compiler_params=pltpu.CompilerParams(vmem_limit_bytes=40 * 1024 * 1024),
        cost_estimate=pl.CostEstimate(
            flops=40_000_000_000, bytes_accessed=16_000_000, transcendentals=10_000_000
        ),
        name="attend_back",
    )(q_low, k_low, v_low, o_low, do_low, log_total, mask)


def per_device(
    links,
    tokens,
    doc_ids,
    w_query,
    w_key,
    w_value,
    w_out,
    w_gate,
    w_up,
    w_down,
    attn_gain,
    ffn_gain,
    query_gain,
    key_gain,
    cotangent,
):
    shards = links.shards
    _, rep = links.here()
    core = rep & 1
    count, model = tokens.shape
    own = model // shards
    half = own // 2
    kv_wide = HK * DH
    heads_own = DH // shards
    hidden_all = w_gate.shape[1]
    hidden_own = hidden_all // shards
    step = hidden_own // (2 * PIECES)
    packed_wide = model + 2 * kv_wide

    gains = jnp.concatenate([attn_gain, ffn_gain, query_gain, key_gain])
    gains = jnp.pad(gains, (0, packed_wide - gains.shape[0]))[None]
    gains = jnp.pad(gains, ((0, GAIN_ROWS - 1), (0, 0)))
    w_qkv = jnp.concatenate([w_query, w_key, w_value], axis=1)
    qkv_part = jnp.concatenate(
        [lax.dynamic_slice_in_dim(w_qkv, core * half, half, 0), gains], axis=0
    )
    qkv_blocks, ids = links.gather(qkv_part)
    (out_part,) = hold([lax.dynamic_slice_in_dim(w_out, core * half, half, 0)], qkv_part)
    out_blocks, _ = links.gather(out_part)

    def both_halves(blocks):
        mine = jnp.stack([block[:half] for block in blocks])
        theirs = links.core_swap(mine)
        whole = jnp.zeros((shards, 2, half, mine.shape[2]), LOW)
        for side, parts in ((core, mine), (1 - core, theirs)):
            for place in range(shards):
                whole = lax.dynamic_update_slice(
                    whole, parts[place][None, None], (ids[place], side, 0, 0)
                )
        return whole.reshape(model, mine.shape[2])

    ffn_weights = []
    marks = [qkv_blocks[1], out_blocks[1]]
    held = hold([w_gate, w_up, w_down, cotangent], qkv_part)
    cot_pair = jnp.concatenate([cotangent, links.core_swap(held[3])], axis=0)
    for piece in range(PIECES):
        def columns(weight):
            parts = []
            for block in range(shards):
                base = block * hidden_own + piece * step
                parts.append(
                    jnp.where(
                        core == 0,
                        weight[:, base : base + step],
                        weight[:, base + hidden_own // 2 : base + hidden_own // 2 + step],
                    )
                )
            return jnp.concatenate(parts, axis=1)

        down = lax.dynamic_slice_in_dim(
            held[2], core * (hidden_own // 2) + piece * step, step, 0
        )
        packed = jnp.concatenate(
            [
                part[:, at : at + 256]
                for part in (columns(held[0]), columns(held[1]), down)
                for at in range(0, part.shape[1], 256)
            ],
            axis=0,
        )
        (packed,) = hold([packed], marks[-2])
        blocks, _ = links.gather(packed)
        marks.append(blocks[1])
        ffn_weights.append(blocks)

    positions = doc_positions(doc_ids).reshape(count)
    freqs = jnp.power(ROPE_BASE, -2.0 * jnp.arange(DH // 2, dtype=FULL) / DH)
    angles = freqs[:, None] * positions.astype(FULL)[None, :]
    cosine, sine = jnp.cos(angles)[None], jnp.sin(angles)[None]
    index = jnp.arange(count)
    doc_row = doc_ids[0]
    mask = (
        (index[:, None] <= index[None, :]) & (doc_row[:, None] == doc_row[None, :])
    ).astype(LOW)

    x_in = tokens.astype(FULL)
    inv_one = inverse_rms(x_in, 1)
    x_hat = x_in * inv_one

    gain_rows = jnp.zeros((shards, packed_wide), LOW)
    for place, block in enumerate(qkv_blocks):
        gain_rows = lax.dynamic_update_slice(gain_rows, block[half][None], (ids[place], 0))
    gain_rows = gain_rows.astype(FULL)
    gain_attn = gain_rows[:, :own].reshape(model)
    gain_ffn = gain_rows[:, own : 2 * own].reshape(model)
    gain_query = gain_rows[:, 2 * own : 2 * own + heads_own].reshape(1, DH, 1)
    gain_key = gain_rows[:, 2 * own + heads_own : 2 * own + 2 * heads_own].reshape(1, DH, 1)
    qkv_full = both_halves(qkv_blocks)
    out_full = both_halves(out_blocks)

    attn_in = (x_hat * gain_attn).astype(LOW)
    qkv = dot(qkv_full, attn_in, 0, 1)
    q_heads = qkv[:model].reshape(HQ, DH, count)
    k_heads = qkv[model : model + kv_wide].reshape(HK, DH, count)
    v_low = qkv[model + kv_wide :].astype(LOW)
    q_inv = inverse_rms(q_heads, 1)
    q_hat = q_heads * q_inv
    k_inv = inverse_rms(k_heads, 1)
    k_hat = k_heads * k_inv
    q_low = (rotate(q_hat * gain_query, cosine, sine).astype(LOW) * DH ** (-0.5)).reshape(
        model, count
    )
    k_low = rotate(k_hat * gain_key, cosine, sine).astype(LOW).reshape(kv_wide, count)
    mix_low, log_total = attend(q_low, k_low, v_low, mask)

    resid = x_in + dot(mix_low, out_full, 0, 0)
    inv_two = inverse_rms(resid, 1)
    resid_hat = resid * inv_two
    ffn_in = (resid_hat * gain_ffn).astype(LOW)
    ffn_pair = jnp.concatenate([ffn_in, links.core_swap(ffn_in)], axis=0)

    sums, sends = None, None
    ffn_totals = []
    for blocks in ffn_weights:
        (order,) = hold([ids], sends) if sends is not None else [ids]
        *sums, leave_a, stay_a, leave_b, stay_b = ffn_piece(
            order, ffn_pair, cot_pair, blocks, sums
        )
        sends = None
        for entry in ffn_totals:
            entry[1] = entry[0].send(stay_a)
            sends = entry[1][0]
        flow = links.total([leave_a, stay_a, leave_b, stay_b], 0, False)
        ffn_totals.append([flow, next(flow)])

    out_sum, ffn_back = sums
    back_other = links.core_swap(ffn_back[count:].astype(LOW))
    out_other = links.core_swap(out_sum[count:].astype(LOW))
    grad_ffn_in = ffn_back[:count] + back_other.astype(FULL)
    grad_gain_ffn = jnp.sum(grad_ffn_in * resid_hat, axis=0)
    grad_resid = cotangent.astype(FULL) + norm_back(grad_ffn_in * gain_ffn, resid_hat, inv_two, 1)
    grad_resid_low = grad_resid.astype(LOW)
    result = (resid + out_sum[:count] + out_other.astype(FULL)).astype(LOW)

    def half_sum(grad):
        blocks = grad.reshape(shards, 2, half, grad.shape[1])
        keep = lax.dynamic_index_in_dim(blocks, core, 1, keepdims=False)
        give = lax.dynamic_index_in_dim(blocks, 1 - core, 1, keepdims=False)
        return add_low(keep, links.core_swap(give))

    def owned(part):
        theirs = links.core_swap(part)
        low = jnp.where(core == 0, part, theirs)
        high = jnp.where(core == 0, theirs, part)
        return jnp.concatenate([low, high], axis=0).astype(FULL)

    grad_mix = dot(out_full, grad_resid_low, 1, 1).astype(LOW)
    grad_out_w = dot(mix_low, grad_resid_low, 1, 0).astype(LOW)
    out_flow = links.total(links.by_mark(half_sum(grad_out_w)), 1, True)
    flows = [entry[0] for entry in ffn_totals] + [out_flow]
    done = [None] * len(flows)

    def advance(token):
        sent = None
        for place, flow in enumerate(flows):
            if done[place] is None:
                got = flow.send(token)
                if isinstance(got, list):
                    sent = got[0]
                else:
                    done[place] = got
        return sent

    sent_out = next(out_flow)
    flows_now = flows
    flows = flows[:-1]
    sent = advance(grad_mix)
    flows = flows_now
    (do_low,) = hold([grad_mix], sent)
    (do_low,) = hold([do_low], sent_out[0])
    dq_rot, dk_rot, dv_low = attend_back(q_low, k_low, v_low, mix_low, do_low, log_total, mask)
    sent = advance(dv_low)
    (dq_rot, dk_rot) = hold([dq_rot, dk_rot], sent)
    dq_norm = unrotate(dq_rot.reshape(HQ, DH, count), cosine, sine)
    dk_norm = unrotate(dk_rot.reshape(HK, DH, count), cosine, sine)
    grad_gain_query = jnp.sum(dq_norm * q_hat, axis=(0, 2))
    grad_gain_key = jnp.sum(dk_norm * k_hat, axis=(0, 2))
    dq_low = norm_back(dq_norm * gain_query, q_hat, q_inv, 1).astype(LOW).reshape(model, count)
    dk_low = norm_back(dk_norm * gain_key, k_hat, k_inv, 1).astype(LOW).reshape(kv_wide, count)
    d_qkv = jnp.concatenate([dq_low, dk_low, dv_low], axis=0)
    grad_qkv_w = dot(attn_in, d_qkv, 0, 1).astype(LOW)
    (d_qkv_later,) = hold([d_qkv], grad_qkv_w)
    grad_attn_in = dot(d_qkv_later, qkv_full, 0, 1)
    grad_gain_attn = jnp.sum(grad_attn_in * x_hat, axis=0)
    grad_input = grad_resid + norm_back(grad_attn_in * gain_attn, x_hat, inv_one, 1)

    gain_grads = jnp.concatenate(
        [
            grad_gain_attn.reshape(shards, own),
            grad_gain_ffn.reshape(shards, own),
            grad_gain_query.reshape(shards, heads_own),
            grad_gain_key.reshape(shards, heads_own),
        ],
        axis=1,
    ).astype(LOW)
    used = gain_grads.shape[1]
    gain_grads = add_low(gain_grads, links.core_swap(gain_grads))
    gain_grads = jnp.pad(gain_grads, ((0, 0), (0, packed_wide - used)))[:, None]
    gain_grads = jnp.pad(gain_grads, ((0, 0), (0, GAIN_ROWS - 1), (0, 0)))
    qkv_flow = links.total(
        links.by_mark(jnp.concatenate([half_sum(grad_qkv_w), gain_grads], axis=1)), 1, True
    )
    flows = flows + [qkv_flow]
    done = done + [None]
    next(qkv_flow)
    token = grad_attn_in
    while None in done:
        advance(token)
        token = None
    qkv_sum, out_w_sum = done[-1], done[-2]
    gain_sum = qkv_sum[half].astype(FULL)
    grad_qkv = owned(qkv_sum[:half])
    grad_out_w = owned(out_w_sum)
    ffn_grads = []
    for part in done[:PIECES]:
        both = []
        for whole in (part, links.core_swap(part)):
            tall = 2 * hidden_all // (2 * PIECES) // 256 * own
            blocks = [whole[at : at + own] for at in range(0, tall, own)]
            middle = len(blocks) // 2
            both += [
                jnp.concatenate(blocks[:middle], axis=1),
                jnp.concatenate(blocks[middle:], axis=1),
                jnp.concatenate(
                    [whole[at : at + step] for at in range(tall, whole.shape[0], step)], axis=1
                ),
            ]
        ffn_grads.append(both)

    gate_parts = []
    up_parts = []
    down_parts = []
    for block in range(shards):
        for side in range(2):
            for gate, up, _, gate_other, up_other, _ in ffn_grads:
                at = block * step
                span = slice(at, at + step)
                gate_parts.append(jnp.where(core == side, gate[:, span], gate_other[:, span]))
                up_parts.append(jnp.where(core == side, up[:, span], up_other[:, span]))
    for side in range(2):
        for _, _, down, _, _, down_other in ffn_grads:
            down_parts.append(jnp.where(core == side, down, down_other))
    return (
        result,
        grad_input,
        grad_qkv[:, :model],
        grad_qkv[:, model : model + kv_wide],
        grad_qkv[:, model + kv_wide :],
        grad_out_w,
        jnp.concatenate(gate_parts, axis=1).astype(FULL),
        jnp.concatenate(up_parts, axis=1).astype(FULL),
        jnp.concatenate(down_parts, axis=0).astype(FULL),
        gain_sum[:own],
        gain_sum[own : 2 * own],
        gain_sum[2 * own : 2 * own + heads_own],
        gain_sum[2 * own + heads_own : 2 * own + 2 * heads_own],
    )


def solution(mesh):
    both = P(("shard", "rep"), None)
    rows = P("shard", None)
    line = P("shard")
    in_specs = (both, both) + (rows,) * 7 + (line,) * 4 + (both,)
    out_specs = (both, both) + (rows,) * 7 + (line,) * 4
    return jax.shard_map(
        functools.partial(per_device, Links(mesh)),
        mesh=mesh,
        in_specs=in_specs,
        out_specs=out_specs,
        check_vma=False,
    )
```

time: 1290 us -> 710 us (0.55)
  waiting for transfers between devices: 685 us -> 172 us
  matrix products: 438 us -> 37.8 us
  Pallas kernels: 0 us -> 174 us
  starting transfers between devices: 0.77 us -> 86.5 us
  local copies, waits for them, and re-layouts: 27.7 us -> 98.1 us
  other arithmetic: 65.6 us -> 130 us
  blocking collectives: 50.7 us -> 0 us
  between operations: 17 us -> 3.11 us
    dot_general x33 -> x6, matrix products: 438 us -> 37.8 us  [dot(): lax.dot_general(first, second, (((first_dim,), (second_dim,)), ((), ())),...]
    reduce_scatter x7 -> x0, waiting for transfers between devices: 305 us -> none  [the longest x1 98.2 us: per_device(): lax.psum_scatter(grad_up_w.astype(jnp.bfloat16), 'shard', scatter_dimensi...]
    all_gather x7 -> x0, waiting for transfers between devices: 260 us -> none  [the longest x1 81.8 us: per_device(): lax.all_gather(w_up, 'shard', axis=0, tiled=True)]
    pallas_call x0 -> x5, Pallas kernels: none -> 174 us  [the longest x3 124 us: ffn_piece(): pl.pallas_call(functools.partial(ffn_kernel, shards=shards, fresh=fresh),...]
    ppermute x0 -> x70, waiting for transfers between devices: none -> 172 us  [the longest x61 144 us: move(): return lax.ppermute(value, AXES, pairs)]
    psum x1 -> x0, waiting for transfers between devices: 115 us -> none  [per_device(): lax.psum(owned[0].astype(jnp.bfloat16), 'rep').astype(jnp.float32)]
    ppermute x0 -> x70, starting transfers between devices: none -> 86.5 us  [the longest x61 64.6 us: move(): return lax.ppermute(value, AXES, pairs)]
    dynamic_update_slice x0 -> x26, local copies, waits for them, and re-layouts: none -> 32.1 us  [the longest x15 24.8 us: both_halves(): lax.dynamic_update_slice(whole, parts[place][None, None], (ids[place], si...]
  transfers between devices with their start and end apart: 15 -> 70, of which waited for: 10 -> 19; matrix products, arithmetic and copies ran while one was open for 23% -> 32% of each run, Pallas kernels for 0% -> 25%
where the time goes in v1:
time: 710 us; the launch traced here: 701 us
  Pallas kernels  174 us (25%)
  waiting for transfers between devices  172 us (24%)
  other arithmetic  130 us (18%)
  local copies, waits for them, and re-layouts  98.1 us (14%)
  starting transfers between devices  86.5 us (12%)
  matrix products  37.8 us (5%)
    ppermute x61, waiting for transfers between devices, move(): return lax.ppermute(value, AXES, pairs)  144 us
    pallas_call x3, Pallas kernels, ffn_piece(): pl.pallas_call(functools.partial(ffn_kernel, shards=shards, fresh=fresh),...  124 us
    ppermute x61, starting transfers between devices, move(): return lax.ppermute(value, AXES, pairs)  64.6 us
    dot_general x6, matrix products, dot(): lax.dot_general(first, second, (((first_dim,), (second_dim,)), ((), ())),...  37.8 us
    pallas_call x1, Pallas kernels, attend_back(): pl.pallas_call(attend_back_kernel, grid=(HK,), in_specs=[two, one, one, t...  30.8 us
    ppermute x9, waiting for transfers between devices, rep_line(): return lax.ppermute(value, AXES, pairs)  28.1 us
    dynamic_update_slice x15, local copies, waits for them, and re-layouts, both_halves(): lax.dynamic_update_slice(whole, parts[place][None, None], (ids[place], si...  24.8 us
    convert_element_type x19, other arithmetic, add_low(): return (first.astype(FULL) + second.astype(FULL)).astype(LOW)  24.5 us
  transfers between devices with their start and end apart: 70, of which 19 were waited for; matrix products, arithmetic and copies ran while one was open for 32% of the time, Pallas kernels for 25%

profile of v1, /device:TPU:0, one launch (start us, length us, event | category | flops | bytes accessed | tf_op | source)
XLA Modules:
  0.0 701.3 jit_solution(14443599648746081743)
XLA Ops:
  1.6 2.5 broadcast_in_dim.14
  5.9 2.9 collective-permute-start
  9.5 3.1 slice_select_fusion.4
  68.4 10.6 %collective-permute-done.2 = bf16[144,2048]{1,0:T(8,128)(2,1)} collective-permute-done((bf16[144,2048]{1,0:T(8,128)(2,1)}, bf16[144,2048]{1,0:T(8,128)(2,1)}, u32[]{:S(2)}, u32[]{:S(2)}) %collective-permute-start.2) | collective-permute-done | bytes 589856 | tf_op jit(solution)/shard_map/ppermute | solution.py:80
  103.0 6.7 fusion.27
  115.5 19.8 %attend.1 = (bf16[1024,1024]{1,0:T(8,128)(2,1)S(1)}, f32[8,2,1024]{2,1,0:T(2,128)S(1)}) custom-call(bf16[1024,1024]{1,0:T(8,128)(2,1)S(1)} %bitcast.182, bf16[512,1024]{1,0:T(8,128)(2,1)S(1)} %bitcast.185, bf16[512,1024]{1,0:T(8,128)(2,1)S(1)} %slice.1520.v_ref, bf16[1024,1024]{1,0:T(8,128)(2,1)S(1)} %fusion.17.mask_ref), custom_call_target="tpu_custom_call" | custom-call | flops 16000000000 | bytes 8000000 | tf_op jit(solution)/shard_map/attend/pallas_call | solution.py:364
  135.3 5.0 multiply_reduce_fusion.3
  147.1 25.6 %collective-permute-done.15.refs_1_ = bf16[2304,256]{1,0:T(8,128)(2,1)} collective-permute-done((bf16[2304,256]{1,0:T(8,128)(2,1)}, bf16[2304,256]{1,0:T(8,128)(2,1)}, u32[]{:S(2)}, u32[]{:S(2)}) %collective-permute-start.15) | collective-permute-done | bytes 1179680 | tf_op jit(solution)/shard_map/ppermute | solution.py:80
  174.6 3.1 constant_dynamic-update-slice_fusion.1
  179.7 3.1 constant_dynamic-update-slice_fusion.cot_ref
  182.8 14.1 %collective-permute-done.18.refs_1_ = bf16[2304,256]{1,0:T(8,128)(2,1)} collective-permute-done((bf16[2304,256]{1,0:T(8,128)(2,1)}, bf16[2304,256]{1,0:T(8,128)(2,1)}, u32[]{:S(2)}, u32[]{:S(2)}) %collective-permute-start.18) | collective-permute-done | bytes 1179680 | tf_op jit(solution)/shard_map/ppermute | solution.py:80
  199.0 4.7 pad_maximum_fusion.ffn_ref
  205.3 39.6 %ffn_piece.3 = (f32[2048,1024]{1,0:T(8,128)}, f32[2048,1024]{1,0:T(8,128)}, bf16[2,1152,256]{2,1,0:T(8,128)(2,1)}, bf16[2,1152,256]{2,1,0:T(8,128)(2,1)}, bf16[2...) custom-call(s32[5]{0:T(128)} %stack.88.ids_ref, bf16[2048,1024]{1,0:T(8,128)(2,1)} %pad_maximum_fusion.ffn_ref, ...), custom_call_target="tpu_custom_call" | custom-call | flops 28991029248 | bytes 40000000 | tf_op jit(solution)/shard_map/ffn_piece/pallas_call | solution.py:315
  246.9 42.2 %ffn_piece.4 = (f32[2048,1024]{1,0:T(8,128)}, f32[2048,1024]{1,0:T(8,128)}, bf16[2,1152,256]{2,1,0:T(8,128)(2,1)}, bf16[2,1152,256]{2,1,0:T(8,128)(2,1)}, bf16[2...) custom-call(s32[5]{0:T(128)} %stack.88.ids_ref, ...), custom_call_target="tpu_custom_call", output_to_operand_aliasing={{0}: (7, {}), {1}: (8, {})} | custom-call | flops 28991029248 | bytes 40000000 | tf_op jit(solution)/shard_map/ffn_piece/pallas_call | solution.py:315
  294.0 41.8 %ffn_piece.5 = (f32[2048,1024]{1,0:T(8,128)}, f32[2048,1024]{1,0:T(8,128)}, bf16[2,1152,256]{2,1,0:T(8,128)(2,1)}, bf16[2,1152,256]{2,1,0:T(8,128)(2,1)}, bf16[2...) custom-call(s32[5]{0:T(128)} %stack.88.ids_ref, ...), custom_call_target="tpu_custom_call", output_to_operand_aliasing={{0}: (7, {}), {1}: (8, {})} | custom-call | flops 28991029248 | bytes 40000000 | tf_op jit(solution)/shard_map/ffn_piece/pallas_call | solution.py:315
  335.8 2.6 slice.1518
  338.5 2.7 slice.1519
  351.5 33.1 %collective-permute-done.51 = bf16[1,1152,256]{2,1,0:T(8,128)(2,1)S(1)} collective-permute-done((bf16[1,1152,256]{2,1,0:T(8,128)(2,1)S(1)}, bf16[1,1152,256]{2,1,0:T(8,128)(2,1)S(1)}, u32[]{:S(2)}, u32[]{:S(2)}) %collective-permute-start.51) | collective-permute-done | bytes 589856 | tf_op jit(solution)/shard_map/ppermute | solution.py:80
  392.8 3.2 collective-permute-start.52
  396.0 5.5 multiply_add_fusion
  401.5 6.9 convolution_convert_fusion.2.do_ref
  410.3 2.4 convolution_convert_fusion.1
  415.1 4.2 collective-permute-done.52
  419.3 3.0 add_convert_fusion.6
  427.3 8.5 %collective-permute-start.60 = (bf16[2304,256]{1,0:T(8,128)(2,1)}, bf16[2304,256]{1,0:T(8,128)(2,1)}, u32[]{:S(2)}, u32[]{:S(2)}) collective-permute-start(bf16[2304,256]{1,0:T(8,128)(2,1)} %pad_maximum_fusion.6), channel_id=1, source_target_pairs={{0,2},{1,3},{6,4},{7,5},{8,10},{9,11},{14,12},{15,13},{16,18},{17,... | collective-permute-start | bytes 3538952 | tf_op jit(solution)/shard_map/ppermute | solution.py:192
  440.8 30.8 %attend_back.1 = (f32[1024,1024]{1,0:T(8,128)}, f32[512,1024]{1,0:T(8,128)S(1)}, bf16[512,1024]{1,0:T(8,128)(2,1)S(1)}) custom-call(bf16[1024,1024]{1,0:T(8,128)(2,1)S(1)} %bitcast.183, bf16[512,1024]{1,0:T(8,128)(2,1)S(1)} %bitcast.186, bf16[512,1024]{1,0:T(8,128)(2,1)S(1)} %slice.1520.v_ref, bf16[1024,1024]{1,0:T(8,128)(2,1)S(1)} %copy-done.8, ...), custom_call_target="tpu_custom_call" | custom-call | flops 40000000000 | bytes 16000000 | tf_op jit(solution)/shard_map/attend_back/pallas_call | solution.py:432
  475.2 2.6 collective-permute-start.66
  494.7 8.7 %convolution_convert_fusion = bf16[1024,2048]{1,0:T(8,128)(2,1)} fusion(bf16[1024,1024]{1,0:T(8,128)(2,1)S(1)} %copy-done.18, f32[1024]{0:T(1024)S(1)} %bitcast.204, f32[1024]{0:T(1024)S(1)} %copy-done.109, bf16[512,1024]{1,0:T(8,128)(2,1)S(1)} %get-tuple-element.104, bf16[512,1024]{1,0:T(8,128)(2,1)S(1)} %get-tuple-element.146, ...), kind=kOutput, calls=%fused_computation.44 | convolution fusion | flops 4313841664 | bytes 10493952 | tf_op jit(solution)/shard_map/dot_general | solution.py:25
  505.0 8.1 %fusion.10 = (bf16[1024]{0:T(1024)(128)(2,1)}, f32[1024]{0:T(1024)S(1)}, f32[1024,1024]{1,0:T(8,128)S(1)}) fusion(bf16[1024,1024]{1,0:T(8,128)(2,1)S(1)} %copy-done.18, f32[1024]{0:T(1024)S(1)} %copy-done.109, f32[1024]{0:T(1024)S(1)} %bitcast.205, bf16[2048,1024]{1,0:T(8,128)(2,1)S(1)} %pad_maximum_fusion.2, bf16[1024,2048]{1,0:T(8,128)(2,1)} %bitcast.12), kind=kOutput, calls=%fused_computation.16 | convolution fusion | flops 4302305280 | bytes 14694400 | tf_op jit(solution)/shard_map/dot_general | solution.py:25
  516.0 2.7 fusion.9
  524.5 4.3 collective-permute-start.44
  530.4 3.3 collective-permute-done.44
  538.4 2.6 collective-permute-start.47
  541.0 20.9 %collective-permute-done.47 = bf16[32,1024]{1,0:T(8,128)(2,1)S(1)} collective-permute-done((bf16[32,1024]{1,0:T(8,128)(2,1)S(1)}, bf16[32,1024]{1,0:T(8,128)(2,1)S(1)}, u32[]{:S(2)}, u32[]{:S(2)}) %collective-permute-start.47) | collective-permute-done | bytes 65568 | tf_op jit(solution)/shard_map/ppermute | solution.py:80
  562.8 5.1 collective-permute-done.48
  568.7 3.8 collective-permute-done.49
  584.7 23.8 %collective-permute-done.62 = bf16[2304,256]{1,0:T(8,128)(2,1)S(1)} collective-permute-done((bf16[2304,256]{1,0:T(8,128)(2,1)S(1)}, bf16[2304,256]{1,0:T(8,128)(2,1)S(1)}, u32[]{:S(2)}, u32[]{:S(2)}) %collective-permute-start.62) | collective-permute-done | bytes 1179680 | tf_op jit(solution)/shard_map/ppermute | solution.py:192
  614.2 7.1 %collective-permute-done.32 = bf16[1,144,1024]{2,1,0:T(8,128)(2,1)S(1)} collective-permute-done((bf16[1,144,1024]{2,1,0:T(8,128)(2,1)S(1)}, bf16[1,144,1024]{2,1,0:T(8,128)(2,1)S(1)}, u32[]{:S(2)}, u32[]{:S(2)}) %collective-permute-start.32) | collective-permute-done | bytes 294944 | tf_op jit(solution)/shard_map/ppermute | solution.py:80
  623.0 7.9 %collective-permute-start.35 = (bf16[36,2048]{1,0:T(8,128)(2,1)S(1)}, bf16[36,2048]{1,0:T(8,128)(2,1)S(1)}, u32[]{:S(2)}, u32[]{:S(2)}) collective-permute-start(bf16[36,2048]{1,0:T(8,128)(2,1)S(1)} %get-tuple-element.293), channel_id=1, source_target_pairs={{0,4},{1,5},{2,6},{3,7},{4,0},{5,1},{6,2},{7,3},{8,12},{9,13},{10,... | collective-permute-start | bytes 442376 | tf_op jit(solution)/shard_map/ppermute | solution.py:80
  632.8 7.4 %collective-permute-done.35 = bf16[36,2048]{1,0:T(8,128)(2,1)S(1)} collective-permute-done((bf16[36,2048]{1,0:T(8,128)(2,1)S(1)}, bf16[36,2048]{1,0:T(8,128)(2,1)S(1)}, u32[]{:S(2)}, u32[]{:S(2)}) %collective-permute-start.35) | collective-permute-done | bytes 147488 | tf_op jit(solution)/shard_map/ppermute | solution.py:80
  640.3 3.5 collective-permute-done.34
  646.1 2.9 collective-permute-start.39
  656.5 3.4 collective-permute-done.38
  681.1 4.3 concatenate.298
  685.6 2.7 convert_element_type.640
  689.4 4.3 concatenate.311
  693.9 2.7 convert_element_type.641
  698.3 2.7 convert_element_type.642
  (570 shorter events, 235.4 us)
Async XLA Ops:
  5.9 55.7 %collective-permute-start = (bf16[144,2048]{1,0:T(8,128)(2,1)}, bf16[144,2048]{1,0:T(8,128)(2,1)}, u32[]{:S(2)}, u32[]{:S(2)}) collective-permute-start(bf16[144,2048]{1,0:T(8,128)(2,1)} %fusion.29), channel_id=1, source_target_pairs={{0,8},{1,9},{2,18},{3,19},{4,12},{5,13},{6,22},{7,23},{8,0},{9,1},... | collective-permute-start | bytes 1769480 | tf_op jit(solution)/shard_map/ppermute | solution.py:80
  8.9 37.4 %collective-permute-start.4 = (bf16[128,1024]{1,0:T(8,128)(2,1)S(1)}, bf16[128,1024]{1,0:T(8,128)(2,1)}, u32[]{:S(2)}, u32[]{:S(2)}) collective-permute-start(bf16[128,1024]{1,0:T(8,128)(2,1)S(1)} %constant_dynamic-slice_fusion.8), channel_id=1, source_target_pairs={{0,8},{1,9},{2,18},{3,19},{4,12},{5,13},{6,22},{7,23},{8,0},{9,1},... | collective-permute-start | bytes 786440 | tf_op jit(solution)/shard_map/ppermute | solution.py:80
  8.9 170.1 %collective-permute-start.9 = (bf16[1024,1024]{1,0:T(8,128)(2,1)}, bf16[1024,1024]{1,0:T(8,128)(2,1)}, u32[]{:S(2)}, u32[]{:S(2)}) collective-permute-start(bf16[1024,1024]{1,0:T(8,128)(2,1)} %param.27), channel_id=1, source_target_pairs={{0,1},{1,0},{2,3},{3,2},{4,5},{5,4},{6,7},{7,6},{8,9},{9,8},{10,11... | collective-permute-start | bytes 6291464 | tf_op jit(solution)/shard_map/ppermute | solution.py:80
  59.2 29.5 %collective-permute-start.7 = (bf16[4,128,1024]{2,1,0:T(8,128)(2,1)}, bf16[4,128,1024]{2,1,0:T(8,128)(2,1)}, u32[]{:S(2)}, u32[]{:S(2)}) collective-permute-start(bf16[4,128,1024]{2,1,0:T(8,128)(2,1)} %pad_maximum_fusion.9), channel_id=1, source_target_pairs={{0,1},{1,0},{2,3},{3,2},{4,5},{5,4},{6,7},{7,6},{8,9},{9,8},{10,11... | collective-permute-start | bytes 3145736 | tf_op jit(solution)/shard_map/ppermute | solution.py:80
  61.6 83.4 %collective-permute-start.10 = (bf16[2304,256]{1,0:T(8,128)(2,1)}, bf16[2304,256]{1,0:T(8,128)(2,1)}, u32[]{:S(2)}, u32[]{:S(2)}) collective-permute-start(bf16[2304,256]{1,0:T(8,128)(2,1)} %get-tuple-element.80.refs_0_), channel_id=1, source_target_pairs={{0,8},{1,9},{2,18},{3,19},{4,12},{5,13},{6,22},{7,23},{8,0},{9,1},... | collective-permute-start | bytes 3538952 | tf_op jit(solution)/shard_map/ppermute | solution.py:80
  63.1 17.0 %collective-permute-start.1 = (bf16[144,2048]{1,0:T(8,128)(2,1)}, bf16[144,2048]{1,0:T(8,128)(2,1)}, u32[]{:S(2)}, u32[]{:S(2)}) collective-permute-start(bf16[144,2048]{1,0:T(8,128)(2,1)} %collective-permute-done), channel_id=1, source_target_pairs={{0,2},{1,3},{2,0},{3,1},{4,6},{5,7},{6,4},{7,5},{8,10},{9,11},{10,... | collective-permute-start | bytes 1769480 | tf_op jit(solution)/shard_map/ppermute | solution.py:80
  142.9 55.4 %collective-permute-start.8 = (bf16[1024,1024]{1,0:T(8,128)(2,1)}, bf16[1024,1024]{1,0:T(8,128)(2,1)}, u32[]{:S(2)}, u32[]{:S(2)}) collective-permute-start(bf16[1024,1024]{1,0:T(8,128)(2,1)} %multiply_convert_fusion), channel_id=1, source_target_pairs={{0,1},{1,0},{2,3},{3,2},{4,5},{5,4},{6,7},{7,6},{8,9},{9,8},{10,11... | collective-permute-start | bytes 6291464 | tf_op jit(solution)/shard_map/ppermute | solution.py:80
  143.5 29.2 %collective-permute-start.15 = (bf16[2304,256]{1,0:T(8,128)(2,1)}, bf16[2304,256]{1,0:T(8,128)(2,1)}, u32[]{:S(2)}, u32[]{:S(2)}) collective-permute-start(bf16[2304,256]{1,0:T(8,128)(2,1)} %get-tuple-element.84.refs_0_), channel_id=1, source_target_pairs={{0,8},{1,9},{2,18},{3,19},{4,12},{5,13},{6,22},{7,23},{8,0},{9,1},... | collective-permute-start | bytes 3538952 | tf_op jit(solution)/shard_map/ppermute | solution.py:80
  145.0 52.0 %collective-permute-start.18 = (bf16[2304,256]{1,0:T(8,128)(2,1)}, bf16[2304,256]{1,0:T(8,128)(2,1)}, u32[]{:S(2)}, u32[]{:S(2)}) collective-permute-start(bf16[2304,256]{1,0:T(8,128)(2,1)} %get-tuple-element.90.refs_0_), channel_id=1, source_target_pairs={{0,8},{1,9},{2,18},{3,19},{4,12},{5,13},{6,22},{7,23},{8,0},{9,1},... | collective-permute-start | bytes 3538952 | tf_op jit(solution)/shard_map/ppermute | solution.py:80
  145.5 58.2 %collective-permute-start.11 = (bf16[2304,256]{1,0:T(8,128)(2,1)}, bf16[2304,256]{1,0:T(8,128)(2,1)}, u32[]{:S(2)}, u32[]{:S(2)}) collective-permute-start(bf16[2304,256]{1,0:T(8,128)(2,1)} %collective-permute-done.10.refs_1_), channel_id=1, source_target_pairs={{0,2},{1,3},{2,0},{3,1},{4,6},{5,7},{6,4},{7,5},{8,10},{9,11},{10,... | collective-permute-start | bytes 3538952 | tf_op jit(solution)/shard_map/ppermute | solution.py:80
  172.6 32.6 %collective-permute-start.12 = (bf16[2304,256]{1,0:T(8,128)(2,1)}, bf16[2304,256]{1,0:T(8,128)(2,1)}, u32[]{:S(2)}, u32[]{:S(2)}) collective-permute-start(bf16[2304,256]{1,0:T(8,128)(2,1)} %collective-permute-done.10.refs_1_), channel_id=1, source_target_pairs={{0,16},{1,17},{2,10},{3,11},{4,20},{5,21},{6,14},{7,15},{8,24},{9,... | collective-permute-start | bytes 3538952 | tf_op jit(solution)/shard_map/ppermute | solution.py:80
  179.0 67.4 %collective-permute-start.16 = (bf16[2304,256]{1,0:T(8,128)(2,1)}, bf16[2304,256]{1,0:T(8,128)(2,1)}, u32[]{:S(2)}, u32[]{:S(2)}) collective-permute-start(bf16[2304,256]{1,0:T(8,128)(2,1)} %collective-permute-done.15.refs_1_), channel_id=1, source_target_pairs={{0,2},{1,3},{2,0},{3,1},{4,6},{5,7},{6,4},{7,5},{8,10},{9,11},{10,... | collective-permute-start | bytes 3538952 | tf_op jit(solution)/shard_map/ppermute | solution.py:80
  196.9 49.9 %collective-permute-start.17 = (bf16[2304,256]{1,0:T(8,128)(2,1)}, bf16[2304,256]{1,0:T(8,128)(2,1)}, u32[]{:S(2)}, u32[]{:S(2)}) collective-permute-start(bf16[2304,256]{1,0:T(8,128)(2,1)} %collective-permute-done.15.refs_1_), channel_id=1, source_target_pairs={{0,16},{1,17},{2,10},{3,11},{4,20},{5,21},{6,14},{7,15},{8,24},{9,... | collective-permute-start | bytes 3538952 | tf_op jit(solution)/shard_map/ppermute | solution.py:80
  198.3 95.7 %collective-permute-start.19 = (bf16[2304,256]{1,0:T(8,128)(2,1)}, bf16[2304,256]{1,0:T(8,128)(2,1)}, u32[]{:S(2)}, u32[]{:S(2)}) collective-permute-start(bf16[2304,256]{1,0:T(8,128)(2,1)} %collective-permute-done.18.refs_1_), channel_id=1, source_target_pairs={{0,2},{1,3},{2,0},{3,1},{4,6},{5,7},{6,4},{7,5},{8,10},{9,11},{10,... | collective-permute-start | bytes 3538952 | tf_op jit(solution)/shard_map/ppermute | solution.py:80
  203.7 90.2 %collective-permute-start.20 = (bf16[2304,256]{1,0:T(8,128)(2,1)}, bf16[2304,256]{1,0:T(8,128)(2,1)}, u32[]{:S(2)}, u32[]{:S(2)}) collective-permute-start(bf16[2304,256]{1,0:T(8,128)(2,1)} %collective-permute-done.18.refs_1_), channel_id=1, source_target_pairs={{0,16},{1,17},{2,10},{3,11},{4,20},{5,21},{6,14},{7,15},{8,24},{9,... | collective-permute-start | bytes 3538952 | tf_op jit(solution)/shard_map/ppermute | solution.py:80
  244.8 44.9 %collective-permute-start.13 = (bf16[2,1152,256]{2,1,0:T(8,128)(2,1)}, bf16[2,1152,256]{2,1,0:T(8,128)(2,1)}, u32[]{:S(2)}, u32[]{:S(2)}) collective-permute-start(bf16[2,1152,256]{2,1,0:T(8,128)(2,1)} %get-tuple-element.82), channel_id=1, source_target_pairs={{0,8},{1,9},{2,10},{3,11},{4,12},{5,13},{6,14},{7,15},{8,0},{9,1},... | collective-permute-start | bytes 3538952 | tf_op jit(solution)/shard_map/ppermute | solution.py:80
  246.4 44.9 %collective-permute-start.14 = (bf16[2,1152,256]{2,1,0:T(8,128)(2,1)}, bf16[2,1152,256]{2,1,0:T(8,128)(2,1)}, u32[]{:S(2)}, u32[]{:S(2)}) collective-permute-start(bf16[2,1152,256]{2,1,0:T(8,128)(2,1)} %get-tuple-element.83), channel_id=1, source_target_pairs={{0,16},{1,17},{2,18},{3,19},{4,20},{5,21},{6,22},{7,23},{8,24},{9,... | collective-permute-start | bytes 3538952 | tf_op jit(solution)/shard_map/ppermute | solution.py:80
  289.1 54.6 %collective-permute-start.56 = (bf16[2,1152,256]{2,1,0:T(8,128)(2,1)}, bf16[2,1152,256]{2,1,0:T(8,128)(2,1)}, u32[]{:S(2)}, u32[]{:S(2)}) collective-permute-start(bf16[2,1152,256]{2,1,0:T(8,128)(2,1)} %get-tuple-element.121), channel_id=1, source_target_pairs={{0,8},{1,9},{2,10},{3,11},{4,12},{5,13},{6,14},{7,15},{8,0},{9,1},... | collective-permute-start | bytes 3538952 | tf_op jit(solution)/shard_map/ppermute | solution.py:80
  289.7 55.5 %collective-permute-start.57 = (bf16[2,1152,256]{2,1,0:T(8,128)(2,1)}, bf16[2,1152,256]{2,1,0:T(8,128)(2,1)}, u32[]{:S(2)}, u32[]{:S(2)}) collective-permute-start(bf16[2,1152,256]{2,1,0:T(8,128)(2,1)} %get-tuple-element.122), channel_id=1, source_target_pairs={{0,16},{1,17},{2,18},{3,19},{4,20},{5,21},{6,22},{7,23},{8,24},{9,... | collective-permute-start | bytes 3538952 | tf_op jit(solution)/shard_map/ppermute | solution.py:80
  293.5 56.4 %collective-permute-start.50 = (bf16[1,1152,256]{2,1,0:T(8,128)(2,1)}, bf16[1,1152,256]{2,1,0:T(8,128)(2,1)}, u32[]{:S(2)}, u32[]{:S(2)}) collective-permute-start(bf16[1,1152,256]{2,1,0:T(8,128)(2,1)} %add_convert_fusion.25), channel_id=1, source_target_pairs={{0,16},{1,17},{2,18},{3,19},{4,20},{5,21},{6,22},{7,23},{8,24},{9,... | collective-permute-start | bytes 1769480 | tf_op jit(solution)/shard_map/ppermute | solution.py:80
  338.4 51.0 %collective-permute-start.22 = (bf16[1024,1024]{1,0:T(8,128)(2,1)S(1)}, bf16[1024,1024]{1,0:T(8,128)(2,1)S(1)}, u32[]{:S(2)}, u32[]{:S(2)}) collective-permute-start(bf16[1024,1024]{1,0:T(8,128)(2,1)S(1)} %slice.1518), channel_id=1, source_target_pairs={{0,1},{1,0},{2,3},{3,2},{4,5},{5,4},{6,7},{7,6},{8,9},{9,8},{10,11... | collective-permute-start | bytes 6291464 | tf_op jit(solution)/shard_map/ppermute | solution.py:80
  341.2 51.6 %collective-permute-start.21 = (bf16[1024,1024]{1,0:T(8,128)(2,1)S(1)}, bf16[1024,1024]{1,0:T(8,128)(2,1)S(1)}, u32[]{:S(2)}, u32[]{:S(2)}) collective-permute-start(bf16[1024,1024]{1,0:T(8,128)(2,1)S(1)} %slice.1519), channel_id=1, source_target_pairs={{0,1},{1,0},{2,3},{3,2},{4,5},{5,4},{6,7},{7,6},{8,9},{9,8},{10,11... | collective-permute-start | bytes 6291464 | tf_op jit(solution)/shard_map/ppermute | solution.py:80
  343.7 64.7 %collective-permute-start.23 = (bf16[2,1152,256]{2,1,0:T(8,128)(2,1)}, bf16[2,1152,256]{2,1,0:T(8,128)(2,1)S(1)}, u32[]{:S(2)}, u32[]{:S(2)}) collective-permute-start(bf16[2,1152,256]{2,1,0:T(8,128)(2,1)} %get-tuple-element.96), channel_id=1, source_target_pairs={{0,8},{1,9},{2,10},{3,11},{4,12},{5,13},{6,14},{7,15},{8,0},{9,1},... | collective-permute-start | bytes 3538952 | tf_op jit(solution)/shard_map/ppermute | solution.py:80
  345.2 39.3 %collective-permute-start.51 = (bf16[1,1152,256]{2,1,0:T(8,128)(2,1)S(1)}, bf16[1,1152,256]{2,1,0:T(8,128)(2,1)S(1)}, u32[]{:S(2)}, u32[]{:S(2)}) collective-permute-start(bf16[1,1152,256]{2,1,0:T(8,128)(2,1)S(1)} %add_convert_fusion.22), channel_id=1, source_target_pairs={{0,8},{1,9},{2,10},{3,11},{4,12},{5,13},{6,14},{7,15},{8,0},{9,1},... | collective-permute-start | bytes 1769480 | tf_op jit(solution)/shard_map/ppermute | solution.py:80
  349.9 58.5 %collective-permute-start.24 = (bf16[2,1152,256]{2,1,0:T(8,128)(2,1)}, bf16[2,1152,256]{2,1,0:T(8,128)(2,1)S(1)}, u32[]{:S(2)}, u32[]{:S(2)}) collective-permute-start(bf16[2,1152,256]{2,1,0:T(8,128)(2,1)} %get-tuple-element.97), channel_id=1, source_target_pairs={{0,16},{1,17},{2,18},{3,19},{4,20},{5,21},{6,22},{7,23},{8,24},{9,... | collective-permute-start | bytes 3538952 | tf_op jit(solution)/shard_map/ppermute | solution.py:80
  384.5 39.4 %collective-permute-start.58 = (bf16[1,1152,256]{2,1,0:T(8,128)(2,1)}, bf16[1,1152,256]{2,1,0:T(8,128)(2,1)}, u32[]{:S(2)}, u32[]{:S(2)}) collective-permute-start(bf16[1,1152,256]{2,1,0:T(8,128)(2,1)} %add_convert_fusion.17), channel_id=1, source_target_pairs={{0,16},{1,17},{2,18},{3,19},{4,20},{5,21},{6,22},{7,23},{8,24},{9,... | collective-permute-start | bytes 1769480 | tf_op jit(solution)/shard_map/ppermute | solution.py:80
  389.4 34.5 %collective-permute-start.59 = (bf16[1,1152,256]{2,1,0:T(8,128)(2,1)}, bf16[1,1152,256]{2,1,0:T(8,128)(2,1)}, u32[]{:S(2)}, u32[]{:S(2)}) collective-permute-start(bf16[1,1152,256]{2,1,0:T(8,128)(2,1)} %add_convert_fusion.16), channel_id=1, source_target_pairs={{0,8},{1,9},{2,10},{3,11},{4,12},{5,13},{6,14},{7,15},{8,0},{9,1},... | collective-permute-start | bytes 1769480 | tf_op jit(solution)/shard_map/ppermute | solution.py:80
  392.8 26.5 %collective-permute-start.52 = (bf16[2304,256]{1,0:T(8,128)(2,1)}, bf16[2304,256]{1,0:T(8,128)(2,1)}, u32[]{:S(2)}, u32[]{:S(2)}) collective-permute-start(bf16[2304,256]{1,0:T(8,128)(2,1)} %pad_maximum_fusion.5), channel_id=1, source_target_pairs={{0,2},{1,3},{6,4},{7,5},{8,10},{9,11},{14,12},{15,13},{16,18},{17,... | collective-permute-start | bytes 3538952 | tf_op jit(solution)/shard_map/ppermute | solution.py:192
  409.6 62.1 %collective-permute-start.64 = (bf16[1,1152,256]{2,1,0:T(8,128)(2,1)}, bf16[1,1152,256]{2,1,0:T(8,128)(2,1)}, u32[]{:S(2)}, u32[]{:S(2)}) collective-permute-start(bf16[1,1152,256]{2,1,0:T(8,128)(2,1)} %add_convert_fusion.24), channel_id=1, source_target_pairs={{0,16},{1,17},{2,18},{3,19},{4,20},{5,21},{6,22},{7,23},{8,24},{9,... | collective-permute-start | bytes 1769480 | tf_op jit(solution)/shard_map/ppermute | solution.py:80
  415.0 21.5 %collective-permute-start.25 = (bf16[4,128,1024]{2,1,0:T(8,128)(2,1)}, bf16[4,128,1024]{2,1,0:T(8,128)(2,1)}, u32[]{:S(2)}, u32[]{:S(2)}) collective-permute-start(bf16[4,128,1024]{2,1,0:T(8,128)(2,1)} %dynamic-slice_bitcast_fusion.1), channel_id=1, source_target_pairs={{0,1},{1,0},{2,3},{3,2},{4,5},{5,4},{6,7},{7,6},{8,9},{9,8},{10,11... | collective-permute-start | bytes 3145736 | tf_op jit(solution)/shard_map/ppermute | solution.py:80
  422.2 55.6 %collective-permute-start.53 = (bf16[2304,256]{1,0:T(8,128)(2,1)}, bf16[2304,256]{1,0:T(8,128)(2,1)}, u32[]{:S(2)}, u32[]{:S(2)}) collective-permute-start(bf16[2304,256]{1,0:T(8,128)(2,1)} %add_convert_fusion.6), channel_id=1, source_target_pairs={{2,4},{3,5},{4,2},{5,3},{10,12},{11,13},{12,10},{13,11},{18,20},{1... | collective-permute-start | bytes 3538952 | tf_op jit(solution)/shard_map/ppermute | solution.py:192
  427.3 53.9 %collective-permute-start.60 = (bf16[2304,256]{1,0:T(8,128)(2,1)}, bf16[2304,256]{1,0:T(8,128)(2,1)}, u32[]{:S(2)}, u32[]{:S(2)}) collective-permute-start(bf16[2304,256]{1,0:T(8,128)(2,1)} %pad_maximum_fusion.6), channel_id=1, source_target_pairs={{0,2},{1,3},{6,4},{7,5},{8,10},{9,11},{14,12},{15,13},{16,18},{17,... | collective-permute-start | bytes 3538952 | tf_op jit(solution)/shard_map/ppermute | solution.py:192
  436.0 36.3 %collective-permute-start.65 = (bf16[1,1152,256]{2,1,0:T(8,128)(2,1)S(1)}, bf16[1,1152,256]{2,1,0:T(8,128)(2,1)S(1)}, u32[]{:S(2)}, u32[]{:S(2)}) collective-permute-start(bf16[1,1152,256]{2,1,0:T(8,128)(2,1)S(1)} %add_convert_fusion.11), channel_id=1, source_target_pairs={{0,8},{1,9},{2,10},{3,11},{4,12},{5,13},{6,14},{7,15},{8,0},{9,1},... | collective-permute-start | bytes 1769480 | tf_op jit(solution)/shard_map/ppermute | solution.py:80
  439.3 43.5 %collective-permute-start.26 = (bf16[2,128,512]{2,1,0:T(8,128)(2,1)}, bf16[2,128,512]{2,1,0:T(8,128)(2,1)}, u32[]{:S(2)}, u32[]{:S(2)}) collective-permute-start(bf16[2,128,512]{2,1,0:T(8,128)(2,1)} %pad_maximum_fusion.18), channel_id=1, source_target_pairs={{0,8},{1,9},{2,10},{3,11},{4,12},{5,13},{6,14},{7,15},{8,0},{9,1},... | collective-permute-start | bytes 786440 | tf_op jit(solution)/shard_map/ppermute | solution.py:80
  475.2 98.4 %collective-permute-start.66 = (bf16[2304,256]{1,0:T(8,128)(2,1)}, bf16[2304,256]{1,0:T(8,128)(2,1)}, u32[]{:S(2)}, u32[]{:S(2)}) collective-permute-start(bf16[2304,256]{1,0:T(8,128)(2,1)} %pad_maximum_fusion.7), channel_id=1, source_target_pairs={{0,2},{1,3},{6,4},{7,5},{8,10},{9,11},{14,12},{15,13},{16,18},{17,... | collective-permute-start | bytes 3538952 | tf_op jit(solution)/shard_map/ppermute | solution.py:192
  479.8 96.2 %collective-permute-start.54 = (bf16[2304,256]{1,0:T(8,128)(2,1)S(1)}, bf16[2304,256]{1,0:T(8,128)(2,1)}, u32[]{:S(2)}, u32[]{:S(2)}) collective-permute-start(bf16[2304,256]{1,0:T(8,128)(2,1)S(1)} %add_convert_fusion.5), channel_id=1, source_target_pairs={{2,0},{3,1},{4,6},{5,7},{10,8},{11,9},{12,14},{13,15},{18,16},{19,... | collective-permute-start | bytes 3538952 | tf_op jit(solution)/shard_map/ppermute | solution.py:192
  503.4 18.8 %collective-permute-start.41 = (bf16[1,128,512]{2,1,0:T(8,128)(2,1)}, bf16[1,128,512]{2,1,0:T(8,128)(2,1)}, u32[]{:S(2)}, u32[]{:S(2)}) collective-permute-start(bf16[1,128,512]{2,1,0:T(8,128)(2,1)} %add_convert_fusion.39), channel_id=1, source_target_pairs={{0,16},{1,17},{2,18},{3,19},{4,20},{5,21},{6,22},{7,23},{8,24},{9,... | collective-permute-start | bytes 393224 | tf_op jit(solution)/shard_map/ppermute | solution.py:80
  529.7 47.9 %collective-permute-start.61 = (bf16[2304,256]{1,0:T(8,128)(2,1)S(1)}, bf16[2304,256]{1,0:T(8,128)(2,1)S(1)}, u32[]{:S(2)}, u32[]{:S(2)}) collective-permute-start(bf16[2304,256]{1,0:T(8,128)(2,1)S(1)} %add_convert_fusion.4), channel_id=1, source_target_pairs={{2,4},{3,5},{4,2},{5,3},{10,12},{11,13},{12,10},{13,11},{18,20},{1... | collective-permute-start | bytes 3538952 | tf_op jit(solution)/shard_map/ppermute | solution.py:192
  533.7 34.3 %collective-permute-start.29 = (bf16[4,544]{1,0:T(4,128)(2,1)S(1)}, bf16[4,544]{1,0:T(4,128)(2,1)S(1)}, u32[]{:S(2)}, u32[]{:S(2)}) collective-permute-start(bf16[4,544]{1,0:T(4,128)(2,1)S(1)} %pad_maximum_fusion.62), channel_id=1, source_target_pairs={{0,1},{1,0},{2,3},{3,2},{4,5},{5,4},{6,7},{7,6},{8,9},{9,8},{10,11... | collective-permute-start | bytes 13064 | tf_op jit(solution)/shard_map/ppermute | solution.py:80
  538.4 23.5 %collective-permute-start.47 = (bf16[32,1024]{1,0:T(8,128)(2,1)S(1)}, bf16[32,1024]{1,0:T(8,128)(2,1)S(1)}, u32[]{:S(2)}, u32[]{:S(2)}) collective-permute-start(bf16[32,1024]{1,0:T(8,128)(2,1)S(1)} %get-tuple-element.140), channel_id=1, source_target_pairs={{0,4},{1,5},{2,6},{3,7},{4,0},{5,1},{6,2},{7,3},{8,12},{9,13},{10,... | collective-permute-start | bytes 196616 | tf_op jit(solution)/shard_map/ppermute | solution.py:80
  577.4 33.1 %collective-permute-start.55 = (bf16[2304,256]{1,0:T(8,128)(2,1)S(1)}, bf16[2304,256]{1,0:T(8,128)(2,1)S(1)}, u32[]{:S(2)}, u32[]{:S(2)}) collective-permute-start(bf16[2304,256]{1,0:T(8,128)(2,1)S(1)} %broadcast_select_fusion.2), channel_id=1, source_target_pairs={{0,1},{1,0},{2,3},{3,2},{4,5},{5,4},{6,7},{7,6},{8,9},{9,8},{10,11... | collective-permute-start | bytes 3538952 | tf_op jit(solution)/shard_map/ppermute | solution.py:80
  577.9 30.7 %collective-permute-start.62 = (bf16[2304,256]{1,0:T(8,128)(2,1)S(1)}, bf16[2304,256]{1,0:T(8,128)(2,1)S(1)}, u32[]{:S(2)}, u32[]{:S(2)}) collective-permute-start(bf16[2304,256]{1,0:T(8,128)(2,1)S(1)} %add_convert_fusion.3), channel_id=1, source_target_pairs={{2,0},{3,1},{4,6},{5,7},{10,8},{11,9},{12,14},{13,15},{18,16},{19,... | collective-permute-start | bytes 3538952 | tf_op jit(solution)/shard_map/ppermute | solution.py:192
  579.9 71.8 %collective-permute-start.68 = (bf16[2304,256]{1,0:T(8,128)(2,1)S(1)}, bf16[2304,256]{1,0:T(8,128)(2,1)}, u32[]{:S(2)}, u32[]{:S(2)}) collective-permute-start(bf16[2304,256]{1,0:T(8,128)(2,1)S(1)} %add_convert_fusion.1), channel_id=1, source_target_pairs={{2,0},{3,1},{4,6},{5,7},{10,8},{11,9},{12,14},{13,15},{18,16},{19,... | collective-permute-start | bytes 3538952 | tf_op jit(solution)/shard_map/ppermute | solution.py:192
  583.3 28.4 %collective-permute-start.30 = (bf16[2,144,1024]{2,1,0:T(8,128)(2,1)S(1)}, bf16[2,144,1024]{2,1,0:T(8,128)(2,1)S(1)}, u32[]{:S(2)}, u32[]{:S(2)}) collective-permute-start(bf16[2,144,1024]{2,1,0:T(8,128)(2,1)S(1)} %pad_maximum_fusion.10), channel_id=1, source_target_pairs={{0,8},{1,9},{2,10},{3,11},{4,12},{5,13},{6,14},{7,15},{8,0},{9,1},... | collective-permute-start | bytes 1769480 | tf_op jit(solution)/shard_map/ppermute | solution.py:80
  584.2 27.6 %collective-permute-start.31 = (bf16[2,144,1024]{2,1,0:T(8,128)(2,1)S(1)}, bf16[2,144,1024]{2,1,0:T(8,128)(2,1)S(1)}, u32[]{:S(2)}, u32[]{:S(2)}) collective-permute-start(bf16[2,144,1024]{2,1,0:T(8,128)(2,1)S(1)} %pad_maximum_fusion.11), channel_id=1, source_target_pairs={{0,16},{1,17},{2,18},{3,19},{4,20},{5,21},{6,22},{7,23},{8,24},{9,... | collective-permute-start | bytes 1769480 | tf_op jit(solution)/shard_map/ppermute | solution.py:80
  608.7 55.9 %collective-permute-start.63 = (bf16[2304,256]{1,0:T(8,128)(2,1)S(1)}, bf16[2304,256]{1,0:T(8,128)(2,1)}, u32[]{:S(2)}, u32[]{:S(2)}) collective-permute-start(bf16[2304,256]{1,0:T(8,128)(2,1)S(1)} %broadcast_select_fusion.1), channel_id=1, source_target_pairs={{0,1},{1,0},{2,3},{3,2},{4,5},{5,4},{6,7},{7,6},{8,9},{9,8},{10,11... | collective-permute-start | bytes 3538952 | tf_op jit(solution)/shard_map/ppermute | solution.py:80
  623.0 17.3 %collective-permute-start.35 = (bf16[36,2048]{1,0:T(8,128)(2,1)S(1)}, bf16[36,2048]{1,0:T(8,128)(2,1)S(1)}, u32[]{:S(2)}, u32[]{:S(2)}) collective-permute-start(bf16[36,2048]{1,0:T(8,128)(2,1)S(1)} %get-tuple-element.293), channel_id=1, source_target_pairs={{0,4},{1,5},{2,6},{3,7},{4,0},{5,1},{6,2},{7,3},{8,12},{9,13},{10,... | collective-permute-start | bytes 442376 | tf_op jit(solution)/shard_map/ppermute | solution.py:80
  653.1 22.7 %collective-permute-start.69 = (bf16[2304,256]{1,0:T(8,128)(2,1)S(1)}, bf16[2304,256]{1,0:T(8,128)(2,1)}, u32[]{:S(2)}, u32[]{:S(2)}) collective-permute-start(bf16[2304,256]{1,0:T(8,128)(2,1)S(1)} %broadcast_select_fusion), channel_id=1, source_target_pairs={{0,1},{1,0},{2,3},{3,2},{4,5},{5,4},{6,7},{7,6},{8,9},{9,8},{10,11... | collective-permute-start | bytes 3538952 | tf_op jit(solution)/shard_map/ppermute | solution.py:80
  (142 other events, 1613.6 us)

commit v2 on v1

--- a/solution.py
+++ b/solution.py
@@ -52,14 +52,6 @@
     )
 
 
-def unrotate(values, cosine, sine):
-    half = DH // 2
-    first, second = values[:, :half], values[:, half:]
-    return jnp.concatenate(
-        [first * cosine + second * sine, second * cosine - first * sine], axis=1
-    )
-
-
 class Links:
     def __init__(self, mesh):
         self.shards = mesh.shape["shard"]
@@ -88,15 +80,18 @@
     def core_swap(self, value):
         return self.rep_swap(value, 0)
 
-    def gather(self, value):
-        shard, rep = self.here()
+    def near(self, value):
         if self.paired:
-            first = self.move(value, lambda s, r: (s ^ (2 if r & 2 else 1), r))
+            return self.move(value, lambda s, r: (s ^ (2 if r & 2 else 1), r))
+        return value
+
+    def gather(self, value, first, *tokens):
+        shard, _ = self.here()
+        if self.paired:
+            (first,) = hold([first], *tokens)
             other = self.rep_swap(first, 1)
             last = self.move(first, lambda s, r: (s ^ (1 if r & 2 else 2), r))
-            near = jnp.where((rep & 2) == 0, 1, 2)
-            ids = jnp.stack([shard, shard ^ near, shard ^ (3 - near), shard ^ 3, shard])
-            return [value, first, other, last], ids.astype(jnp.int32)
+            return [value, first, other, last]
         whole = value[None]
         for bit in range(self.shard_bits):
             came = self.shard_swap(whole, bit)
@@ -106,27 +101,27 @@
                 jnp.concatenate([whole, came], axis=0),
                 jnp.concatenate([came, whole], axis=0),
             )
-        ids = jnp.concatenate([jnp.arange(self.shards), shard[None]])
-        return [whole[block] for block in range(self.shards)], ids.astype(jnp.int32)
+        return [whole[block] for block in range(self.shards)]
+
+    def ids(self):
+        shard, rep = self.here()
+        if self.paired:
+            near = jnp.where((rep & 2) == 0, 1, 2)
+            ids = jnp.stack([shard, shard ^ near, shard ^ (3 - near), shard ^ 3, shard])
+        else:
+            ids = jnp.concatenate([jnp.arange(self.shards), shard[None]])
+        return ids.astype(jnp.int32)
 
     def by_mark(self, blocks):
-        shard, _ = self.here()
         wide = blocks.shape[2] // 2
         sides = []
         for stream, (_, leave, stay) in enumerate(block_orders(self.shard_bits)):
             part = blocks[:, :, stream * wide : (stream + 1) * wide]
             for marks in (leave, stay):
-                sides.append(
-                    jnp.stack(
-                        [
-                            lax.dynamic_index_in_dim(part, shard ^ mark, 0, keepdims=False)
-                            for mark in marks
-                        ]
-                    )
-                )
+                sides.append(jnp.stack([part[mark] for mark in marks]))
         return sides
 
-    def total(self, sides, axis, tail):
+    def total(self, sides, axis):
         _, rep = self.here()
         streams = []
         for stream, (order, _, _) in enumerate(block_orders(self.shard_bits)):
@@ -147,25 +142,6 @@
         if self.rep_bits != 3:
             for bit in range(1, self.rep_bits):
                 value = add_low(value, self.rep_swap(value, bit))
-        elif tail:
-            quarter = value.shape[0] // 4
-            place = rep >> 1
-            pick = lambda at: lax.dynamic_slice_in_dim(value, at * quarter, quarter, 0)
-            sends = [pick(place ^ mark) for mark in (1, 2, 3)]
-            came = [self.rep_move(send, mark) for send, mark in zip(sends, (1, 2, 3), strict=True)]
-            token = yield sends
-            came = hold(came, token)
-            mine = pick(place).astype(FULL)
-            for arrived in came:
-                mine = mine + arrived.astype(FULL)
-            mine = mine.astype(LOW)
-            came = [self.rep_move(mine, mark) for mark in (1, 2, 3)]
-            token = yield [mine]
-            value = jnp.zeros_like(value)
-            for mark, part in enumerate([mine] + hold(came, token)):
-                value = lax.dynamic_update_slice_in_dim(
-                    value, part, (place ^ mark) * quarter, 0
-                )
         else:
             came = self.rep_line(value, {0: 1, 3: 2})
             token = yield [value]
@@ -179,9 +155,6 @@
             value = jnp.where(middle, value, hold([came], token)[0])
         yield value
 
-    def rep_move(self, value, mark):
-        return self.move(value, lambda s, r: (s, r ^ (mark << 1)))
-
     def rep_line(self, value, targets):
         pairs = []
         for shard in range(self.shards):
@@ -196,10 +169,9 @@
     return (first.astype(FULL) + second.astype(FULL)).astype(LOW)
 
 
-def hold(values, token):
-    if token is None:
-        return list(values)
-    return list(lax.optimization_barrier(tuple(values) + (token,))[:-1])
+def hold(values, *tokens):
+    tokens = tuple(token for token in tokens if token is not None)
+    return list(lax.optimization_barrier(tuple(values) + tokens)[: len(values)])
 
 
 def block_orders(bits):
@@ -210,7 +182,405 @@
         yield order, [m | (1 << order[0]) for m in stay], stay
 
 
-def ffn_kernel(ids_ref, ffn_ref, cot_ref, *refs, shards, fresh):
+def split_step(step):
+    return step * 2 // 3, step // 3
+
+
+def runs(step, shards, side, piece):
+    big, small = split_step(step)
+    number = side * PIECES + piece
+    for shard in range(shards):
+        yield shard, number * big, big, shard * big
+    for shard in range(shards):
+        yield shard, 2 * PIECES * big + number * small, small, shards * big + shard * small
+
+
+def pack_kernel(core_ref, gate_ref, up_ref, down_ref, *outs, shards):
+    own = gate_ref.shape[0]
+    hidden = gate_ref.shape[1] // shards
+    step = hidden // (2 * PIECES)
+    tall = shards * step // 256 * own
+    big, small = split_step(step)
+    for side in range(2):
+
+        @pl.when(core_ref[0] == side)
+        def _():
+            for piece, out in enumerate(outs):
+                for number, weight in enumerate((gate_ref, up_ref)):
+                    for shard, start, count, place in runs(step, shards, side, piece):
+                        row = number * tall + place // 256 * own
+                        column = place % 256
+                        at = shard * hidden + start
+                        out[row : row + own, column : column + count] = weight[:, at : at + count]
+                for part in range(down_ref.shape[1] // 256):
+                    row = 2 * tall + part * step
+                    columns = slice(part * 256, part * 256 + 256)
+                    at = (side * PIECES + piece) * big
+                    out[row : row + big] = down_ref[at : at + big, columns]
+                    at = 2 * PIECES * big + (side * PIECES + piece) * small
+                    out[row + big : row + step] = down_ref[at : at + small, columns]
+
+
+def pack(core, w_gate, w_up, w_down, shards):
+    own, hidden_all = w_gate.shape
+    rows = 3 * hidden_all // (2 * PIECES) * own // 256
+    return pl.pallas_call(
+        functools.partial(pack_kernel, shards=shards),
+        grid_spec=pltpu.PrefetchScalarGridSpec(
+            num_scalar_prefetch=1,
+            grid=(1,),
+            in_specs=[pl.BlockSpec(w.shape, lambda i, core: (0, 0)) for w in (w_gate, w_up, w_down)],
+            out_specs=[pl.BlockSpec((rows, 256), lambda i, core: (0, 0))] * PIECES,
+        ),
+        out_shape=[jax.ShapeDtypeStruct((rows, 256), LOW)] * PIECES,
+        compiler_params=pltpu.CompilerParams(vmem_limit_bytes=48 * 1024 * 1024),
+        cost_estimate=pl.CostEstimate(flops=0, bytes_accessed=11_000_000, transcendentals=0),
+        name="pack",
+    )(core, w_gate, w_up, w_down)
+
+
+def unpack_kernel(core_ref, *refs, shards):
+    mine, theirs = refs[:PIECES], refs[PIECES : 2 * PIECES]
+    gate_ref, up_ref, down_ref = refs[2 * PIECES :]
+    own = gate_ref.shape[0]
+    hidden = gate_ref.shape[1] // shards
+    step = hidden // (2 * PIECES)
+    tall = shards * step // 256 * own
+    big, small = split_step(step)
+    for core in range(2):
+
+        @pl.when(core_ref[0] == core)
+        def _():
+            for side in range(2):
+                for piece in range(PIECES):
+                    part = (mine if side == core else theirs)[piece]
+                    for number, grad in enumerate((gate_ref, up_ref)):
+                        for shard, start, count, place in runs(step, shards, side, piece):
+                            row = number * tall + place // 256 * own
+                            column = place % 256
+                            at = shard * hidden + start
+                            grad[:, at : at + count] = part[
+                                row : row + own, column : column + count
+                            ].astype(FULL)
+                    for block in range(down_ref.shape[1] // 256):
+                        row = 2 * tall + block * step
+                        columns = slice(block * 256, block * 256 + 256)
+                        at = (side * PIECES + piece) * big
+                        down_ref[at : at + big, columns] = part[row : row + big].astype(FULL)
+                        at = 2 * PIECES * big + (side * PIECES + piece) * small
+                        down_ref[at : at + small, columns] = part[row + big : row + step].astype(
+                            FULL
+                        )
+
+
+def unpack(core, mine, theirs, shapes, shards):
+    rows = mine[0].shape[0]
+    return pl.pallas_call(
+        functools.partial(unpack_kernel, shards=shards),
+        grid_spec=pltpu.PrefetchScalarGridSpec(
+            num_scalar_prefetch=1,
+            grid=(1,),
+            in_specs=[pl.BlockSpec((rows, 256), lambda i, core: (0, 0))] * (2 * PIECES),
+            out_specs=[pl.BlockSpec(shape, lambda i, core: (0, 0)) for shape in shapes],
+        ),
+        out_shape=[jax.ShapeDtypeStruct(shape, FULL) for shape in shapes],
+        compiler_params=pltpu.CompilerParams(vmem_limit_bytes=56 * 1024 * 1024),
+        cost_estimate=pl.CostEstimate(flops=0, bytes_accessed=21_000_000, transcendentals=0),
+        name="unpack",
+    )(core, *mine, *theirs)
+
+
+def run_copies(copies):
+    for copy in copies:
+        copy.start()
+    for copy in copies:
+        copy.wait()
+
+
+def line_up_kernel(ids_ref, *refs, half):
+    *blocks, out, sem = refs
+    run_copies(
+        [
+            pltpu.make_async_copy(block.at[pl.ds(0, half)], out.at[ids_ref[place]], sem)
+            for place, block in enumerate(blocks)
+        ]
+    )
+
+
+def line_up(ids, blocks, half):
+    wide = blocks[0].shape[1]
+    where = pl.BlockSpec(memory_space=pl.ANY)
+    return pl.pallas_call(
+        functools.partial(line_up_kernel, half=half),
+        grid_spec=pltpu.PrefetchScalarGridSpec(
+            num_scalar_prefetch=1,
+            grid=(1,),
+            in_specs=[where] * len(blocks),
+            out_specs=pl.BlockSpec((len(blocks), half, wide), lambda i, ids: (0, 0, 0)),
+            scratch_shapes=[pltpu.SemaphoreType.DMA],
+        ),
+        out_shape=jax.ShapeDtypeStruct((len(blocks), half, wide), LOW),
+        cost_estimate=pl.CostEstimate(flops=0, bytes_accessed=8_000_000, transcendentals=0),
+        compiler_params=pltpu.CompilerParams(vmem_limit_bytes=32 * 1024 * 1024),
+        name="line_up",
+    )(ids, *blocks)
+
+
+def both_cores_kernel(core_ref, mine, theirs, out, sem):
+    core = core_ref[0]
+    run_copies(
+        [
+            pltpu.make_async_copy(mine.at[shard], out.at[shard, core], sem)
+            for shard in range(mine.shape[0])
+        ]
+        + [
+            pltpu.make_async_copy(theirs.at[shard], out.at[shard, 1 - core], sem)
+            for shard in range(mine.shape[0])
+        ]
+    )
+
+
+def both_cores(core, mine, theirs):
+    shards, half, wide = mine.shape
+    where = pl.BlockSpec(memory_space=pl.ANY)
+    out = pl.pallas_call(
+        both_cores_kernel,
+        grid_spec=pltpu.PrefetchScalarGridSpec(
+            num_scalar_prefetch=1,
+            grid=(1,),
+            in_specs=[where] * 2,
+            out_specs=pl.BlockSpec((shards, 2, half, wide), lambda i, core: (0, 0, 0, 0)),
+            scratch_shapes=[pltpu.SemaphoreType.DMA],
+        ),
+        out_shape=jax.ShapeDtypeStruct((shards, 2, half, wide), LOW),
+        cost_estimate=pl.CostEstimate(flops=0, bytes_accessed=16_000_000, transcendentals=0),
+        compiler_params=pltpu.CompilerParams(vmem_limit_bytes=32 * 1024 * 1024),
+        name="both_cores",
+    )(core, mine, theirs)
+    return out.reshape(shards * 2 * half, wide)
+
+
+def sort_out_kernel(place_ref, *refs, half):
+    *grads, gains, keep, give, sem = refs
+    shard, core = place_ref[0], place_ref[1]
+    copies = []
+    for mark in range(keep.shape[0]):
+        block = lax.bitwise_xor(shard, jnp.int32(mark))
+        column = 0
+        for grad in grads:
+            wide = grad.shape[1]
+            for side, target in ((core, keep), (1 - core, give)):
+                row = pl.multiple_of((2 * block + side) * half, half)
+                copies.append(
+                    pltpu.make_async_copy(
+                        grad.at[pl.ds(row, half)], target.at[mark, pl.ds(0, half), pl.ds(column, wide)], sem
+                    )
+                )
+            column += wide
+        for target in (keep, give):
+            copies.append(
+                pltpu.make_async_copy(
+                    gains.at[block], target.at[mark, pl.ds(half, gains.shape[1])], sem
+                )
+            )
+    run_copies(copies)
+
+
+def sort_out(place, grads, gains):
+    shards, extra, wide = gains.shape
+    half = grads[0].shape[0] // (2 * shards)
+    where = pl.BlockSpec(memory_space=pl.ANY)
+    return pl.pallas_call(
+        functools.partial(sort_out_kernel, half=half),
+        grid_spec=pltpu.PrefetchScalarGridSpec(
+            num_scalar_prefetch=1,
+            grid=(1,),
+            in_specs=[where] * (len(grads) + 1),
+            out_specs=[pl.BlockSpec((shards, half + extra, wide), lambda i, place: (0, 0, 0))] * 2,
+            scratch_shapes=[pltpu.SemaphoreType.DMA],
+        ),
+        out_shape=[jax.ShapeDtypeStruct((shards, half + extra, wide), LOW)] * 2,
+        cost_estimate=pl.CostEstimate(flops=0, bytes_accessed=12_000_000, transcendentals=0),
+        compiler_params=pltpu.CompilerParams(vmem_limit_bytes=32 * 1024 * 1024),
+        name="sort_out",
+    )(place, *grads, gains)
+
+
+def head_back(grad, pre, gain, cosine, sine):
+    half = DH // 2
+    inverse = inverse_rms(pre, 0)
+    hat = pre * inverse
+    first, second = grad[:half], grad[half:]
+    grad = jnp.concatenate(
+        [first * cosine + second * sine, second * cosine - first * sine], axis=0
+    )
+    own = jnp.sum(grad * hat, axis=1, keepdims=True)
+    return norm_back(grad * gain, hat, inverse, 0).astype(LOW), own
+
+
+def attend_grads_kernel(
+    dq_ref,
+    dk_ref,
+    dv_ref,
+    q_ref,
+    k_ref,
+    cos_ref,
+    sin_ref,
+    gain_q_ref,
+    gain_k_ref,
+    in_ref,
+    wq_ref,
+    wk_ref,
+    wv_ref,
+    mix_ref,
+    resid_ref,
+    tokens_ref,
+    inv_ref,
+    gain_in_ref,
+    above_ref,
+    gq_ref,
+    gk_ref,
+    gv_ref,
+    go_ref,
+    back_ref,
+    own_q_ref,
+    own_k_ref,
+    own_in_ref,
+):
+    @pl.when(pl.program_id(0) == 0)
+    def _():
+        own_q_ref[...] = jnp.zeros_like(own_q_ref)
+        own_k_ref[...] = jnp.zeros_like(own_k_ref)
+
+    cosine, sine = cos_ref[...], sin_ref[...]
+    sides = []
+    for grad_ref, pre_ref, gain_ref, own_ref in (
+        (dq_ref, q_ref, gain_q_ref, own_q_ref),
+        (dk_ref, k_ref, gain_k_ref, own_k_ref),
+    ):
+        parts = []
+        for at in range(0, grad_ref.shape[0], DH):
+            rows = slice(at, at + DH)
+            part, own = head_back(grad_ref[rows], pre_ref[rows], gain_ref[...], cosine, sine)
+            own_ref[...] += own
+            parts.append(part)
+        sides.append(jnp.concatenate(parts, axis=0))
+    wide = dq_ref.shape[0]
+    narrow = dk_ref.shape[0]
+    grads = jnp.concatenate(sides + [dv_ref[...]], axis=0)
+    weights = jnp.concatenate([wq_ref[...], wk_ref[...], wv_ref[...]], axis=1)
+    weight_grad = dot(in_ref[...], grads, 0, 1).astype(LOW)
+    gq_ref[...] = weight_grad[:, :wide]
+    gk_ref[...] = weight_grad[:, wide : wide + narrow]
+    gv_ref[...] = weight_grad[:, wide + narrow :]
+    go_ref[...] = dot(mix_ref[...], resid_ref[...], 1, 0).astype(LOW)
+    back = dot(grads, weights, 0, 1)
+
+    @pl.when(pl.program_id(0) == 0)
+    def _():
+        back_ref[...] = back
+
+    @pl.when(pl.program_id(0) != 0)
+    def _():
+        back_ref[...] += back
+
+    @pl.when(pl.program_id(0) == pl.num_programs(0) - 1)
+    def _():
+        own_in_ref[...] = jnp.zeros_like(own_in_ref)
+        size = min(128, back_ref.shape[0])
+
+        @pl.loop(0, back_ref.shape[0] // size)
+        def _(at):
+            rows = pl.ds(pl.multiple_of(at * size, size), size)
+            inverse = inv_ref[rows]
+            hat = tokens_ref[rows].astype(FULL) * inverse
+            grad = back_ref[rows]
+            own_in_ref[...] += jnp.sum(grad * hat, axis=0, keepdims=True)
+            back_ref[rows] = above_ref[rows] + norm_back(
+                grad * gain_in_ref[...], hat, inverse, 1
+            )
+
+
+def attend_grads(
+    dq, dk, dv, qkv, cosine, sine, gain_q, gain_k, attn_in, weights, mix, resid, *ends
+):
+    count, model = attn_in.shape
+    steps = 4
+    wide, narrow = HQ * DH // steps, HK * DH // steps
+    key_at, value_at = HQ * DH // narrow, (HQ + HK) * DH // narrow
+    rows = lambda size, at=0: pl.BlockSpec((size, count), lambda i: (at + i, 0))
+    columns = lambda size, at=0: pl.BlockSpec((model, size), lambda i: (0, at + i))
+    whole = lambda shape: pl.BlockSpec(shape, lambda i: (0, 0))
+    one = jax.ShapeDtypeStruct((DH, 1), FULL)
+    return pl.pallas_call(
+        attend_grads_kernel,
+        grid=(steps,),
+        in_specs=[
+            rows(wide),
+            rows(narrow),
+            rows(narrow),
+            rows(wide),
+            rows(narrow, key_at),
+            whole(cosine.shape),
+            whole(sine.shape),
+            whole((DH, 1)),
+            whole((DH, 1)),
+            whole(attn_in.shape),
+            columns(wide),
+            columns(narrow, key_at),
+            columns(narrow, value_at),
+            whole(mix.shape),
+            pl.BlockSpec((count, wide), lambda i: (0, i)),
+        ]
+        + [whole(end.shape) for end in ends],
+        out_specs=[
+            columns(wide),
+            columns(narrow),
+            columns(narrow),
+            columns(wide),
+            whole((count, model)),
+            whole((DH, 1)),
+            whole((DH, 1)),
+            whole((1, model)),
+        ],
+        out_shape=[
+            jax.ShapeDtypeStruct((model, HQ * DH), LOW),
+            jax.ShapeDtypeStruct((model, HK * DH), LOW),
+            jax.ShapeDtypeStruct((model, HK * DH), LOW),
+            jax.ShapeDtypeStruct((HQ * DH, model), LOW),
+            jax.ShapeDtypeStruct((count, model), FULL),
+            one,
+            one,
+            jax.ShapeDtypeStruct((1, model), FULL),
+        ],
+        compiler_params=pltpu.CompilerParams(vmem_limit_bytes=58 * 1024 * 1024),
+        cost_estimate=pl.CostEstimate(
+            flops=40_000_000_000, bytes_accessed=40_000_000, transcendentals=0
+        ),
+        name="attend_grads",
+    )(
+        dq,
+        dk,
+        dv,
+        qkv,
+        qkv,
+        cosine,
+        sine,
+        gain_q,
+        gain_k,
+        attn_in,
+        weights,
+        weights,
+        weights,
+        mix,
+        resid,
+        *ends,
+    )
+
+
+def ffn_kernel(
+    ids_ref, ffn_ref, ffn_other_ref, cot_ref, cot_other_ref, *refs, shards, fresh
+):
     blocks = refs[:shards]
     refs = refs[shards:]
     if not fresh:
@@ -223,21 +593,24 @@
     own = model // shards
     wide = w_down.shape[0]
     step = wide // shards
+    big, small = split_step(step)
     at_row = pl.program_id(0)
     parts = []
     for part in range(2 * wide // 256):
-        parts.append((part * own, own, part * 256, True))
+        parts.append((part * own, own, part * 256, True, 0))
     for part in range(model // 256):
-        parts.append((2 * wide // 256 * own + part * step, step, part * 256, False))
+        start = 2 * wide // 256 * own + part * step
+        parts.append((start, big, part * 256, False, 0))
+        parts.append((start + big, small, part * 256, False, shards * big))
 
     @pl.when(at_row == 0)
     def _():
         copies = []
         for place, block in enumerate(blocks):
             shard = ids_ref[place]
-            for start, count, column, first in parts:
+            for start, count, column, first, base in parts:
                 target = w_in if first else w_down
-                row = pl.multiple_of(shard * count, count)
+                row = pl.multiple_of(shard * count + base, count)
                 copies.append(
                     pltpu.make_async_copy(
                         block.at[pl.ds(start, count)],
@@ -252,8 +625,9 @@
         for copy in copies:
             copy.wait()
 
-    ffn = ffn_ref[...]
-    cot = cot_ref[...]
+    mine = at_row < pl.num_programs(0) // 2
+    ffn = jnp.where(mine, ffn_ref[...], ffn_other_ref[...])
+    cot = jnp.where(mine, cot_ref[...], cot_other_ref[...])
     both = dot(ffn, w_in[...], 1, 0)
     grad_hidden = dot(cot, w_down[...], 1, 1)
     gate, upper = both[:, :wide], both[:, wide:]
@@ -275,9 +649,9 @@
         shard = ids_ref[shards]
         for mark in range(shards):
             block = lax.bitwise_xor(shard, jnp.int32(mark))
-            for start, count, column, first in parts:
+            for start, count, column, first, base in parts:
                 source = g_in if first else g_down
-                row = pl.multiple_of(block * count, count)
+                row = pl.multiple_of(block * count + base, count)
                 stage[mark, start : start + count] = source[
                     pl.ds(row, count), column : column + 256
                 ].astype(LOW)
@@ -299,14 +673,17 @@
             copy.wait()
 
 
-def ffn_piece(ids, ffn_pair, cot_pair, blocks, sums, tile=512):
+def ffn_piece(ids, ffn_pair, cot_pair, blocks, sums, tile=256):
     shards = len(blocks)
     rows = blocks[0].shape[0]
-    count, model = ffn_pair.shape
-    own = model // shards
+    count, model = ffn_pair[0].shape
+    count = 2 * count
+    half = count // tile // 2
     wide = shards * rows * 256 // (3 * model)
     fresh = sums is None
     tall = pl.BlockSpec((tile, model), lambda i, ids: (i, 0))
+    mine = pl.BlockSpec((tile, model), lambda i, ids: (jnp.minimum(i, half - 1), 0))
+    other = pl.BlockSpec((tile, model), lambda i, ids: (jnp.maximum(i - half, 0), 0))
     where = pl.BlockSpec(memory_space=pl.ANY)
     sums = () if fresh else tuple(sums)
     side = jax.ShapeDtypeStruct((shards // 2, rows // 2, 256), LOW)
@@ -317,7 +694,7 @@
         grid_spec=pltpu.PrefetchScalarGridSpec(
             num_scalar_prefetch=1,
             grid=(count // tile,),
-            in_specs=[tall, tall] + [where] * shards + [tall] * len(sums),
+            in_specs=[mine, other] * 2 + [where] * shards + [tall] * len(sums),
             out_specs=[tall, tall] + [where] * 4,
             scratch_shapes=[
                 pltpu.VMEM((model, 2 * wide), LOW),
@@ -330,11 +707,11 @@
             ],
         ),
         out_shape=[total, total] + [side] * 4,
-        input_output_aliases={} if fresh else {3 + shards: 0, 4 + shards: 1},
+        input_output_aliases={} if fresh else {5 + shards: 0, 6 + shards: 1},
         compiler_params=pltpu.CompilerParams(vmem_limit_bytes=60 * 1024 * 1024),
         cost_estimate=pl.CostEstimate(flops=flops, bytes_accessed=40_000_000, transcendentals=0),
         name="ffn_piece",
-    )(ids, ffn_pair, cot_pair, *blocks, *sums)
+    )(ids, *ffn_pair, *cot_pair, *blocks, *sums)
 
 
 def query_blocks(length):
@@ -486,61 +863,31 @@
     step = hidden_own // (2 * PIECES)
     packed_wide = model + 2 * kv_wide
 
+    whole_wide = packed_wide + model
     gains = jnp.concatenate([attn_gain, ffn_gain, query_gain, key_gain])
-    gains = jnp.pad(gains, (0, packed_wide - gains.shape[0]))[None]
+    gains = jnp.pad(gains, (0, whole_wide - gains.shape[0]))[None]
     gains = jnp.pad(gains, ((0, GAIN_ROWS - 1), (0, 0)))
-    w_qkv = jnp.concatenate([w_query, w_key, w_value], axis=1)
-    qkv_part = jnp.concatenate(
-        [lax.dynamic_slice_in_dim(w_qkv, core * half, half, 0), gains], axis=0
-    )
-    qkv_blocks, ids = links.gather(qkv_part)
-    (out_part,) = hold([lax.dynamic_slice_in_dim(w_out, core * half, half, 0)], qkv_part)
-    out_blocks, _ = links.gather(out_part)
-
-    def both_halves(blocks):
-        mine = jnp.stack([block[:half] for block in blocks])
-        theirs = links.core_swap(mine)
-        whole = jnp.zeros((shards, 2, half, mine.shape[2]), LOW)
-        for side, parts in ((core, mine), (1 - core, theirs)):
-            for place in range(shards):
-                whole = lax.dynamic_update_slice(
-                    whole, parts[place][None, None], (ids[place], side, 0, 0)
-                )
-        return whole.reshape(model, mine.shape[2])
-
-    ffn_weights = []
-    marks = [qkv_blocks[1], out_blocks[1]]
-    held = hold([w_gate, w_up, w_down, cotangent], qkv_part)
-    cot_pair = jnp.concatenate([cotangent, links.core_swap(held[3])], axis=0)
-    for piece in range(PIECES):
-        def columns(weight):
-            parts = []
-            for block in range(shards):
-                base = block * hidden_own + piece * step
-                parts.append(
-                    jnp.where(
-                        core == 0,
-                        weight[:, base : base + step],
-                        weight[:, base + hidden_own // 2 : base + hidden_own // 2 + step],
-                    )
-                )
-            return jnp.concatenate(parts, axis=1)
-
-        down = lax.dynamic_slice_in_dim(
-            held[2], core * (hidden_own // 2) + piece * step, step, 0
-        )
-        packed = jnp.concatenate(
-            [
-                part[:, at : at + 256]
-                for part in (columns(held[0]), columns(held[1]), down)
-                for at in range(0, part.shape[1], 256)
-            ],
-            axis=0,
-        )
-        (packed,) = hold([packed], marks[-2])
-        blocks, _ = links.gather(packed)
-        marks.append(blocks[1])
-        ffn_weights.append(blocks)
+    attn_part = jnp.concatenate(
+        [
+            lax.dynamic_slice_in_dim(weight, core * half, half, 0)
+            for weight in (w_query, w_key, w_value, w_out)
+        ],
+        axis=1,
+    )
+    attn_part = jnp.concatenate([attn_part, gains], axis=0)
+    ids = links.ids()
+    core_line = core[None]
+    attn_near = links.near(attn_part)
+    held = hold([w_gate, w_up, w_down, cotangent], attn_part)
+    cot_pair = [cotangent, links.core_swap(held[3])]
+    packed = list(pack(core_line, *held[:3], shards))
+    attn_blocks = links.gather(attn_part, attn_near, packed[0], cot_pair[1])
+    (packed[0],) = hold([packed[0]], attn_blocks[1])
+    nears = [links.near(packed[0])]
+    (line,) = hold([ids], nears[0])
+    attn_mine = line_up(line, attn_blocks, half)
+    attn_full = both_cores(core_line, attn_mine, links.core_swap(attn_mine))
+    qkv_full, out_full = attn_full[:, :packed_wide], attn_full[:, packed_wide:]
 
     positions = doc_positions(doc_ids).reshape(count)
     freqs = jnp.power(ROPE_BASE, -2.0 * jnp.arange(DH // 2, dtype=FULL) / DH)
@@ -556,18 +903,20 @@
     inv_one = inverse_rms(x_in, 1)
     x_hat = x_in * inv_one
 
-    gain_rows = jnp.zeros((shards, packed_wide), LOW)
-    for place, block in enumerate(qkv_blocks):
+    gain_rows = jnp.zeros((shards, whole_wide), LOW)
+    for place, block in enumerate(attn_blocks):
         gain_rows = lax.dynamic_update_slice(gain_rows, block[half][None], (ids[place], 0))
     gain_rows = gain_rows.astype(FULL)
     gain_attn = gain_rows[:, :own].reshape(model)
     gain_ffn = gain_rows[:, own : 2 * own].reshape(model)
     gain_query = gain_rows[:, 2 * own : 2 * own + heads_own].reshape(1, DH, 1)
     gain_key = gain_rows[:, 2 * own + heads_own : 2 * own + 2 * heads_own].reshape(1, DH, 1)
-    qkv_full = both_halves(qkv_blocks)
-    out_full = both_halves(out_blocks)
 
     attn_in = (x_hat * gain_attn).astype(LOW)
+    (attn_in,) = hold([attn_in], nears[0])
+    ffn_weights = [links.gather(packed[0], nears[0])]
+    (packed[1],) = hold([packed[1]], nears[0])
+    nears.append(links.near(packed[1]))
     qkv = dot(qkv_full, attn_in, 0, 1)
     q_heads = qkv[:model].reshape(HQ, DH, count)
     k_heads = qkv[model : model + kv_wide].reshape(HK, DH, count)
@@ -581,41 +930,44 @@
     )
     k_low = rotate(k_hat * gain_key, cosine, sine).astype(LOW).reshape(kv_wide, count)
     mix_low, log_total = attend(q_low, k_low, v_low, mask)
+    (mix_low,) = hold([mix_low], nears[1], *ffn_weights[0])
+    ffn_weights.append(links.gather(packed[1], nears[1]))
+    for piece in range(2, PIECES):
+        (packed[piece],) = hold([packed[piece]], nears[piece - 1])
+        nears.append(links.near(packed[piece]))
 
     resid = x_in + dot(mix_low, out_full, 0, 0)
     inv_two = inverse_rms(resid, 1)
     resid_hat = resid * inv_two
     ffn_in = (resid_hat * gain_ffn).astype(LOW)
-    ffn_pair = jnp.concatenate([ffn_in, links.core_swap(ffn_in)], axis=0)
-
-    sums, sends = None, None
+    ffn_pair = [ffn_in, links.core_swap(ffn_in)]
+
+    sums, sends = None, []
     ffn_totals = []
-    for blocks in ffn_weights:
-        (order,) = hold([ids], sends) if sends is not None else [ids]
+    for piece in range(PIECES):
+        (order,) = hold([ids], *sends)
         *sums, leave_a, stay_a, leave_b, stay_b = ffn_piece(
-            order, ffn_pair, cot_pair, blocks, sums
+            order, ffn_pair, cot_pair, ffn_weights[piece], sums
         )
-        sends = None
-        for entry in ffn_totals:
+        if piece + 2 < PIECES:
+            ffn_weights.append(links.gather(packed[piece + 2], nears[piece + 2], stay_a))
+        sends = []
+        for number, entry in enumerate(ffn_totals):
+            if piece == PIECES - 1 and number == 0:
+                continue
             entry[1] = entry[0].send(stay_a)
-            sends = entry[1][0]
-        flow = links.total([leave_a, stay_a, leave_b, stay_b], 0, False)
+            sends += entry[1]
+        flow = links.total([leave_a, stay_a, leave_b, stay_b], 0)
         ffn_totals.append([flow, next(flow)])
 
     out_sum, ffn_back = sums
-    back_other = links.core_swap(ffn_back[count:].astype(LOW))
-    out_other = links.core_swap(out_sum[count:].astype(LOW))
+    first_sent = ffn_totals[0][0].send(stay_a)
+    (back_low,) = hold([ffn_back[count:].astype(LOW)], *first_sent, *sends)
+    back_other = links.core_swap(back_low)
     grad_ffn_in = ffn_back[:count] + back_other.astype(FULL)
     grad_gain_ffn = jnp.sum(grad_ffn_in * resid_hat, axis=0)
     grad_resid = cotangent.astype(FULL) + norm_back(grad_ffn_in * gain_ffn, resid_hat, inv_two, 1)
     grad_resid_low = grad_resid.astype(LOW)
-    result = (resid + out_sum[:count] + out_other.astype(FULL)).astype(LOW)
-
-    def half_sum(grad):
-        blocks = grad.reshape(shards, 2, half, grad.shape[1])
-        keep = lax.dynamic_index_in_dim(blocks, core, 1, keepdims=False)
-        give = lax.dynamic_index_in_dim(blocks, 1 - core, 1, keepdims=False)
-        return add_low(keep, links.core_swap(give))
 
     def owned(part):
         theirs = links.core_swap(part)
@@ -624,111 +976,110 @@
         return jnp.concatenate([low, high], axis=0).astype(FULL)
 
     grad_mix = dot(out_full, grad_resid_low, 1, 1).astype(LOW)
-    grad_out_w = dot(mix_low, grad_resid_low, 1, 0).astype(LOW)
-    out_flow = links.total(links.by_mark(half_sum(grad_out_w)), 1, True)
-    flows = [entry[0] for entry in ffn_totals] + [out_flow]
+    flows = [entry[0] for entry in ffn_totals]
     done = [None] * len(flows)
 
-    def advance(token):
-        sent = None
-        for place, flow in enumerate(flows):
+    def advance(*tokens):
+        sent = []
+        token = tokens[0] if tokens else None
+        for place in reversed(range(len(flows))):
             if done[place] is None:
-                got = flow.send(token)
+                got = flows[place].send(token)
+                if place >= PIECES and isinstance(got, list):
+                    token = got[0]
                 if isinstance(got, list):
-                    sent = got[0]
+                    sent += got
                 else:
                     done[place] = got
         return sent
 
-    sent_out = next(out_flow)
-    flows_now = flows
-    flows = flows[:-1]
-    sent = advance(grad_mix)
-    flows = flows_now
-    (do_low,) = hold([grad_mix], sent)
-    (do_low,) = hold([do_low], sent_out[0])
+    do_low = grad_mix
     dq_rot, dk_rot, dv_low = attend_back(q_low, k_low, v_low, mix_low, do_low, log_total, mask)
     sent = advance(dv_low)
-    (dq_rot, dk_rot) = hold([dq_rot, dk_rot], sent)
-    dq_norm = unrotate(dq_rot.reshape(HQ, DH, count), cosine, sine)
-    dk_norm = unrotate(dk_rot.reshape(HK, DH, count), cosine, sine)
-    grad_gain_query = jnp.sum(dq_norm * q_hat, axis=(0, 2))
-    grad_gain_key = jnp.sum(dk_norm * k_hat, axis=(0, 2))
-    dq_low = norm_back(dq_norm * gain_query, q_hat, q_inv, 1).astype(LOW).reshape(model, count)
-    dk_low = norm_back(dk_norm * gain_key, k_hat, k_inv, 1).astype(LOW).reshape(kv_wide, count)
-    d_qkv = jnp.concatenate([dq_low, dk_low, dv_low], axis=0)
-    grad_qkv_w = dot(attn_in, d_qkv, 0, 1).astype(LOW)
-    (d_qkv_later,) = hold([d_qkv], grad_qkv_w)
-    grad_attn_in = dot(d_qkv_later, qkv_full, 0, 1)
-    grad_gain_attn = jnp.sum(grad_attn_in * x_hat, axis=0)
-    grad_input = grad_resid + norm_back(grad_attn_in * gain_attn, x_hat, inv_one, 1)
+    (dq_rot, dk_rot) = hold([dq_rot, dk_rot], *sent)
+    (
+        grad_query_w,
+        grad_key_w,
+        grad_value_w,
+        grad_out_w,
+        grad_input,
+        own_q,
+        own_k,
+        grad_gain_attn,
+    ) = attend_grads(
+        dq_rot,
+        dk_rot,
+        dv_low,
+        qkv,
+        cosine[0],
+        sine[0],
+        gain_query[0],
+        gain_key[0],
+        attn_in,
+        attn_full,
+        mix_low,
+        grad_resid_low,
+        tokens,
+        inv_one,
+        gain_attn[None],
+        grad_resid,
+    )
+    advance(grad_key_w)
 
     gain_grads = jnp.concatenate(
         [
             grad_gain_attn.reshape(shards, own),
             grad_gain_ffn.reshape(shards, own),
-            grad_gain_query.reshape(shards, heads_own),
-            grad_gain_key.reshape(shards, heads_own),
+            own_q.reshape(shards, heads_own),
+            own_k.reshape(shards, heads_own),
         ],
         axis=1,
-    ).astype(LOW)
-    used = gain_grads.shape[1]
-    gain_grads = add_low(gain_grads, links.core_swap(gain_grads))
-    gain_grads = jnp.pad(gain_grads, ((0, 0), (0, packed_wide - used)))[:, None]
-    gain_grads = jnp.pad(gain_grads, ((0, 0), (0, GAIN_ROWS - 1), (0, 0)))
-    qkv_flow = links.total(
-        links.by_mark(jnp.concatenate([half_sum(grad_qkv_w), gain_grads], axis=1)), 1, True
-    )
-    flows = flows + [qkv_flow]
+    )
+    gain_rows = jnp.pad(
+        gain_grads.astype(LOW), ((0, 0), (0, whole_wide - gain_grads.shape[1]))
+    )[:, None]
+    gain_rows = jnp.pad(gain_rows, ((0, 0), (0, GAIN_ROWS - 1), (0, 0)))
+    shard_line = jnp.stack([ids[shards], core])
+    keep, give = sort_out(
+        shard_line, [grad_query_w, grad_key_w, grad_value_w, grad_out_w], gain_rows
+    )
+    came = links.core_swap(give)
+    attn_flow = links.total(links.by_mark(add_low(keep, came)), 1)
+    flows = flows + [attn_flow]
     done = done + [None]
-    next(qkv_flow)
-    token = grad_attn_in
-    while None in done:
+    token = next(attn_flow)[0]
+    while None in done[:PIECES]:
         advance(token)
         token = None
-    qkv_sum, out_w_sum = done[-1], done[-2]
-    gain_sum = qkv_sum[half].astype(FULL)
-    grad_qkv = owned(qkv_sum[:half])
-    grad_out_w = owned(out_w_sum)
-    ffn_grads = []
-    for part in done[:PIECES]:
-        both = []
-        for whole in (part, links.core_swap(part)):
-            tall = 2 * hidden_all // (2 * PIECES) // 256 * own
-            blocks = [whole[at : at + own] for at in range(0, tall, own)]
-            middle = len(blocks) // 2
-            both += [
-                jnp.concatenate(blocks[:middle], axis=1),
-                jnp.concatenate(blocks[middle:], axis=1),
-                jnp.concatenate(
-                    [whole[at : at + step] for at in range(tall, whole.shape[0], step)], axis=1
-                ),
-            ]
-        ffn_grads.append(both)
-
-    gate_parts = []
-    up_parts = []
-    down_parts = []
-    for block in range(shards):
-        for side in range(2):
-            for gate, up, _, gate_other, up_other, _ in ffn_grads:
-                at = block * step
-                span = slice(at, at + step)
-                gate_parts.append(jnp.where(core == side, gate[:, span], gate_other[:, span]))
-                up_parts.append(jnp.where(core == side, up[:, span], up_other[:, span]))
-    for side in range(2):
-        for _, _, down, _, _, down_other in ffn_grads:
-            down_parts.append(jnp.where(core == side, down, down_other))
+    advance()
+    (out_low,) = hold([out_sum[count:].astype(LOW)], done[1])
+    out_other = links.core_swap(out_low)
+    result = (resid + out_sum[:count] + out_other.astype(FULL)).astype(LOW)
+    ffn_mine = done[:PIECES]
+    ffn_theirs = [links.core_swap(part) for part in ffn_mine]
+    grad_gate_w, grad_up_w, grad_down_w = unpack(
+        core_line, ffn_mine, ffn_theirs, (w_gate.shape, w_up.shape, w_down.shape), shards
+    )
+    while None in done:
+        advance(grad_down_w)
+    gain_sum = done[-1][half].astype(FULL)
+    attn_sum = owned(done[-1][:half])
+    ffn_mine = done[:PIECES]
+    ffn_theirs = [links.core_swap(part) for part in ffn_mine]
+    grad_gate_w, grad_up_w, grad_down_w = unpack(
+        core_line, ffn_mine, ffn_theirs, (w_gate.shape, w_up.shape, w_down.shape), shards
+    )
+    at_value = model + kv_wide
     return (
         result,
         grad_input,
-        grad_qkv[:, :model],
-        grad_qkv[:, model : model + kv_wide],
-        grad_qkv[:, model + kv_wide :],
-        grad_out_w,
-        jnp.concatenate(gate_parts, axis=1).astype(FULL),
-        jnp.concatenate(up_parts, axis=1).astype(FULL),
-        jnp.concatenate(down_parts, axis=0).astype(FULL),
+        attn_sum[:, :model],
+        attn_sum[:, model:at_value],
+        attn_sum[:, at_value:packed_wide],
+        attn_sum[:, packed_wide:],
+        grad_gate_w,
+        grad_up_w,
+        grad_down_w,
         gain_sum[:own],
         gain_sum[own : 2 * own],
         gain_sum[2 * own : 2 * own + heads_own],

time: 710 us -> 535 us (0.75)
  other arithmetic: 130 us -> 66.6 us
  local copies, waits for them, and re-layouts: 98.1 us -> 45.4 us
  Pallas kernels: 174 us -> 219 us
  waiting for transfers between devices: 172 us -> 130 us
  starting transfers between devices: 86.5 us -> 57.1 us
  matrix products: 37.8 us -> 9.81 us
    ppermute x61 -> x38, waiting for transfers between devices: 144 us -> 74.2 us  [move(): return lax.ppermute(value, AXES, pairs)]
    pallas_call x0 -> x6, Pallas kernels: none -> 46.4 us  [the longest x1 27 us: attend_grads(): pl.pallas_call(attend_grads_kernel, grid=(steps,), in_specs=[rows(wide),...]
    dynamic_update_slice x22 -> x0, local copies, waits for them, and re-layouts: 31.6 us -> none  [the longest x15 24.8 us: both_halves(): lax.dynamic_update_slice(whole, parts[place][None, None], (ids[place], si...]
    ppermute x61 -> x38, starting transfers between devices: 64.6 us -> 33.6 us  [move(): return lax.ppermute(value, AXES, pairs)]
    dot_general x6 -> x3, matrix products: 37.8 us -> 9.81 us  [dot(): lax.dot_general(first, second, (((first_dim,), (second_dim,)), ((), ())),...]
    ppermute x9 -> x12, waiting for transfers between devices: 28.1 us -> 55.9 us  [rep_line(): return lax.ppermute(value, AXES, pairs)]
    unnamed x24 -> x1, other arithmetic: 20.1 us -> 0.01 us
    select_n x13 -> x0, other arithmetic: 18.7 us -> none  [the longest x6 8.68 us: per_device(): up_parts.append(jnp.where(core == side, up[:, span], up_other[:, span]))]
  transfers between devices with their start and end apart: 70 -> 50, of which waited for: 19 -> 16; matrix products, arithmetic and copies ran while one was open for 32% -> 14% of each run, Pallas kernels for 25% -> 36%
where the time goes in v2:
time: 535 us; the launch traced here: 530 us
  Pallas kernels  219 us (41%)
  waiting for transfers between devices  130 us (24%)
  other arithmetic  66.6 us (12%)
  starting transfers between devices  57.1 us (11%)
  local copies, waits for them, and re-layouts  45.4 us (8%)
  matrix products  9.81 us (2%)
    pallas_call x3, Pallas kernels, ffn_piece(): pl.pallas_call(functools.partial(ffn_kernel, shards=shards, fresh=fresh),...  122 us
    ppermute x38, waiting for transfers between devices, move(): return lax.ppermute(value, AXES, pairs)  74.2 us
    ppermute x12, waiting for transfers between devices, rep_line(): return lax.ppermute(value, AXES, pairs)  55.9 us
    ppermute x38, starting transfers between devices, move(): return lax.ppermute(value, AXES, pairs)  33.6 us
    pallas_call x1, Pallas kernels, attend_back(): pl.pallas_call(attend_back_kernel, grid=(HK,), in_specs=[two, one, one, t...  30.8 us
    pallas_call x1, Pallas kernels, attend_grads(): pl.pallas_call(attend_grads_kernel, grid=(steps,), in_specs=[rows(wide),...  27 us
    unnamed x142, local copies, waits for them, and re-layouts  26.6 us
    ppermute x12, starting transfers between devices, rep_line(): return lax.ppermute(value, AXES, pairs)  23.6 us
  transfers between devices with their start and end apart: 50, of which 16 were waited for; matrix products, arithmetic and copies ran while one was open for 14% of the time, Pallas kernels for 36%

profile of v2, /device:TPU:0, one launch (start us, length us, event | category | flops | bytes accessed | tf_op | source)
XLA Modules:
  0.0 530.1 jit_solution(9923139078625204576)
XLA Ops:
  4.3 2.6 collective-permute-start
  6.9 4.5 pack.1
  12.4 14.7 %collective-permute-done.refs_1_ = bf16[144,3072]{1,0:T(8,128)(2,1)S(1)} collective-permute-done((bf16[144,3072]{1,0:T(8,128)(2,1)S(1)}, bf16[144,3072]{1,0:T(8,128)(2,1)S(1)}, u32[]{:S(2)}, u32[]{:S(2)}) %collective-permute-start) | collective-permute-done | bytes 884768 | tf_op jit(solution)/shard_map/ppermute | solution.py:72
  27.1 1.8 collective-permute-start.2
  32.8 22.4 %collective-permute-done.2.refs_1_ = bf16[2304,256]{1,0:T(8,128)(2,1)} collective-permute-done((bf16[2304,256]{1,0:T(8,128)(2,1)}, bf16[2304,256]{1,0:T(8,128)(2,1)}, u32[]{:S(2)}, u32[]{:S(2)}) %collective-permute-start.2) | collective-permute-done | bytes 1179680 | tf_op jit(solution)/shard_map/ppermute | solution.py:72
  63.5 2.1 fusion
  66.2 1.8 fusion.6.mask_ref
  71.6 2.2 fusion.2.in_ref
  73.8 1.7 collective-permute-start.7
  78.6 2.1 both_cores.1
  80.7 4.8 fusion.3.q_ref.k_ref
  87.0 1.8 copy-done.28
  91.6 1.8 copy-done.4
  93.4 19.7 %attend.1 = (bf16[1024,1024]{1,0:T(8,128)(2,1)S(1)}, f32[8,2,1024]{2,1,0:T(2,128)S(1)}) custom-call(bf16[1024,1024]{1,0:T(8,128)(2,1)S(1)} %bitcast.64, bf16[512,1024]{1,0:T(8,128)(2,1)S(1)} %bitcast.66, bf16[512,1024]{1,0:T(8,128)(2,1)S(1)} %slice.390.v_ref, bf16[1024,1024]{1,0:T(8,128)(2,1)S(1)} %copy-done.4), custom_call_target="tpu_custom_call" | custom-call | flops 16000000000 | bytes 8000000 | tf_op jit(solution)/shard_map/attend/pallas_call | solution.py:741
  113.2 2.7 multiply_reduce_fusion.2
  122.2 40.0 %ffn_piece.3 = (f32[2048,1024]{1,0:T(8,128)}, f32[2048,1024]{1,0:T(8,128)}, bf16[2,1152,256]{2,1,0:T(8,128)(2,1)}, bf16[2,1152,256]{2,1,0:T(8,128)(2,1)}, bf16[2...) custom-call(s32[5]{0:T(128)} %copy-done.19, bf16[1024,1024]{1,0:T(8,128)(2,1)} %copy-done.44, ...), custom_call_target="tpu_custom_call" | custom-call | flops 28991029248 | bytes 40000000 | tf_op jit(solution)/shard_map/ffn_piece/pallas_call | solution.py:692
  165.9 41.2 %ffn_piece.4 = (f32[2048,1024]{1,0:T(8,128)}, f32[2048,1024]{1,0:T(8,128)}, bf16[2,1152,256]{2,1,0:T(8,128)(2,1)}, bf16[2,1152,256]{2,1,0:T(8,128)(2,1)}, bf16[2...) custom-call(s32[5]{0:T(128)} %copy-done.19, ...), custom_call_target="tpu_custom_call", output_to_operand_aliasing={{0}: (9, {}), {1}: (10, {})} | custom-call | flops 28991029248 | bytes 40000000 | tf_op jit(solution)/shard_map/ffn_piece/pallas_call | solution.py:692
  209.2 7.9 %collective-permute-done.11 = bf16[2,1152,256]{2,1,0:T(8,128)(2,1)} collective-permute-done((bf16[2,1152,256]{2,1,0:T(8,128)(2,1)}, bf16[2,1152,256]{2,1,0:T(8,128)(2,1)}, u32[]{:S(2)}, u32[]{:S(2)}) %collective-permute-start.11) | collective-permute-done | bytes 1179680 | tf_op jit(solution)/shard_map/ppermute | solution.py:72
  217.2 2.2 add_convert_fusion.27
  220.6 2.0 add_convert_fusion.28
  224.1 40.9 %ffn_piece.5 = (f32[2048,1024]{1,0:T(8,128)}, f32[2048,1024]{1,0:T(8,128)}, bf16[2,1152,256]{2,1,0:T(8,128)(2,1)}, bf16[2,1152,256]{2,1,0:T(8,128)(2,1)}, bf16[2...) custom-call(s32[5]{0:T(128)} %copy-done.19, ...), custom_call_target="tpu_custom_call", output_to_operand_aliasing={{0}: (9, {}), {1}: (10, {})} | custom-call | flops 28991029248 | bytes 40000000 | tf_op jit(solution)/shard_map/ffn_piece/pallas_call | solution.py:692
  265.1 2.2 add_convert_fusion.25
  267.3 4.0 slice.388
  271.3 2.1 add_convert_fusion.24
  284.9 3.4 collective-permute-start.27
  288.3 5.6 %multiply_reduce_fusion = (bf16[1024]{0:T(1024)(128)(2,1)S(1)}, f32[1024]{0:T(1024)S(1)}) fusion(f32[1024,1024]{1,0:T(8,128)} %copy-done.26, f32[1024]{0:T(1024)S(1)} %add_rsqrt_fusion.2, bf16[1024,1024]{1,0:T(8,128)(2,1)} %collective-permute-done.23, f32[2048,1024]{1,0:T(8,128)} %get-tuple-element.130, f32[1024]{0:T(1024)S(1)} %bitcast.69), kind=kLoop, calls=%fused_computation.12 | loop fusion | flops 8386560 | bytes 10500096 | tf_op jit(solution)/shard_map/reduce_sum | solution.py:968
  294.0 5.1 fusion.34
  299.1 2.4 convolution_convert_fusion.do_ref
  302.4 30.8 %attend_back.1 = (f32[1024,1024]{1,0:T(8,128)}, f32[512,1024]{1,0:T(8,128)S(1)}, bf16[512,1024]{1,0:T(8,128)(2,1)S(1)}) custom-call(bf16[1024,1024]{1,0:T(8,128)(2,1)S(1)} %bitcast.65, bf16[512,1024]{1,0:T(8,128)(2,1)S(1)} %bitcast.67, bf16[512,1024]{1,0:T(8,128)(2,1)S(1)} %slice.390.v_ref, bf16[1024,1024]{1,0:T(8,128)(2,1)S(1)} %copy-done.23, ...), custom_call_target="tpu_custom_call" | custom-call | flops 40000000000 | bytes 16000000 | tf_op jit(solution)/shard_map/attend_back/pallas_call | solution.py:809
  333.6 1.7 copy-done.47
  341.3 27.0 %attend_grads.1 = (bf16[1024,1024]{1,0:T(8,128)(2,1)}, bf16[1024,512]{1,0:T(8,128)(2,1)}, bf16[1024,512]{1,0:T(8,128)(2,1)}, bf16[1024,1024]{1,0:T(8,128)(2,1)},...) custom-call(f32[1024,1024]{1,0:T(8,128)} %get-tuple-element.146.dq_ref, ...), custom_call_target="tpu_custom_call" | custom-call | flops 40000000000 | bytes 40000000 | tf_op jit(solution)/shard_map/attend_grads/pallas_call | solution.py:515
  376.8 2.1 sort_out.1
  381.9 3.4 collective-permute-start.24
  385.4 9.4 %collective-permute-done.42 = bf16[1,1152,256]{2,1,0:T(8,128)(2,1)S(1)} collective-permute-done((bf16[1,1152,256]{2,1,0:T(8,128)(2,1)S(1)}, bf16[1,1152,256]{2,1,0:T(8,128)(2,1)S(1)}, u32[]{:S(2)}, u32[]{:S(2)}) %collective-permute-start.42) | collective-permute-done | bytes 589856 | tf_op jit(solution)/shard_map/ppermute | solution.py:72
  402.9 8.8 %collective-permute-done.24 = bf16[2304,256]{1,0:T(8,128)(2,1)S(1)} collective-permute-done((bf16[2304,256]{1,0:T(8,128)(2,1)S(1)}, bf16[2304,256]{1,0:T(8,128)(2,1)S(1)}, u32[]{:S(2)}, u32[]{:S(2)}) %collective-permute-start.24) | collective-permute-done | bytes 1179680 | tf_op jit(solution)/shard_map/ppermute | solution.py:165
  412.8 7.7 %collective-permute-done.30 = bf16[2,144,1536]{2,1,0:T(8,128)(2,1)S(1)} collective-permute-done((bf16[2,144,1536]{2,1,0:T(8,128)(2,1)S(1)}, bf16[2,144,1536]{2,1,0:T(8,128)(2,1)S(1)}, u32[]{:S(2)}, u32[]{:S(2)}) %collective-permute-start.30) | collective-permute-done | bytes 884768 | tf_op jit(solution)/shard_map/ppermute | solution.py:72
  422.1 13.4 %collective-permute-done.43 = bf16[2304,256]{1,0:T(8,128)(2,1)S(1)} collective-permute-done((bf16[2304,256]{1,0:T(8,128)(2,1)S(1)}, bf16[2304,256]{1,0:T(8,128)(2,1)S(1)}, u32[]{:S(2)}, u32[]{:S(2)}) %collective-permute-start.43) | collective-permute-done | bytes 1179680 | tf_op jit(solution)/shard_map/ppermute | solution.py:165
  435.9 1.7 collective-permute-start.44
  440.5 7.8 %collective-permute-done.34 = bf16[1,144,1536]{2,1,0:T(8,128)(2,1)S(1)} collective-permute-done((bf16[1,144,1536]{2,1,0:T(8,128)(2,1)S(1)}, bf16[1,144,1536]{2,1,0:T(8,128)(2,1)S(1)}, u32[]{:S(2)}, u32[]{:S(2)}) %collective-permute-start.34) | collective-permute-done | bytes 442400 | tf_op jit(solution)/shard_map/ppermute | solution.py:72
  450.4 6.4 %collective-permute-start.36 = (bf16[144,3072]{1,0:T(8,128)(2,1)}, bf16[144,3072]{1,0:T(8,128)(2,1)}, u32[]{:S(2)}, u32[]{:S(2)}) collective-permute-start(bf16[144,3072]{1,0:T(8,128)(2,1)} %pad_maximum_fusion.5), channel_id=1, source_target_pairs={{0,2},{1,3},{6,4},{7,5},{8,10},{9,11},{14,12},{15,13},{16,18},{17,... | collective-permute-start | bytes 2654216 | tf_op jit(solution)/shard_map/ppermute | solution.py:165
  456.8 3.8 slice.389
  463.6 6.8 %collective-permute-done.32 = bf16[2304,256]{1,0:T(8,128)(2,1)} collective-permute-done((bf16[2304,256]{1,0:T(8,128)(2,1)S(1)}, bf16[2304,256]{1,0:T(8,128)(2,1)}, u32[]{:S(2)}, u32[]{:S(2)}) %collective-permute-start.32) | collective-permute-done | bytes 1179680 | tf_op jit(solution)/shard_map/ppermute | solution.py:165
  470.4 2.4 collective-permute-done.36
  476.5 1.7 broadcast_select_fusion.1.refs_0_
  478.8 18.2 %collective-permute-done.45 = bf16[2304,256]{1,0:T(8,128)(2,1)S(1)} collective-permute-done((bf16[2304,256]{1,0:T(8,128)(2,1)S(1)}, bf16[2304,256]{1,0:T(8,128)(2,1)S(1)}, u32[]{:S(2)}, u32[]{:S(2)}) %collective-permute-start.45) | collective-permute-done | bytes 1179680 | tf_op jit(solution)/shard_map/ppermute | solution.py:165
  499.7 6.7 %add_convert_fusion.1 = bf16[1024,1024]{1,0:T(8,128)(2,1)} fusion(bf16[1024,1024]{1,0:T(8,128)(2,1)} %collective-permute-done.35, f32[1024,1024]{1,0:T(8,128)} %copy-done.26, f32[2048,1024]{1,0:T(8,128)} %get-tuple-element.123), kind=kLoop, calls=%fused_computation.11 | loop fusion | flops 4194304 | bytes 12582912 | tf_op jit(solution)/shard_map/convert_element_type | solution.py:1057
  506.4 9.9 %unpack.1 = (f32[256,4608]{1,0:T(8,128)}, f32[256,4608]{1,0:T(8,128)}, f32[1152,1024]{1,0:T(8,128)}) custom-call(s32[1]{0:T(128)} %bitcast.core_ref, bf16[2304,256]{1,0:T(8,128)(2,1)} %copy-done.35, bf16[2304,256]{1,0:T(8,128)(2,1)} %copy-done.34, bf16[2304,256]{1,0:T(8,128)(2,1)} %copy-done.36, bf16[2304,256]{1,0:T(8,128)(2,1)} %collective-permute-done.46.refs_3_, ...), custom_call_target="tpu_custom_call" | custom-call | bytes 21000000 | tf_op jit(solution)/shard_map/unpack/pallas_call | solution.py:278
  516.3 6.3 %collective-permute-done.38 = bf16[144,3072]{1,0:T(8,128)(2,1)} collective-permute-done((bf16[144,3072]{1,0:T(8,128)(2,1)}, bf16[144,3072]{1,0:T(8,128)(2,1)}, u32[]{:S(2)}, u32[]{:S(2)}) %collective-permute-start.38) | collective-permute-done | bytes 884768 | tf_op jit(solution)/shard_map/ppermute | solution.py:165
  (314 shorter events, 106.3 us)
Async XLA Ops:
  3.8 23.3 %collective-permute-start.1 = (bf16[1024,1024]{1,0:T(8,128)(2,1)}, bf16[1024,1024]{1,0:T(8,128)(2,1)S(1)}, u32[]{:S(2)}, u32[]{:S(2)}) collective-permute-start(bf16[1024,1024]{1,0:T(8,128)(2,1)} %cot_ref.5), channel_id=1, source_target_pairs={{0,1},{1,0},{2,3},{3,2},{4,5},{5,4},{6,7},{7,6},{8,9},{9,8},{10,11... | collective-permute-start | bytes 6291464 | tf_op jit(solution)/shard_map/ppermute | solution.py:72
  4.3 22.8 %collective-permute-start = (bf16[144,3072]{1,0:T(8,128)(2,1)S(1)}, bf16[144,3072]{1,0:T(8,128)(2,1)S(1)}, u32[]{:S(2)}, u32[]{:S(2)}) collective-permute-start(bf16[144,3072]{1,0:T(8,128)(2,1)S(1)} %fusion.10.refs_0_), channel_id=1, source_target_pairs={{0,8},{1,9},{2,18},{3,19},{4,12},{5,13},{6,22},{7,23},{8,0},{9,1},... | collective-permute-start | bytes 2654216 | tf_op jit(solution)/shard_map/ppermute | solution.py:72
  27.1 28.0 %collective-permute-start.2 = (bf16[2304,256]{1,0:T(8,128)(2,1)}, bf16[2304,256]{1,0:T(8,128)(2,1)}, u32[]{:S(2)}, u32[]{:S(2)}) collective-permute-start(bf16[2304,256]{1,0:T(8,128)(2,1)} %get-tuple-element.101.refs_0_), channel_id=1, source_target_pairs={{0,8},{1,9},{2,18},{3,19},{4,12},{5,13},{6,22},{7,23},{8,0},{9,1},... | collective-permute-start | bytes 3538952 | tf_op jit(solution)/shard_map/ppermute | solution.py:72
  28.9 26.3 %collective-permute-start.3 = (bf16[144,3072]{1,0:T(8,128)(2,1)S(1)}, bf16[144,3072]{1,0:T(8,128)(2,1)S(1)}, u32[]{:S(2)}, u32[]{:S(2)}) collective-permute-start(bf16[144,3072]{1,0:T(8,128)(2,1)S(1)} %collective-permute-done.refs_1_), channel_id=1, source_target_pairs={{0,2},{1,3},{2,0},{3,1},{4,6},{5,7},{6,4},{7,5},{8,10},{9,11},{10,... | collective-permute-start | bytes 2654216 | tf_op jit(solution)/shard_map/ppermute | solution.py:72
  30.5 25.6 %collective-permute-start.4 = (bf16[144,3072]{1,0:T(8,128)(2,1)S(1)}, bf16[144,3072]{1,0:T(8,128)(2,1)S(1)}, u32[]{:S(2)}, u32[]{:S(2)}) collective-permute-start(bf16[144,3072]{1,0:T(8,128)(2,1)S(1)} %collective-permute-done.refs_1_), channel_id=1, source_target_pairs={{0,16},{1,17},{2,10},{3,11},{4,20},{5,21},{6,14},{7,15},{8,24},{9,... | collective-permute-start | bytes 2654216 | tf_op jit(solution)/shard_map/ppermute | solution.py:72
  62.9 15.6 %collective-permute-start.5 = (bf16[4,128,3072]{2,1,0:T(8,128)(2,1)S(1)}, bf16[4,128,3072]{2,1,0:T(8,128)(2,1)}, u32[]{:S(2)}, u32[]{:S(2)}) collective-permute-start(bf16[4,128,3072]{2,1,0:T(8,128)(2,1)S(1)} %line_up.1.mine), channel_id=1, source_target_pairs={{0,1},{1,0},{2,3},{3,2},{4,5},{5,4},{6,7},{7,6},{8,9},{9,8},{10,11... | collective-permute-start | bytes 9437192 | tf_op jit(solution)/shard_map/ppermute | solution.py:72
  73.8 39.3 %collective-permute-start.7 = (bf16[2304,256]{1,0:T(8,128)(2,1)}, bf16[2304,256]{1,0:T(8,128)(2,1)S(1)}, u32[]{:S(2)}, u32[]{:S(2)}) collective-permute-start(bf16[2304,256]{1,0:T(8,128)(2,1)} %collective-permute-done.2.refs_1_), channel_id=1, source_target_pairs={{0,2},{1,3},{2,0},{3,1},{4,6},{5,7},{6,4},{7,5},{8,10},{9,11},{10,... | collective-permute-start | bytes 3538952 | tf_op jit(solution)/shard_map/ppermute | solution.py:72
  75.6 37.6 %collective-permute-start.8 = (bf16[2304,256]{1,0:T(8,128)(2,1)}, bf16[2304,256]{1,0:T(8,128)(2,1)S(1)}, u32[]{:S(2)}, u32[]{:S(2)}) collective-permute-start(bf16[2304,256]{1,0:T(8,128)(2,1)} %collective-permute-done.2.refs_1_), channel_id=1, source_target_pairs={{0,16},{1,17},{2,10},{3,11},{4,20},{5,21},{6,14},{7,15},{8,24},{9,... | collective-permute-start | bytes 3538952 | tf_op jit(solution)/shard_map/ppermute | solution.py:72
  77.1 36.1 %collective-permute-start.6 = (bf16[2304,256]{1,0:T(8,128)(2,1)S(1)}, bf16[2304,256]{1,0:T(8,128)(2,1)}, u32[]{:S(2)}, u32[]{:S(2)}) collective-permute-start(bf16[2304,256]{1,0:T(8,128)(2,1)S(1)} %copy-done.21), channel_id=1, source_target_pairs={{0,8},{1,9},{2,18},{3,19},{4,12},{5,13},{6,22},{7,23},{8,0},{9,1},... | collective-permute-start | bytes 3538952 | tf_op jit(solution)/shard_map/ppermute | solution.py:72
  119.2 46.2 %collective-permute-start.12 = (bf16[2304,256]{1,0:T(8,128)(2,1)}, bf16[2304,256]{1,0:T(8,128)(2,1)}, u32[]{:S(2)}, u32[]{:S(2)}) collective-permute-start(bf16[2304,256]{1,0:T(8,128)(2,1)} %collective-permute-done.6.refs_1_), channel_id=1, source_target_pairs={{0,2},{1,3},{2,0},{3,1},{4,6},{5,7},{6,4},{7,5},{8,10},{9,11},{10,... | collective-permute-start | bytes 3538952 | tf_op jit(solution)/shard_map/ppermute | solution.py:72
  119.7 46.2 %collective-permute-start.13 = (bf16[2304,256]{1,0:T(8,128)(2,1)}, bf16[2304,256]{1,0:T(8,128)(2,1)}, u32[]{:S(2)}, u32[]{:S(2)}) collective-permute-start(bf16[2304,256]{1,0:T(8,128)(2,1)} %collective-permute-done.6.refs_1_), channel_id=1, source_target_pairs={{0,16},{1,17},{2,10},{3,11},{4,20},{5,21},{6,14},{7,15},{8,24},{9,... | collective-permute-start | bytes 3538952 | tf_op jit(solution)/shard_map/ppermute | solution.py:72
  120.2 42.0 %collective-permute-start.14 = (bf16[2304,256]{1,0:T(8,128)(2,1)}, bf16[2304,256]{1,0:T(8,128)(2,1)}, u32[]{:S(2)}, u32[]{:S(2)}) collective-permute-start(bf16[2304,256]{1,0:T(8,128)(2,1)} %get-tuple-element.119.refs_0_), channel_id=1, source_target_pairs={{0,8},{1,9},{2,18},{3,19},{4,12},{5,13},{6,22},{7,23},{8,0},{9,1},... | collective-permute-start | bytes 3538952 | tf_op jit(solution)/shard_map/ppermute | solution.py:72
  162.2 60.4 %collective-permute-start.15 = (bf16[2304,256]{1,0:T(8,128)(2,1)}, bf16[2304,256]{1,0:T(8,128)(2,1)}, u32[]{:S(2)}, u32[]{:S(2)}) collective-permute-start(bf16[2304,256]{1,0:T(8,128)(2,1)} %collective-permute-done.14.refs_1_), channel_id=1, source_target_pairs={{0,2},{1,3},{2,0},{3,1},{4,6},{5,7},{6,4},{7,5},{8,10},{9,11},{10,... | collective-permute-start | bytes 3538952 | tf_op jit(solution)/shard_map/ppermute | solution.py:72
  162.7 61.4 %collective-permute-start.16 = (bf16[2304,256]{1,0:T(8,128)(2,1)}, bf16[2304,256]{1,0:T(8,128)(2,1)}, u32[]{:S(2)}, u32[]{:S(2)}) collective-permute-start(bf16[2304,256]{1,0:T(8,128)(2,1)} %collective-permute-done.14.refs_1_), channel_id=1, source_target_pairs={{0,16},{1,17},{2,10},{3,11},{4,20},{5,21},{6,14},{7,15},{8,24},{9,... | collective-permute-start | bytes 3538952 | tf_op jit(solution)/shard_map/ppermute | solution.py:72
  163.9 44.2 %collective-permute-start.10 = (bf16[2,1152,256]{2,1,0:T(8,128)(2,1)}, bf16[2,1152,256]{2,1,0:T(8,128)(2,1)}, u32[]{:S(2)}, u32[]{:S(2)}) collective-permute-start(bf16[2,1152,256]{2,1,0:T(8,128)(2,1)} %get-tuple-element.109), channel_id=1, source_target_pairs={{0,8},{1,9},{2,10},{3,11},{4,12},{5,13},{6,14},{7,15},{8,0},{9,1},... | collective-permute-start | bytes 3538952 | tf_op jit(solution)/shard_map/ppermute | solution.py:72
  165.4 51.8 %collective-permute-start.11 = (bf16[2,1152,256]{2,1,0:T(8,128)(2,1)}, bf16[2,1152,256]{2,1,0:T(8,128)(2,1)}, u32[]{:S(2)}, u32[]{:S(2)}) collective-permute-start(bf16[2,1152,256]{2,1,0:T(8,128)(2,1)} %get-tuple-element.110), channel_id=1, source_target_pairs={{0,16},{1,17},{2,18},{3,19},{4,20},{5,21},{6,22},{7,23},{8,24},{9,... | collective-permute-start | bytes 3538952 | tf_op jit(solution)/shard_map/ppermute | solution.py:72
  207.1 58.0 %collective-permute-start.17 = (bf16[2,1152,256]{2,1,0:T(8,128)(2,1)}, bf16[2,1152,256]{2,1,0:T(8,128)(2,1)}, u32[]{:S(2)}, u32[]{:S(2)}) collective-permute-start(bf16[2,1152,256]{2,1,0:T(8,128)(2,1)} %get-tuple-element.124), channel_id=1, source_target_pairs={{0,8},{1,9},{2,10},{3,11},{4,12},{5,13},{6,14},{7,15},{8,0},{9,1},... | collective-permute-start | bytes 3538952 | tf_op jit(solution)/shard_map/ppermute | solution.py:72
  208.0 57.0 %collective-permute-start.18 = (bf16[2,1152,256]{2,1,0:T(8,128)(2,1)}, bf16[2,1152,256]{2,1,0:T(8,128)(2,1)}, u32[]{:S(2)}, u32[]{:S(2)}) collective-permute-start(bf16[2,1152,256]{2,1,0:T(8,128)(2,1)} %get-tuple-element.125), channel_id=1, source_target_pairs={{0,16},{1,17},{2,18},{3,19},{4,20},{5,21},{6,22},{7,23},{8,24},{9,... | collective-permute-start | bytes 3538952 | tf_op jit(solution)/shard_map/ppermute | solution.py:72
  219.4 54.0 %collective-permute-start.22 = (bf16[1,1152,256]{2,1,0:T(8,128)(2,1)}, bf16[1,1152,256]{2,1,0:T(8,128)(2,1)}, u32[]{:S(2)}, u32[]{:S(2)}) collective-permute-start(bf16[1,1152,256]{2,1,0:T(8,128)(2,1)} %add_convert_fusion.27), channel_id=1, source_target_pairs={{0,8},{1,9},{2,10},{3,11},{4,12},{5,13},{6,14},{7,15},{8,0},{9,1},... | collective-permute-start | bytes 1769480 | tf_op jit(solution)/shard_map/ppermute | solution.py:72
  222.6 50.8 %collective-permute-start.21 = (bf16[1,1152,256]{2,1,0:T(8,128)(2,1)}, bf16[1,1152,256]{2,1,0:T(8,128)(2,1)}, u32[]{:S(2)}, u32[]{:S(2)}) collective-permute-start(bf16[1,1152,256]{2,1,0:T(8,128)(2,1)} %add_convert_fusion.28), channel_id=1, source_target_pairs={{0,16},{1,17},{2,18},{3,19},{4,20},{5,21},{6,22},{7,23},{8,24},{9,... | collective-permute-start | bytes 1769480 | tf_op jit(solution)/shard_map/ppermute | solution.py:72
  277.8 7.1 %collective-permute-start.23 = (bf16[1024,1024]{1,0:T(8,128)(2,1)}, bf16[1024,1024]{1,0:T(8,128)(2,1)}, u32[]{:S(2)}, u32[]{:S(2)}) collective-permute-start(bf16[1024,1024]{1,0:T(8,128)(2,1)} %slice.388), channel_id=1, source_target_pairs={{0,1},{1,0},{2,3},{3,2},{4,5},{5,4},{6,7},{7,6},{8,9},{9,8},{10,11... | collective-permute-start | bytes 6291464 | tf_op jit(solution)/shard_map/ppermute | solution.py:72
  280.8 54.6 %collective-permute-start.20 = (bf16[1,1152,256]{2,1,0:T(8,128)(2,1)}, bf16[1,1152,256]{2,1,0:T(8,128)(2,1)S(1)}, u32[]{:S(2)}, u32[]{:S(2)}) collective-permute-start(bf16[1,1152,256]{2,1,0:T(8,128)(2,1)} %add_convert_fusion.24), channel_id=1, source_target_pairs={{0,8},{1,9},{2,10},{3,11},{4,12},{5,13},{6,14},{7,15},{8,0},{9,1},... | collective-permute-start | bytes 1769480 | tf_op jit(solution)/shard_map/ppermute | solution.py:72
  281.4 54.1 %collective-permute-start.19 = (bf16[1,1152,256]{2,1,0:T(8,128)(2,1)}, bf16[1,1152,256]{2,1,0:T(8,128)(2,1)S(1)}, u32[]{:S(2)}, u32[]{:S(2)}) collective-permute-start(bf16[1,1152,256]{2,1,0:T(8,128)(2,1)} %add_convert_fusion.25), channel_id=1, source_target_pairs={{0,16},{1,17},{2,18},{3,19},{4,20},{5,21},{6,22},{7,23},{8,24},{9,... | collective-permute-start | bytes 1769480 | tf_op jit(solution)/shard_map/ppermute | solution.py:72
  282.2 51.4 %collective-permute-start.25 = (bf16[2,1152,256]{2,1,0:T(8,128)(2,1)}, bf16[2,1152,256]{2,1,0:T(8,128)(2,1)S(1)}, u32[]{:S(2)}, u32[]{:S(2)}) collective-permute-start(bf16[2,1152,256]{2,1,0:T(8,128)(2,1)} %get-tuple-element.140), channel_id=1, source_target_pairs={{0,8},{1,9},{2,10},{3,11},{4,12},{5,13},{6,14},{7,15},{8,0},{9,1},... | collective-permute-start | bytes 3538952 | tf_op jit(solution)/shard_map/ppermute | solution.py:72
  283.4 50.2 %collective-permute-start.26 = (bf16[2,1152,256]{2,1,0:T(8,128)(2,1)}, bf16[2,1152,256]{2,1,0:T(8,128)(2,1)S(1)}, u32[]{:S(2)}, u32[]{:S(2)}) collective-permute-start(bf16[2,1152,256]{2,1,0:T(8,128)(2,1)} %get-tuple-element.141), channel_id=1, source_target_pairs={{0,16},{1,17},{2,18},{3,19},{4,20},{5,21},{6,22},{7,23},{8,24},{9,... | collective-permute-start | bytes 3538952 | tf_op jit(solution)/shard_map/ppermute | solution.py:72
  284.9 48.3 %collective-permute-start.27 = (bf16[2304,256]{1,0:T(8,128)(2,1)}, bf16[2304,256]{1,0:T(8,128)(2,1)S(1)}, u32[]{:S(2)}, u32[]{:S(2)}) collective-permute-start(bf16[2304,256]{1,0:T(8,128)(2,1)} %pad_maximum_fusion), channel_id=1, source_target_pairs={{0,2},{1,3},{6,4},{7,5},{8,10},{9,11},{14,12},{15,13},{16,18},{17,... | collective-permute-start | bytes 3538952 | tf_op jit(solution)/shard_map/ppermute | solution.py:165
  378.9 19.0 %collective-permute-start.29 = (bf16[4,144,3072]{2,1,0:T(8,128)(2,1)S(1)}, bf16[4,144,3072]{2,1,0:T(8,128)(2,1)S(1)}, u32[]{:S(2)}, u32[]{:S(2)}) collective-permute-start(bf16[4,144,3072]{2,1,0:T(8,128)(2,1)S(1)} %get-tuple-element.157), channel_id=1, source_target_pairs={{0,1},{1,0},{2,3},{3,2},{4,5},{5,4},{6,7},{7,6},{8,9},{9,8},{10,11... | collective-permute-start | bytes 10616840 | tf_op jit(solution)/shard_map/ppermute | solution.py:72
  379.0 15.7 %collective-permute-start.42 = (bf16[1,1152,256]{2,1,0:T(8,128)(2,1)S(1)}, bf16[1,1152,256]{2,1,0:T(8,128)(2,1)S(1)}, u32[]{:S(2)}, u32[]{:S(2)}) collective-permute-start(bf16[1,1152,256]{2,1,0:T(8,128)(2,1)S(1)} %copy-done.62), channel_id=1, source_target_pairs={{0,8},{1,9},{2,10},{3,11},{4,12},{5,13},{6,14},{7,15},{8,0},{9,1},... | collective-permute-start | bytes 1769480 | tf_op jit(solution)/shard_map/ppermute | solution.py:72
  380.6 15.4 %collective-permute-start.41 = (bf16[1,1152,256]{2,1,0:T(8,128)(2,1)S(1)}, bf16[1,1152,256]{2,1,0:T(8,128)(2,1)S(1)}, u32[]{:S(2)}, u32[]{:S(2)}) collective-permute-start(bf16[1,1152,256]{2,1,0:T(8,128)(2,1)S(1)} %add_convert_fusion.16), channel_id=1, source_target_pairs={{0,16},{1,17},{2,18},{3,19},{4,20},{5,21},{6,22},{7,23},{8,24},{9,... | collective-permute-start | bytes 1769480 | tf_op jit(solution)/shard_map/ppermute | solution.py:72
  381.2 16.7 %collective-permute-start.39 = (bf16[2304,256]{1,0:T(8,128)(2,1)S(1)}, bf16[2304,256]{1,0:T(8,128)(2,1)S(1)}, u32[]{:S(2)}, u32[]{:S(2)}) collective-permute-start(bf16[2304,256]{1,0:T(8,128)(2,1)S(1)} %add_convert_fusion.7), channel_id=1, source_target_pairs={{2,4},{3,5},{4,2},{5,3},{10,12},{11,13},{12,10},{13,11},{18,20},{1... | collective-permute-start | bytes 3538952 | tf_op jit(solution)/shard_map/ppermute | solution.py:165
  381.9 29.7 %collective-permute-start.24 = (bf16[2304,256]{1,0:T(8,128)(2,1)S(1)}, bf16[2304,256]{1,0:T(8,128)(2,1)S(1)}, u32[]{:S(2)}, u32[]{:S(2)}) collective-permute-start(bf16[2304,256]{1,0:T(8,128)(2,1)S(1)} %copy-done.56), channel_id=1, source_target_pairs={{0,2},{1,3},{6,4},{7,5},{8,10},{9,11},{14,12},{15,13},{16,18},{17,... | collective-permute-start | bytes 3538952 | tf_op jit(solution)/shard_map/ppermute | solution.py:165
  396.5 39.0 %collective-permute-start.43 = (bf16[2304,256]{1,0:T(8,128)(2,1)S(1)}, bf16[2304,256]{1,0:T(8,128)(2,1)S(1)}, u32[]{:S(2)}, u32[]{:S(2)}) collective-permute-start(bf16[2304,256]{1,0:T(8,128)(2,1)S(1)} %pad_maximum_fusion.2), channel_id=1, source_target_pairs={{0,2},{1,3},{6,4},{7,5},{8,10},{9,11},{14,12},{15,13},{16,18},{17,... | collective-permute-start | bytes 3538952 | tf_op jit(solution)/shard_map/ppermute | solution.py:165
  399.6 20.9 %collective-permute-start.30 = (bf16[2,144,1536]{2,1,0:T(8,128)(2,1)S(1)}, bf16[2,144,1536]{2,1,0:T(8,128)(2,1)S(1)}, u32[]{:S(2)}, u32[]{:S(2)}) collective-permute-start(bf16[2,144,1536]{2,1,0:T(8,128)(2,1)S(1)} %pad_maximum_fusion.4), channel_id=1, source_target_pairs={{0,8},{1,9},{2,10},{3,11},{4,12},{5,13},{6,14},{7,15},{8,0},{9,1},... | collective-permute-start | bytes 2654216 | tf_op jit(solution)/shard_map/ppermute | solution.py:72
  400.2 20.7 %collective-permute-start.31 = (bf16[2,144,1536]{2,1,0:T(8,128)(2,1)S(1)}, bf16[2,144,1536]{2,1,0:T(8,128)(2,1)S(1)}, u32[]{:S(2)}, u32[]{:S(2)}) collective-permute-start(bf16[2,144,1536]{2,1,0:T(8,128)(2,1)S(1)} %stack.34), channel_id=1, source_target_pairs={{0,16},{1,17},{2,18},{3,19},{4,20},{5,21},{6,22},{7,23},{8,24},{9,... | collective-permute-start | bytes 2654216 | tf_op jit(solution)/shard_map/ppermute | solution.py:72
  401.6 59.1 %collective-permute-start.40 = (bf16[2304,256]{1,0:T(8,128)(2,1)S(1)}, bf16[2304,256]{1,0:T(8,128)(2,1)}, u32[]{:S(2)}, u32[]{:S(2)}) collective-permute-start(bf16[2304,256]{1,0:T(8,128)(2,1)S(1)} %add_convert_fusion.4), channel_id=1, source_target_pairs={{2,0},{3,1},{4,6},{5,7},{10,8},{11,9},{12,14},{13,15},{18,16},{19,... | collective-permute-start | bytes 3538952 | tf_op jit(solution)/shard_map/ppermute | solution.py:165
  412.0 26.8 %collective-permute-start.28 = (bf16[2304,256]{1,0:T(8,128)(2,1)S(1)}, bf16[2304,256]{1,0:T(8,128)(2,1)S(1)}, u32[]{:S(2)}, u32[]{:S(2)}) collective-permute-start(bf16[2304,256]{1,0:T(8,128)(2,1)S(1)} %add_convert_fusion.6), channel_id=1, source_target_pairs={{2,4},{3,5},{4,2},{5,3},{10,12},{11,13},{12,10},{13,11},{18,20},{1... | collective-permute-start | bytes 3538952 | tf_op jit(solution)/shard_map/ppermute | solution.py:165
  421.1 19.5 %collective-permute-start.33 = (bf16[1,144,1536]{2,1,0:T(8,128)(2,1)S(1)}, bf16[1,144,1536]{2,1,0:T(8,128)(2,1)S(1)}, u32[]{:S(2)}, u32[]{:S(2)}) collective-permute-start(bf16[1,144,1536]{2,1,0:T(8,128)(2,1)S(1)} %get-tuple-element.186), channel_id=1, source_target_pairs={{0,16},{1,17},{2,18},{3,19},{4,20},{5,21},{6,22},{7,23},{8,24},{9,... | collective-permute-start | bytes 1327112 | tf_op jit(solution)/shard_map/ppermute | solution.py:72
  435.9 24.8 %collective-permute-start.44 = (bf16[2304,256]{1,0:T(8,128)(2,1)S(1)}, bf16[2304,256]{1,0:T(8,128)(2,1)}, u32[]{:S(2)}, u32[]{:S(2)}) collective-permute-start(bf16[2304,256]{1,0:T(8,128)(2,1)S(1)} %add_convert_fusion.3), channel_id=1, source_target_pairs={{2,4},{3,5},{4,2},{5,3},{10,12},{11,13},{12,10},{13,11},{18,20},{1... | collective-permute-start | bytes 3538952 | tf_op jit(solution)/shard_map/ppermute | solution.py:165
  437.5 10.8 %collective-permute-start.34 = (bf16[1,144,1536]{2,1,0:T(8,128)(2,1)S(1)}, bf16[1,144,1536]{2,1,0:T(8,128)(2,1)S(1)}, u32[]{:S(2)}, u32[]{:S(2)}) collective-permute-start(bf16[1,144,1536]{2,1,0:T(8,128)(2,1)S(1)} %get-tuple-element.185), channel_id=1, source_target_pairs={{0,8},{1,9},{2,10},{3,11},{4,12},{5,13},{6,14},{7,15},{8,0},{9,1},... | collective-permute-start | bytes 1327112 | tf_op jit(solution)/shard_map/ppermute | solution.py:72
  439.2 31.2 %collective-permute-start.32 = (bf16[2304,256]{1,0:T(8,128)(2,1)S(1)}, bf16[2304,256]{1,0:T(8,128)(2,1)}, u32[]{:S(2)}, u32[]{:S(2)}) collective-permute-start(bf16[2304,256]{1,0:T(8,128)(2,1)S(1)} %add_convert_fusion.5), channel_id=1, source_target_pairs={{2,0},{3,1},{4,6},{5,7},{10,8},{11,9},{12,14},{13,15},{18,16},{19,... | collective-permute-start | bytes 3538952 | tf_op jit(solution)/shard_map/ppermute | solution.py:165
  450.4 22.4 %collective-permute-start.36 = (bf16[144,3072]{1,0:T(8,128)(2,1)}, bf16[144,3072]{1,0:T(8,128)(2,1)}, u32[]{:S(2)}, u32[]{:S(2)}) collective-permute-start(bf16[144,3072]{1,0:T(8,128)(2,1)} %pad_maximum_fusion.5), channel_id=1, source_target_pairs={{0,2},{1,3},{6,4},{7,5},{8,10},{9,11},{14,12},{15,13},{16,18},{17,... | collective-permute-start | bytes 2654216 | tf_op jit(solution)/shard_map/ppermute | solution.py:165
  462.3 34.7 %collective-permute-start.45 = (bf16[2304,256]{1,0:T(8,128)(2,1)S(1)}, bf16[2304,256]{1,0:T(8,128)(2,1)S(1)}, u32[]{:S(2)}, u32[]{:S(2)}) collective-permute-start(bf16[2304,256]{1,0:T(8,128)(2,1)S(1)} %add_convert_fusion.2), channel_id=1, source_target_pairs={{2,0},{3,1},{4,6},{5,7},{10,8},{11,9},{12,14},{13,15},{18,16},{19,... | collective-permute-start | bytes 3538952 | tf_op jit(solution)/shard_map/ppermute | solution.py:165
  474.2 4.6 collective-permute-start.37
  476.4 23.3 %collective-permute-start.35 = (bf16[1024,1024]{1,0:T(8,128)(2,1)}, bf16[1024,1024]{1,0:T(8,128)(2,1)}, u32[]{:S(2)}, u32[]{:S(2)}) collective-permute-start(bf16[1024,1024]{1,0:T(8,128)(2,1)} %slice.389), channel_id=1, source_target_pairs={{0,1},{1,0},{2,3},{3,2},{4,5},{5,4},{6,7},{7,6},{8,9},{9,8},{10,11... | collective-permute-start | bytes 6291464 | tf_op jit(solution)/shard_map/ppermute | solution.py:72
  478.2 28.1 %collective-permute-start.46 = (bf16[2304,256]{1,0:T(8,128)(2,1)S(1)}, bf16[2304,256]{1,0:T(8,128)(2,1)}, u32[]{:S(2)}, u32[]{:S(2)}) collective-permute-start(bf16[2304,256]{1,0:T(8,128)(2,1)S(1)} %broadcast_select_fusion.1.refs_0_), channel_id=1, source_target_pairs={{0,1},{1,0},{2,3},{3,2},{4,5},{5,4},{6,7},{7,6},{8,9},{9,8},{10,11... | collective-permute-start | bytes 3538952 | tf_op jit(solution)/shard_map/ppermute | solution.py:72
  478.4 27.9 %collective-permute-start.47 = (bf16[2304,256]{1,0:T(8,128)(2,1)S(1)}, bf16[2304,256]{1,0:T(8,128)(2,1)}, u32[]{:S(2)}, u32[]{:S(2)}) collective-permute-start(bf16[2304,256]{1,0:T(8,128)(2,1)S(1)} %broadcast_select_fusion.2.refs_1_), channel_id=1, source_target_pairs={{0,1},{1,0},{2,3},{3,2},{4,5},{5,4},{6,7},{7,6},{8,9},{9,8},{10,11... | collective-permute-start | bytes 3538952 | tf_op jit(solution)/shard_map/ppermute | solution.py:72
  497.1 9.3 %collective-permute-start.48 = (bf16[2304,256]{1,0:T(8,128)(2,1)S(1)}, bf16[2304,256]{1,0:T(8,128)(2,1)}, u32[]{:S(2)}, u32[]{:S(2)}) collective-permute-start(bf16[2304,256]{1,0:T(8,128)(2,1)S(1)} %broadcast_select_fusion.refs_2_), channel_id=1, source_target_pairs={{0,1},{1,0},{2,3},{3,2},{4,5},{5,4},{6,7},{7,6},{8,9},{9,8},{10,11... | collective-permute-start | bytes 3538952 | tf_op jit(solution)/shard_map/ppermute | solution.py:72
  498.4 24.2 %collective-permute-start.38 = (bf16[144,3072]{1,0:T(8,128)(2,1)}, bf16[144,3072]{1,0:T(8,128)(2,1)}, u32[]{:S(2)}, u32[]{:S(2)}) collective-permute-start(bf16[144,3072]{1,0:T(8,128)(2,1)} %add_convert_fusion.9), channel_id=1, source_target_pairs={{2,0},{3,1},{4,6},{5,7},{10,8},{11,9},{12,14},{13,15},{18,16},{19,... | collective-permute-start | bytes 2654216 | tf_op jit(solution)/shard_map/ppermute | solution.py:165
  (71 other events, 540.4 us)

commit v3 on v2

--- a/solution.py
+++ b/solution.py
@@ -121,7 +121,7 @@
                 sides.append(jnp.stack([part[mark] for mark in marks]))
         return sides
 
-    def total(self, sides, axis):
+    def total(self, sides, axis, split=False):
         _, rep = self.here()
         streams = []
         for stream, (order, _, _) in enumerate(block_orders(self.shard_bits)):
@@ -138,22 +138,31 @@
                     entry[2] = add_low(stay[:half], arrived[:half])
                 else:
                     entry[2] = add_low(stay, arrived)
-        value = jnp.concatenate([entry[2][0] for entry in streams], axis=axis)
+        values = [entry[2][0] for entry in streams]
+        if not split:
+            values = [jnp.concatenate(values, axis=axis)]
         if self.rep_bits != 3:
             for bit in range(1, self.rep_bits):
-                value = add_low(value, self.rep_swap(value, bit))
+                values = [add_low(value, self.rep_swap(value, bit)) for value in values]
         else:
-            came = self.rep_line(value, {0: 1, 3: 2})
-            token = yield [value]
-            value = add_low(value, hold([came], token)[0])
-            came = self.rep_line(value, {1: 2, 2: 1})
-            token = yield [value]
-            value = add_low(value, hold([came], token)[0])
-            came = self.rep_line(value, {1: 0, 2: 3})
-            token = yield [value]
+            for targets in ({0: 1, 3: 2}, {1: 2, 2: 1}):
+                came = [self.rep_line(value, targets) for value in values]
+                token = yield values
+                for number, arrived in enumerate(came):
+                    values[number] = add_low(values[number], hold([arrived], token)[0])
+                    token = values[number]
+            came = [self.rep_line(value, {1: 0, 2: 3}) for value in values]
+            token = yield values
+            if isinstance(token, tuple):
+                came = [hold([part], at)[0] for part, at in zip(came, token, strict=True)]
+            else:
+                came = hold(came, token)
             middle = ((rep >> 1) == 1) | ((rep >> 1) == 2)
-            value = jnp.where(middle, value, hold([came], token)[0])
-        yield value
+            values = [
+                jnp.where(middle, value, arrived)
+                for value, arrived in zip(values, came, strict=True)
+            ]
+        yield jnp.concatenate(values, axis=axis) if split else values[0]
 
     def rep_line(self, value, targets):
         pairs = []
@@ -285,7 +294,7 @@
         ),
         out_shape=[jax.ShapeDtypeStruct(shape, FULL) for shape in shapes],
         compiler_params=pltpu.CompilerParams(vmem_limit_bytes=56 * 1024 * 1024),
-        cost_estimate=pl.CostEstimate(flops=0, bytes_accessed=21_000_000, transcendentals=0),
+        cost_estimate=pl.CostEstimate(flops=0, bytes_accessed=1_000, transcendentals=0),
         name="unpack",
     )(core, *mine, *theirs)
 
@@ -309,7 +318,7 @@
 
 def line_up(ids, blocks, half):
     wide = blocks[0].shape[1]
-    where = pl.BlockSpec(memory_space=pl.ANY)
+    where = pl.BlockSpec(memory_space=pltpu.HBM)
     return pl.pallas_call(
         functools.partial(line_up_kernel, half=half),
         grid_spec=pltpu.PrefetchScalarGridSpec(
@@ -342,7 +351,7 @@
 
 def both_cores(core, mine, theirs):
     shards, half, wide = mine.shape
-    where = pl.BlockSpec(memory_space=pl.ANY)
+    where = pl.BlockSpec(memory_space=pltpu.HBM)
     out = pl.pallas_call(
         both_cores_kernel,
         grid_spec=pltpu.PrefetchScalarGridSpec(
@@ -389,7 +398,7 @@
 def sort_out(place, grads, gains):
     shards, extra, wide = gains.shape
     half = grads[0].shape[0] // (2 * shards)
-    where = pl.BlockSpec(memory_space=pl.ANY)
+    where = pl.BlockSpec(memory_space=pltpu.HBM)
     return pl.pallas_call(
         functools.partial(sort_out_kernel, half=half),
         grid_spec=pltpu.PrefetchScalarGridSpec(
@@ -400,7 +409,7 @@
             scratch_shapes=[pltpu.SemaphoreType.DMA],
         ),
         out_shape=[jax.ShapeDtypeStruct((shards, half + extra, wide), LOW)] * 2,
-        cost_estimate=pl.CostEstimate(flops=0, bytes_accessed=12_000_000, transcendentals=0),
+        cost_estimate=pl.CostEstimate(flops=0, bytes_accessed=1_000, transcendentals=0),
         compiler_params=pltpu.CompilerParams(vmem_limit_bytes=32 * 1024 * 1024),
         name="sort_out",
     )(place, *grads, gains)
@@ -684,7 +693,7 @@
     tall = pl.BlockSpec((tile, model), lambda i, ids: (i, 0))
     mine = pl.BlockSpec((tile, model), lambda i, ids: (jnp.minimum(i, half - 1), 0))
     other = pl.BlockSpec((tile, model), lambda i, ids: (jnp.maximum(i - half, 0), 0))
-    where = pl.BlockSpec(memory_space=pl.ANY)
+    where = pl.BlockSpec(memory_space=pltpu.HBM)
     sums = () if fresh else tuple(sums)
     side = jax.ShapeDtypeStruct((shards // 2, rows // 2, 256), LOW)
     total = jax.ShapeDtypeStruct((count, model), FULL)
@@ -884,10 +893,6 @@
     attn_blocks = links.gather(attn_part, attn_near, packed[0], cot_pair[1])
     (packed[0],) = hold([packed[0]], attn_blocks[1])
     nears = [links.near(packed[0])]
-    (line,) = hold([ids], nears[0])
-    attn_mine = line_up(line, attn_blocks, half)
-    attn_full = both_cores(core_line, attn_mine, links.core_swap(attn_mine))
-    qkv_full, out_full = attn_full[:, :packed_wide], attn_full[:, packed_wide:]
 
     positions = doc_positions(doc_ids).reshape(count)
     freqs = jnp.power(ROPE_BASE, -2.0 * jnp.arange(DH // 2, dtype=FULL) / DH)
@@ -902,6 +907,10 @@
     x_in = tokens.astype(FULL)
     inv_one = inverse_rms(x_in, 1)
     x_hat = x_in * inv_one
+    (line,) = hold([ids], nears[0], inv_one, cosine, sine, mask)
+    attn_mine = line_up(line, attn_blocks, half)
+    attn_full = both_cores(core_line, attn_mine, links.core_swap(attn_mine))
+    qkv_full, out_full = attn_full[:, :packed_wide], attn_full[:, packed_wide:]
 
     gain_rows = jnp.zeros((shards, whole_wide), LOW)
     for place, block in enumerate(attn_blocks):
@@ -962,8 +971,9 @@
 
     out_sum, ffn_back = sums
     first_sent = ffn_totals[0][0].send(stay_a)
-    (back_low,) = hold([ffn_back[count:].astype(LOW)], *first_sent, *sends)
-    back_other = links.core_swap(back_low)
+    (back_other,) = hold(
+        [links.core_swap(ffn_back[count:].astype(LOW))], *first_sent, *sends
+    )
     grad_ffn_in = ffn_back[:count] + back_other.astype(FULL)
     grad_gain_ffn = jnp.sum(grad_ffn_in * resid_hat, axis=0)
     grad_resid = cotangent.astype(FULL) + norm_back(grad_ffn_in * gain_ffn, resid_hat, inv_two, 1)
@@ -1024,7 +1034,7 @@
         gain_attn[None],
         grad_resid,
     )
-    advance(grad_key_w)
+    sent = advance(grad_key_w)
 
     gain_grads = jnp.concatenate(
         [
@@ -1039,29 +1049,35 @@
         gain_grads.astype(LOW), ((0, 0), (0, whole_wide - gain_grads.shape[1]))
     )[:, None]
     gain_rows = jnp.pad(gain_rows, ((0, 0), (0, GAIN_ROWS - 1), (0, 0)))
-    shard_line = jnp.stack([ids[shards], core])
+    (shard_line,) = hold([jnp.stack([ids[shards], core])], *sent)
     keep, give = sort_out(
         shard_line, [grad_query_w, grad_key_w, grad_value_w, grad_out_w], gain_rows
     )
     came = links.core_swap(give)
-    attn_flow = links.total(links.by_mark(add_low(keep, came)), 1)
+    attn_flow = links.total(links.by_mark(add_low(keep, came)), 1, True)
     flows = flows + [attn_flow]
     done = done + [None]
     token = next(attn_flow)[0]
-    while None in done[:PIECES]:
+    while None in done[: PIECES - 1]:
         advance(token)
         token = None
-    advance()
-    (out_low,) = hold([out_sum[count:].astype(LOW)], done[1])
+    (out_low,) = hold([out_sum[count:].astype(LOW)], done[0])
     out_other = links.core_swap(out_low)
     result = (resid + out_sum[:count] + out_other.astype(FULL)).astype(LOW)
+    while done[PIECES - 1] is None:
+        token = None
+        if links.paired and links.rep_bits == 3:
+            attn_flow.send(None)
+            attn_flow.send(None)
+            token = result
+        done[PIECES - 1] = flows[PIECES - 1].send(token)
     ffn_mine = done[:PIECES]
     ffn_theirs = [links.core_swap(part) for part in ffn_mine]
     grad_gate_w, grad_up_w, grad_down_w = unpack(
         core_line, ffn_mine, ffn_theirs, (w_gate.shape, w_up.shape, w_down.shape), shards
     )
     while None in done:
-        advance(grad_down_w)
+        advance((result, grad_down_w))
     gain_sum = done[-1][half].astype(FULL)
     attn_sum = owned(done[-1][:half])
     ffn_mine = done[:PIECES]

time: 535 us -> 533 us (level)
  local copies, waits for them, and re-layouts: 45.4 us -> 35.2 us
  starting transfers between devices: 57.1 us -> 65.4 us
    ppermute x38, waiting for transfers between devices: 74.2 us -> 64.7 us  [move(): return lax.ppermute(value, AXES, pairs)]
    unnamed x142 -> x138, local copies, waits for them, and re-layouts: 26.6 us -> 18.3 us
    ppermute x12 -> x15, waiting for transfers between devices: 55.9 us -> 63.8 us  [rep_line(): return lax.ppermute(value, AXES, pairs)]
    ppermute x12 -> x15, starting transfers between devices: 23.6 us -> 30.8 us  [rep_line(): return lax.ppermute(value, AXES, pairs)]
    squeeze x7, other arithmetic: 6.49 us -> 12.3 us  [total(): values = [entry[2][0] for entry in streams]]
    convert_element_type x16 -> x18, other arithmetic: 17.2 us -> 22.1 us  [add_low(): return (first.astype(FULL) + second.astype(FULL)).astype(LOW)]
  transfers between devices with their start and end apart: 50 -> 53, of which waited for: 16 -> 15; matrix products, arithmetic and copies ran while one was open for 14% -> 14% of each run, Pallas kernels for 36% -> 41%
where the time goes in v3:
time: 533 us; the launch traced here: 528 us
  Pallas kernels  219 us (41%)
  waiting for transfers between devices  129 us (24%)
  other arithmetic  68 us (13%)
  starting transfers between devices  65.4 us (12%)
  local copies, waits for them, and re-layouts  35.2 us (7%)
  matrix products  9.81 us (2%)
    pallas_call x3, Pallas kernels, ffn_piece(): pl.pallas_call(functools.partial(ffn_kernel, shards=shards, fresh=fresh),...  122 us
    ppermute x38, waiting for transfers between devices, move(): return lax.ppermute(value, AXES, pairs)  64.7 us
    ppermute x15, waiting for transfers between devices, rep_line(): return lax.ppermute(value, AXES, pairs)  63.8 us
    ppermute x38, starting transfers between devices, move(): return lax.ppermute(value, AXES, pairs)  34.6 us
    ppermute x15, starting transfers between devices, rep_line(): return lax.ppermute(value, AXES, pairs)  30.8 us
    pallas_call x1, Pallas kernels, attend_back(): pl.pallas_call(attend_back_kernel, grid=(HK,), in_specs=[two, one, one, t...  30.8 us
    pallas_call x1, Pallas kernels, attend_grads(): pl.pallas_call(attend_grads_kernel, grid=(steps,), in_specs=[rows(wide),...  27 us
    convert_element_type x18, other arithmetic, add_low(): return (first.astype(FULL) + second.astype(FULL)).astype(LOW)  22.1 us
  transfers between devices with their start and end apart: 53, of which 15 were waited for; matrix products, arithmetic and copies ran while one was open for 14% of the time, Pallas kernels for 41%

profile of v3, /device:TPU:0, one launch (start us, length us, event | category | flops | bytes accessed | tf_op | source)
XLA Modules:
  0.0 528.1 jit_solution(13863266631868068100)
XLA Ops:
  4.3 2.6 collective-permute-start
  6.9 4.1 pack.1
  13.1 14.0 %collective-permute-done.refs_1_ = bf16[144,3072]{1,0:T(8,128)(2,1)S(1)} collective-permute-done((bf16[144,3072]{1,0:T(8,128)(2,1)S(1)}, bf16[144,3072]{1,0:T(8,128)(2,1)S(1)}, u32[]{:S(2)}, u32[]{:S(2)}) %collective-permute-start) | collective-permute-done | bytes 884768 | tf_op jit(solution)/shard_map/ppermute | solution.py:72
  27.1 1.8 collective-permute-start.2
  31.9 2.1 fusion
  34.1 1.8 fusion.6.mask_ref
  35.9 19.3 %collective-permute-done.2.refs_1_ = bf16[2304,256]{1,0:T(8,128)(2,1)} collective-permute-done((bf16[2304,256]{1,0:T(8,128)(2,1)}, bf16[2304,256]{1,0:T(8,128)(2,1)}, u32[]{:S(2)}, u32[]{:S(2)}) %collective-permute-start.2) | collective-permute-done | bytes 1179680 | tf_op jit(solution)/shard_map/ppermute | solution.py:72
  65.9 2.2 fusion.2.in_ref
  72.9 2.1 both_cores.1
  75.0 4.8 fusion.3.q_ref.k_ref
  87.7 19.8 %attend.1 = (bf16[1024,1024]{1,0:T(8,128)(2,1)S(1)}, f32[8,2,1024]{2,1,0:T(2,128)S(1)}) custom-call(bf16[1024,1024]{1,0:T(8,128)(2,1)S(1)} %bitcast.64, bf16[512,1024]{1,0:T(8,128)(2,1)S(1)} %bitcast.66, bf16[512,1024]{1,0:T(8,128)(2,1)S(1)} %slice.387.v_ref, bf16[1024,1024]{1,0:T(8,128)(2,1)S(1)} %copy-done.4), custom_call_target="tpu_custom_call" | custom-call | flops 16000000000 | bytes 8000000 | tf_op jit(solution)/shard_map/attend/pallas_call | solution.py:750
  109.1 2.6 multiply_reduce_fusion.2
  111.8 2.0 multiply_convert_fusion.ffn_ref
  118.9 40.0 %ffn_piece.3 = (f32[2048,1024]{1,0:T(8,128)}, f32[2048,1024]{1,0:T(8,128)}, bf16[2,1152,256]{2,1,0:T(8,128)(2,1)}, bf16[2,1152,256]{2,1,0:T(8,128)(2,1)}, bf16[2...) custom-call(s32[5]{0:T(128)} %copy-done.19, bf16[1024,1024]{1,0:T(8,128)(2,1)} %multiply_convert_fusion.ffn_ref, ...), custom_call_target="tpu_custom_call" | custom-call | flops 28991029248 | bytes 40000000 | tf_op jit(solution)/shard_map/ffn_piece/pallas_call | solution.py:701
  164.1 41.4 %ffn_piece.4 = (f32[2048,1024]{1,0:T(8,128)}, f32[2048,1024]{1,0:T(8,128)}, bf16[2,1152,256]{2,1,0:T(8,128)(2,1)}, bf16[2,1152,256]{2,1,0:T(8,128)(2,1)}, bf16[2...) custom-call(s32[5]{0:T(128)} %copy-done.19, ...), custom_call_target="tpu_custom_call", output_to_operand_aliasing={{0}: (9, {}), {1}: (10, {})} | custom-call | flops 28991029248 | bytes 40000000 | tf_op jit(solution)/shard_map/ffn_piece/pallas_call | solution.py:701
  207.6 7.5 %collective-permute-done.11 = bf16[2,1152,256]{2,1,0:T(8,128)(2,1)} collective-permute-done((bf16[2,1152,256]{2,1,0:T(8,128)(2,1)}, bf16[2,1152,256]{2,1,0:T(8,128)(2,1)}, u32[]{:S(2)}, u32[]{:S(2)}) %collective-permute-start.11) | collective-permute-done | bytes 1179680 | tf_op jit(solution)/shard_map/ppermute | solution.py:72
  215.1 2.2 add_convert_fusion.25
  218.8 2.0 add_convert_fusion.26
  222.4 40.9 %ffn_piece.5 = (f32[2048,1024]{1,0:T(8,128)}, f32[2048,1024]{1,0:T(8,128)}, bf16[2,1152,256]{2,1,0:T(8,128)(2,1)}, bf16[2,1152,256]{2,1,0:T(8,128)(2,1)}, bf16[2...) custom-call(s32[5]{0:T(128)} %copy-done.19, ...), custom_call_target="tpu_custom_call", output_to_operand_aliasing={{0}: (9, {}), {1}: (10, {})} | custom-call | flops 28991029248 | bytes 40000000 | tf_op jit(solution)/shard_map/ffn_piece/pallas_call | solution.py:701
  263.3 2.7 slice.385
  266.0 3.0 add_convert_fusion.19
  269.5 2.1 add_convert_fusion.20
  279.7 3.1 collective-permute-start.19
  282.8 2.0 multiply_reduce_fusion
  284.8 2.9 fusion.37
  287.8 2.4 convolution_convert_fusion.do_ref
  291.1 30.8 %attend_back.1 = (f32[1024,1024]{1,0:T(8,128)}, f32[512,1024]{1,0:T(8,128)S(1)}, bf16[512,1024]{1,0:T(8,128)(2,1)S(1)}) custom-call(bf16[1024,1024]{1,0:T(8,128)(2,1)S(1)} %bitcast.65, bf16[512,1024]{1,0:T(8,128)(2,1)S(1)} %bitcast.67, bf16[512,1024]{1,0:T(8,128)(2,1)S(1)} %slice.387.v_ref, bf16[1024,1024]{1,0:T(8,128)(2,1)S(1)} %copy-done.24, ...), custom_call_target="tpu_custom_call" | custom-call | flops 40000000000 | bytes 16000000 | tf_op jit(solution)/shard_map/attend_back/pallas_call | solution.py:818
  322.9 2.6 fusion.14
  329.9 2.1 add_convert_fusion.17
  335.7 27.0 %attend_grads.1 = (bf16[1024,1024]{1,0:T(8,128)(2,1)}, bf16[1024,512]{1,0:T(8,128)(2,1)}, bf16[1024,512]{1,0:T(8,128)(2,1)}, bf16[1024,1024]{1,0:T(8,128)(2,1)},...) custom-call(f32[1024,1024]{1,0:T(8,128)} %get-tuple-element.150.dq_ref, ...), custom_call_target="tpu_custom_call" | custom-call | flops 40000000000 | bytes 40000000 | tf_op jit(solution)/shard_map/attend_grads/pallas_call | solution.py:524
  373.4 2.8 add_convert_fusion.6
  376.2 2.1 sort_out.1
  378.4 6.2 %collective-permute-done.32 = bf16[4,144,3072]{2,1,0:T(8,128)(2,1)S(1)} collective-permute-done((bf16[4,144,3072]{2,1,0:T(8,128)(2,1)S(1)}, bf16[4,144,3072]{2,1,0:T(8,128)(2,1)S(1)}, u32[]{:S(2)}, u32[]{:S(2)}) %collective-permute-start.32) | collective-permute-done | bytes 3538976 | tf_op jit(solution)/shard_map/ppermute | solution.py:72
  390.0 4.5 collective-permute-start.46
  394.5 2.7 slice.386
  399.4 10.6 %collective-permute-done.33 = bf16[2,144,1536]{2,1,0:T(8,128)(2,1)} collective-permute-done((bf16[2,144,1536]{2,1,0:T(8,128)(2,1)}, bf16[2,144,1536]{2,1,0:T(8,128)(2,1)}, u32[]{:S(2)}, u32[]{:S(2)}) %collective-permute-start.33) | collective-permute-done | bytes 884768 | tf_op jit(solution)/shard_map/ppermute | solution.py:72
  413.1 5.6 %collective-permute-done.46 = bf16[2304,256]{1,0:T(8,128)(2,1)} collective-permute-done((bf16[2304,256]{1,0:T(8,128)(2,1)}, bf16[2304,256]{1,0:T(8,128)(2,1)}, u32[]{:S(2)}, u32[]{:S(2)}) %collective-permute-start.46) | collective-permute-done | bytes 1179680 | tf_op jit(solution)/shard_map/ppermute | solution.py:174
  421.7 4.7 collective-permute-done.28
  427.2 4.8 collective-permute-done.37
  433.4 6.0 %collective-permute-start.38 = (bf16[144,1536]{1,0:T(8,128)(2,1)S(1)}, bf16[144,1536]{1,0:T(8,128)(2,1)S(1)}, u32[]{:S(2)}, u32[]{:S(2)}) collective-permute-start(bf16[144,1536]{1,0:T(8,128)(2,1)S(1)} %get-tuple-element.192), channel_id=1, source_target_pairs={{0,2},{1,3},{6,4},{7,5},{8,10},{9,11},{14,12},{15,13},{16,18},{17,... | collective-permute-start | bytes 1327112 | tf_op jit(solution)/shard_map/ppermute | solution.py:174
  441.1 5.6 %collective-permute-done.38 = bf16[144,1536]{1,0:T(8,128)(2,1)S(1)} collective-permute-done((bf16[144,1536]{1,0:T(8,128)(2,1)S(1)}, bf16[144,1536]{1,0:T(8,128)(2,1)S(1)}, u32[]{:S(2)}, u32[]{:S(2)}) %collective-permute-start.38) | collective-permute-done | bytes 442400 | tf_op jit(solution)/shard_map/ppermute | solution.py:174
  446.7 4.4 collective-permute-start.41
  451.3 6.2 %collective-permute-done.41 = bf16[144,1536]{1,0:T(8,128)(2,1)S(1)} collective-permute-done((bf16[144,1536]{1,0:T(8,128)(2,1)S(1)}, bf16[144,1536]{1,0:T(8,128)(2,1)S(1)}, u32[]{:S(2)}, u32[]{:S(2)}) %collective-permute-start.41) | collective-permute-done | bytes 442400 | tf_op jit(solution)/shard_map/ppermute | solution.py:174
  459.3 7.7 %collective-permute-done.45 = bf16[2304,256]{1,0:T(8,128)(2,1)S(1)} collective-permute-done((bf16[2304,256]{1,0:T(8,128)(2,1)S(1)}, bf16[2304,256]{1,0:T(8,128)(2,1)S(1)}, u32[]{:S(2)}, u32[]{:S(2)}) %collective-permute-start.45) | collective-permute-done | bytes 1179680 | tf_op jit(solution)/shard_map/ppermute | solution.py:174
  468.9 2.6 add_convert_fusion.1
  471.5 21.8 %collective-permute-done.48 = bf16[2304,256]{1,0:T(8,128)(2,1)S(1)} collective-permute-done((bf16[2304,256]{1,0:T(8,128)(2,1)S(1)}, bf16[2304,256]{1,0:T(8,128)(2,1)S(1)}, u32[]{:S(2)}, u32[]{:S(2)}) %collective-permute-start.48) | collective-permute-done | bytes 1179680 | tf_op jit(solution)/shard_map/ppermute | solution.py:174
  496.4 12.1 %collective-permute-done.40 = bf16[144,1536]{1,0:T(8,128)(2,1)S(1)} collective-permute-done((bf16[144,1536]{1,0:T(8,128)(2,1)S(1)}, bf16[144,1536]{1,0:T(8,128)(2,1)S(1)}, u32[]{:S(2)}, u32[]{:S(2)}) %collective-permute-start.40) | collective-permute-done | bytes 442400 | tf_op jit(solution)/shard_map/ppermute | solution.py:174
  511.8 9.9 %unpack.1 = (f32[256,4608]{1,0:T(8,128)}, f32[256,4608]{1,0:T(8,128)}, f32[1152,1024]{1,0:T(8,128)}) custom-call(s32[1]{0:T(128)} %bitcast.core_ref, bf16[2304,256]{1,0:T(8,128)(2,1)} %copy-done.38, bf16[2304,256]{1,0:T(8,128)(2,1)} %copy-done.40, bf16[2304,256]{1,0:T(8,128)(2,1)} %copy-done.41, bf16[2304,256]{1,0:T(8,128)(2,1)} %copy-done.45, ...), custom_call_target="tpu_custom_call" | custom-call | bytes 1000 | tf_op jit(solution)/shard_map/unpack/pallas_call | solution.py:287
  (318 shorter events, 111.6 us)
Async XLA Ops:
  3.8 23.3 %collective-permute-start.1 = (bf16[1024,1024]{1,0:T(8,128)(2,1)}, bf16[1024,1024]{1,0:T(8,128)(2,1)S(1)}, u32[]{:S(2)}, u32[]{:S(2)}) collective-permute-start(bf16[1024,1024]{1,0:T(8,128)(2,1)} %cot_ref.5), channel_id=1, source_target_pairs={{0,1},{1,0},{2,3},{3,2},{4,5},{5,4},{6,7},{7,6},{8,9},{9,8},{10,11... | collective-permute-start | bytes 6291464 | tf_op jit(solution)/shard_map/ppermute | solution.py:72
  4.3 22.8 %collective-permute-start = (bf16[144,3072]{1,0:T(8,128)(2,1)S(1)}, bf16[144,3072]{1,0:T(8,128)(2,1)S(1)}, u32[]{:S(2)}, u32[]{:S(2)}) collective-permute-start(bf16[144,3072]{1,0:T(8,128)(2,1)S(1)} %fusion.10.refs_0_), channel_id=1, source_target_pairs={{0,8},{1,9},{2,18},{3,19},{4,12},{5,13},{6,22},{7,23},{8,0},{9,1},... | collective-permute-start | bytes 2654216 | tf_op jit(solution)/shard_map/ppermute | solution.py:72
  27.1 28.1 %collective-permute-start.2 = (bf16[2304,256]{1,0:T(8,128)(2,1)}, bf16[2304,256]{1,0:T(8,128)(2,1)}, u32[]{:S(2)}, u32[]{:S(2)}) collective-permute-start(bf16[2304,256]{1,0:T(8,128)(2,1)} %get-tuple-element.105.refs_0_), channel_id=1, source_target_pairs={{0,8},{1,9},{2,18},{3,19},{4,12},{5,13},{6,22},{7,23},{8,0},{9,1},... | collective-permute-start | bytes 3538952 | tf_op jit(solution)/shard_map/ppermute | solution.py:72
  28.9 26.3 %collective-permute-start.3 = (bf16[144,3072]{1,0:T(8,128)(2,1)S(1)}, bf16[144,3072]{1,0:T(8,128)(2,1)S(1)}, u32[]{:S(2)}, u32[]{:S(2)}) collective-permute-start(bf16[144,3072]{1,0:T(8,128)(2,1)S(1)} %collective-permute-done.refs_1_), channel_id=1, source_target_pairs={{0,2},{1,3},{2,0},{3,1},{4,6},{5,7},{6,4},{7,5},{8,10},{9,11},{10,... | collective-permute-start | bytes 2654216 | tf_op jit(solution)/shard_map/ppermute | solution.py:72
  30.5 25.6 %collective-permute-start.4 = (bf16[144,3072]{1,0:T(8,128)(2,1)S(1)}, bf16[144,3072]{1,0:T(8,128)(2,1)S(1)}, u32[]{:S(2)}, u32[]{:S(2)}) collective-permute-start(bf16[144,3072]{1,0:T(8,128)(2,1)S(1)} %collective-permute-done.refs_1_), channel_id=1, source_target_pairs={{0,16},{1,17},{2,10},{3,11},{4,20},{5,21},{6,14},{7,15},{8,24},{9,... | collective-permute-start | bytes 2654216 | tf_op jit(solution)/shard_map/ppermute | solution.py:72
  61.3 11.6 %collective-permute-start.5 = (bf16[4,128,3072]{2,1,0:T(8,128)(2,1)S(1)}, bf16[4,128,3072]{2,1,0:T(8,128)(2,1)}, u32[]{:S(2)}, u32[]{:S(2)}) collective-permute-start(bf16[4,128,3072]{2,1,0:T(8,128)(2,1)S(1)} %line_up.1.mine), channel_id=1, source_target_pairs={{0,1},{1,0},{2,3},{3,2},{4,5},{5,4},{6,7},{7,6},{8,9},{9,8},{10,11... | collective-permute-start | bytes 9437192 | tf_op jit(solution)/shard_map/ppermute | solution.py:72
  68.2 39.4 %collective-permute-start.7 = (bf16[2304,256]{1,0:T(8,128)(2,1)}, bf16[2304,256]{1,0:T(8,128)(2,1)S(1)}, u32[]{:S(2)}, u32[]{:S(2)}) collective-permute-start(bf16[2304,256]{1,0:T(8,128)(2,1)} %collective-permute-done.2.refs_1_), channel_id=1, source_target_pairs={{0,2},{1,3},{2,0},{3,1},{4,6},{5,7},{6,4},{7,5},{8,10},{9,11},{10,... | collective-permute-start | bytes 3538952 | tf_op jit(solution)/shard_map/ppermute | solution.py:72
  69.9 37.7 %collective-permute-start.8 = (bf16[2304,256]{1,0:T(8,128)(2,1)}, bf16[2304,256]{1,0:T(8,128)(2,1)S(1)}, u32[]{:S(2)}, u32[]{:S(2)}) collective-permute-start(bf16[2304,256]{1,0:T(8,128)(2,1)} %collective-permute-done.2.refs_1_), channel_id=1, source_target_pairs={{0,16},{1,17},{2,10},{3,11},{4,20},{5,21},{6,14},{7,15},{8,24},{9,... | collective-permute-start | bytes 3538952 | tf_op jit(solution)/shard_map/ppermute | solution.py:72
  71.4 36.2 %collective-permute-start.6 = (bf16[2304,256]{1,0:T(8,128)(2,1)S(1)}, bf16[2304,256]{1,0:T(8,128)(2,1)S(1)}, u32[]{:S(2)}, u32[]{:S(2)}) collective-permute-start(bf16[2304,256]{1,0:T(8,128)(2,1)S(1)} %copy-done.22), channel_id=1, source_target_pairs={{0,8},{1,9},{2,18},{3,19},{4,12},{5,13},{6,22},{7,23},{8,0},{9,1},... | collective-permute-start | bytes 3538952 | tf_op jit(solution)/shard_map/ppermute | solution.py:72
  117.5 46.2 %collective-permute-start.12 = (bf16[2304,256]{1,0:T(8,128)(2,1)}, bf16[2304,256]{1,0:T(8,128)(2,1)}, u32[]{:S(2)}, u32[]{:S(2)}) collective-permute-start(bf16[2304,256]{1,0:T(8,128)(2,1)} %copy-done.60), channel_id=1, source_target_pairs={{0,2},{1,3},{2,0},{3,1},{4,6},{5,7},{6,4},{7,5},{8,10},{9,11},{10,... | collective-permute-start | bytes 3538952 | tf_op jit(solution)/shard_map/ppermute | solution.py:72
  117.9 46.2 %collective-permute-start.13 = (bf16[2304,256]{1,0:T(8,128)(2,1)}, bf16[2304,256]{1,0:T(8,128)(2,1)}, u32[]{:S(2)}, u32[]{:S(2)}) collective-permute-start(bf16[2304,256]{1,0:T(8,128)(2,1)} %copy-done.60), channel_id=1, source_target_pairs={{0,16},{1,17},{2,10},{3,11},{4,20},{5,21},{6,14},{7,15},{8,24},{9,... | collective-permute-start | bytes 3538952 | tf_op jit(solution)/shard_map/ppermute | solution.py:72
  118.4 40.4 %collective-permute-start.14 = (bf16[2304,256]{1,0:T(8,128)(2,1)}, bf16[2304,256]{1,0:T(8,128)(2,1)}, u32[]{:S(2)}, u32[]{:S(2)}) collective-permute-start(bf16[2304,256]{1,0:T(8,128)(2,1)} %copy-done.20), channel_id=1, source_target_pairs={{0,8},{1,9},{2,18},{3,19},{4,12},{5,13},{6,22},{7,23},{8,0},{9,1},... | collective-permute-start | bytes 3538952 | tf_op jit(solution)/shard_map/ppermute | solution.py:72
  158.9 62.0 %collective-permute-start.15 = (bf16[2304,256]{1,0:T(8,128)(2,1)}, bf16[2304,256]{1,0:T(8,128)(2,1)}, u32[]{:S(2)}, u32[]{:S(2)}) collective-permute-start(bf16[2304,256]{1,0:T(8,128)(2,1)} %collective-permute-done.14.refs_1_), channel_id=1, source_target_pairs={{0,2},{1,3},{2,0},{3,1},{4,6},{5,7},{6,4},{7,5},{8,10},{9,11},{10,... | collective-permute-start | bytes 3538952 | tf_op jit(solution)/shard_map/ppermute | solution.py:72
  160.6 61.8 %collective-permute-start.16 = (bf16[2304,256]{1,0:T(8,128)(2,1)}, bf16[2304,256]{1,0:T(8,128)(2,1)}, u32[]{:S(2)}, u32[]{:S(2)}) collective-permute-start(bf16[2304,256]{1,0:T(8,128)(2,1)} %collective-permute-done.14.refs_1_), channel_id=1, source_target_pairs={{0,16},{1,17},{2,10},{3,11},{4,20},{5,21},{6,14},{7,15},{8,24},{9,... | collective-permute-start | bytes 3538952 | tf_op jit(solution)/shard_map/ppermute | solution.py:72
  162.1 44.0 %collective-permute-start.10 = (bf16[2,1152,256]{2,1,0:T(8,128)(2,1)}, bf16[2,1152,256]{2,1,0:T(8,128)(2,1)}, u32[]{:S(2)}, u32[]{:S(2)}) collective-permute-start(bf16[2,1152,256]{2,1,0:T(8,128)(2,1)} %get-tuple-element.113), channel_id=1, source_target_pairs={{0,8},{1,9},{2,10},{3,11},{4,12},{5,13},{6,14},{7,15},{8,0},{9,1},... | collective-permute-start | bytes 3538952 | tf_op jit(solution)/shard_map/ppermute | solution.py:72
  163.6 51.5 %collective-permute-start.11 = (bf16[2,1152,256]{2,1,0:T(8,128)(2,1)}, bf16[2,1152,256]{2,1,0:T(8,128)(2,1)}, u32[]{:S(2)}, u32[]{:S(2)}) collective-permute-start(bf16[2,1152,256]{2,1,0:T(8,128)(2,1)} %get-tuple-element.114), channel_id=1, source_target_pairs={{0,16},{1,17},{2,18},{3,19},{4,20},{5,21},{6,22},{7,23},{8,24},{9,... | collective-permute-start | bytes 3538952 | tf_op jit(solution)/shard_map/ppermute | solution.py:72
  205.5 57.7 %collective-permute-start.21 = (bf16[2,1152,256]{2,1,0:T(8,128)(2,1)}, bf16[2,1152,256]{2,1,0:T(8,128)(2,1)}, u32[]{:S(2)}, u32[]{:S(2)}) collective-permute-start(bf16[2,1152,256]{2,1,0:T(8,128)(2,1)} %get-tuple-element.132), channel_id=1, source_target_pairs={{0,8},{1,9},{2,10},{3,11},{4,12},{5,13},{6,14},{7,15},{8,0},{9,1},... | collective-permute-start | bytes 3538952 | tf_op jit(solution)/shard_map/ppermute | solution.py:72
  206.1 57.1 %collective-permute-start.22 = (bf16[2,1152,256]{2,1,0:T(8,128)(2,1)}, bf16[2,1152,256]{2,1,0:T(8,128)(2,1)}, u32[]{:S(2)}, u32[]{:S(2)}) collective-permute-start(bf16[2,1152,256]{2,1,0:T(8,128)(2,1)} %get-tuple-element.133), channel_id=1, source_target_pairs={{0,16},{1,17},{2,18},{3,19},{4,20},{5,21},{6,22},{7,23},{8,24},{9,... | collective-permute-start | bytes 3538952 | tf_op jit(solution)/shard_map/ppermute | solution.py:72
  217.3 54.8 %collective-permute-start.18 = (bf16[1,1152,256]{2,1,0:T(8,128)(2,1)}, bf16[1,1152,256]{2,1,0:T(8,128)(2,1)}, u32[]{:S(2)}, u32[]{:S(2)}) collective-permute-start(bf16[1,1152,256]{2,1,0:T(8,128)(2,1)} %add_convert_fusion.25), channel_id=1, source_target_pairs={{0,8},{1,9},{2,10},{3,11},{4,12},{5,13},{6,14},{7,15},{8,0},{9,1},... | collective-permute-start | bytes 1769480 | tf_op jit(solution)/shard_map/ppermute | solution.py:72
  220.8 52.8 %collective-permute-start.17 = (bf16[1,1152,256]{2,1,0:T(8,128)(2,1)}, bf16[1,1152,256]{2,1,0:T(8,128)(2,1)}, u32[]{:S(2)}, u32[]{:S(2)}) collective-permute-start(bf16[1,1152,256]{2,1,0:T(8,128)(2,1)} %add_convert_fusion.26), channel_id=1, source_target_pairs={{0,16},{1,17},{2,18},{3,19},{4,20},{5,21},{6,22},{7,23},{8,24},{9,... | collective-permute-start | bytes 1769480 | tf_op jit(solution)/shard_map/ppermute | solution.py:72
  266.0 13.7 %collective-permute-start.20 = (bf16[1024,1024]{1,0:T(8,128)(2,1)S(1)}, bf16[1024,1024]{1,0:T(8,128)(2,1)S(1)}, u32[]{:S(2)}, u32[]{:S(2)}) collective-permute-start(bf16[1024,1024]{1,0:T(8,128)(2,1)S(1)} %slice.385), channel_id=1, source_target_pairs={{0,1},{1,0},{2,3},{3,2},{4,5},{5,4},{6,7},{7,6},{8,9},{9,8},{10,11... | collective-permute-start | bytes 6291464 | tf_op jit(solution)/shard_map/ppermute | solution.py:72
  269.0 53.8 %collective-permute-start.27 = (bf16[1,1152,256]{2,1,0:T(8,128)(2,1)}, bf16[1,1152,256]{2,1,0:T(8,128)(2,1)}, u32[]{:S(2)}, u32[]{:S(2)}) collective-permute-start(bf16[1,1152,256]{2,1,0:T(8,128)(2,1)} %add_convert_fusion.19), channel_id=1, source_target_pairs={{0,8},{1,9},{2,10},{3,11},{4,12},{5,13},{6,14},{7,15},{8,0},{9,1},... | collective-permute-start | bytes 1769480 | tf_op jit(solution)/shard_map/ppermute | solution.py:72
  271.6 51.2 %collective-permute-start.26 = (bf16[1,1152,256]{2,1,0:T(8,128)(2,1)}, bf16[1,1152,256]{2,1,0:T(8,128)(2,1)}, u32[]{:S(2)}, u32[]{:S(2)}) collective-permute-start(bf16[1,1152,256]{2,1,0:T(8,128)(2,1)} %add_convert_fusion.20), channel_id=1, source_target_pairs={{0,16},{1,17},{2,18},{3,19},{4,20},{5,21},{6,22},{7,23},{8,24},{9,... | collective-permute-start | bytes 1769480 | tf_op jit(solution)/shard_map/ppermute | solution.py:72
  272.1 49.7 %collective-permute-start.24 = (bf16[2,1152,256]{2,1,0:T(8,128)(2,1)}, bf16[2,1152,256]{2,1,0:T(8,128)(2,1)S(1)}, u32[]{:S(2)}, u32[]{:S(2)}) collective-permute-start(bf16[2,1152,256]{2,1,0:T(8,128)(2,1)} %get-tuple-element.143), channel_id=1, source_target_pairs={{0,8},{1,9},{2,10},{3,11},{4,12},{5,13},{6,14},{7,15},{8,0},{9,1},... | collective-permute-start | bytes 3538952 | tf_op jit(solution)/shard_map/ppermute | solution.py:72
  273.6 48.3 %collective-permute-start.25 = (bf16[2,1152,256]{2,1,0:T(8,128)(2,1)}, bf16[2,1152,256]{2,1,0:T(8,128)(2,1)}, u32[]{:S(2)}, u32[]{:S(2)}) collective-permute-start(bf16[2,1152,256]{2,1,0:T(8,128)(2,1)} %get-tuple-element.144), channel_id=1, source_target_pairs={{0,16},{1,17},{2,18},{3,19},{4,20},{5,21},{6,22},{7,23},{8,24},{9,... | collective-permute-start | bytes 3538952 | tf_op jit(solution)/shard_map/ppermute | solution.py:72
  279.7 47.3 %collective-permute-start.19 = (bf16[2304,256]{1,0:T(8,128)(2,1)}, bf16[2304,256]{1,0:T(8,128)(2,1)S(1)}, u32[]{:S(2)}, u32[]{:S(2)}) collective-permute-start(bf16[2304,256]{1,0:T(8,128)(2,1)} %pad_maximum_fusion), channel_id=1, source_target_pairs={{0,2},{1,3},{6,4},{7,5},{8,10},{9,11},{14,12},{15,13},{16,18},{17,... | collective-permute-start | bytes 3538952 | tf_op jit(solution)/shard_map/ppermute | solution.py:174
  328.5 43.6 %collective-permute-start.31 = (bf16[2304,256]{1,0:T(8,128)(2,1)}, bf16[2304,256]{1,0:T(8,128)(2,1)S(1)}, u32[]{:S(2)}, u32[]{:S(2)}) collective-permute-start(bf16[2304,256]{1,0:T(8,128)(2,1)} %pad_maximum_fusion.1), channel_id=1, source_target_pairs={{0,2},{1,3},{6,4},{7,5},{8,10},{9,11},{14,12},{15,13},{16,18},{17,... | collective-permute-start | bytes 3538952 | tf_op jit(solution)/shard_map/ppermute | solution.py:174
  331.9 35.6 %collective-permute-start.30 = (bf16[1,1152,256]{2,1,0:T(8,128)(2,1)}, bf16[1,1152,256]{2,1,0:T(8,128)(2,1)}, u32[]{:S(2)}, u32[]{:S(2)}) collective-permute-start(bf16[1,1152,256]{2,1,0:T(8,128)(2,1)} %add_convert_fusion.17), channel_id=1, source_target_pairs={{0,8},{1,9},{2,10},{3,11},{4,12},{5,13},{6,14},{7,15},{8,0},{9,1},... | collective-permute-start | bytes 1769480 | tf_op jit(solution)/shard_map/ppermute | solution.py:72
  332.3 35.2 %collective-permute-start.29 = (bf16[1,1152,256]{2,1,0:T(8,128)(2,1)}, bf16[1,1152,256]{2,1,0:T(8,128)(2,1)}, u32[]{:S(2)}, u32[]{:S(2)}) collective-permute-start(bf16[1,1152,256]{2,1,0:T(8,128)(2,1)} %add_convert_fusion.18), channel_id=1, source_target_pairs={{0,16},{1,17},{2,18},{3,19},{4,20},{5,21},{6,22},{7,23},{8,24},{9,... | collective-permute-start | bytes 1769480 | tf_op jit(solution)/shard_map/ppermute | solution.py:72
  334.0 39.5 %collective-permute-start.23 = (bf16[2304,256]{1,0:T(8,128)(2,1)S(1)}, bf16[2304,256]{1,0:T(8,128)(2,1)}, u32[]{:S(2)}, u32[]{:S(2)}) collective-permute-start(bf16[2304,256]{1,0:T(8,128)(2,1)S(1)} %add_convert_fusion.7), channel_id=1, source_target_pairs={{2,4},{3,5},{4,2},{5,3},{10,12},{11,13},{12,10},{13,11},{18,20},{1... | collective-permute-start | bytes 3538952 | tf_op jit(solution)/shard_map/ppermute | solution.py:174
  388.0 22.0 %collective-permute-start.33 = (bf16[2,144,1536]{2,1,0:T(8,128)(2,1)}, bf16[2,144,1536]{2,1,0:T(8,128)(2,1)}, u32[]{:S(2)}, u32[]{:S(2)}) collective-permute-start(bf16[2,144,1536]{2,1,0:T(8,128)(2,1)} %pad_maximum_fusion.4), channel_id=1, source_target_pairs={{0,8},{1,9},{2,10},{3,11},{4,12},{5,13},{6,14},{7,15},{8,0},{9,1},... | collective-permute-start | bytes 2654216 | tf_op jit(solution)/shard_map/ppermute | solution.py:72
  389.5 21.7 %collective-permute-start.34 = (bf16[2,144,1536]{2,1,0:T(8,128)(2,1)}, bf16[2,144,1536]{2,1,0:T(8,128)(2,1)}, u32[]{:S(2)}, u32[]{:S(2)}) collective-permute-start(bf16[2,144,1536]{2,1,0:T(8,128)(2,1)} %stack.34), channel_id=1, source_target_pairs={{0,16},{1,17},{2,18},{3,19},{4,20},{5,21},{6,22},{7,23},{8,24},{9,... | collective-permute-start | bytes 2654216 | tf_op jit(solution)/shard_map/ppermute | solution.py:72
  390.0 28.8 %collective-permute-start.46 = (bf16[2304,256]{1,0:T(8,128)(2,1)}, bf16[2304,256]{1,0:T(8,128)(2,1)}, u32[]{:S(2)}, u32[]{:S(2)}) collective-permute-start(bf16[2304,256]{1,0:T(8,128)(2,1)} %pad_maximum_fusion.2), channel_id=1, source_target_pairs={{0,2},{1,3},{6,4},{7,5},{8,10},{9,11},{14,12},{15,13},{16,18},{17,... | collective-permute-start | bytes 3538952 | tf_op jit(solution)/shard_map/ppermute | solution.py:174
  397.2 29.2 %collective-permute-start.28 = (bf16[2304,256]{1,0:T(8,128)(2,1)S(1)}, bf16[2304,256]{1,0:T(8,128)(2,1)S(1)}, u32[]{:S(2)}, u32[]{:S(2)}) collective-permute-start(bf16[2304,256]{1,0:T(8,128)(2,1)S(1)} %copy-done.39), channel_id=1, source_target_pairs={{2,0},{3,1},{4,6},{5,7},{10,8},{11,9},{12,14},{13,15},{18,16},{19,... | collective-permute-start | bytes 3538952 | tf_op jit(solution)/shard_map/ppermute | solution.py:174
  398.7 28.0 %collective-permute-start.44 = (bf16[2304,256]{1,0:T(8,128)(2,1)S(1)}, bf16[2304,256]{1,0:T(8,128)(2,1)S(1)}, u32[]{:S(2)}, u32[]{:S(2)}) collective-permute-start(bf16[2304,256]{1,0:T(8,128)(2,1)S(1)} %copy-done.37), channel_id=1, source_target_pairs={{2,4},{3,5},{4,2},{5,3},{10,12},{11,13},{12,10},{13,11},{18,20},{1... | collective-permute-start | bytes 3538952 | tf_op jit(solution)/shard_map/ppermute | solution.py:174
  412.6 14.6 %collective-permute-start.36 = (bf16[1,144,1536]{2,1,0:T(8,128)(2,1)S(1)}, bf16[1,144,1536]{2,1,0:T(8,128)(2,1)S(1)}, u32[]{:S(2)}, u32[]{:S(2)}) collective-permute-start(bf16[1,144,1536]{2,1,0:T(8,128)(2,1)S(1)} %get-tuple-element.194), channel_id=1, source_target_pairs={{0,16},{1,17},{2,18},{3,19},{4,20},{5,21},{6,22},{7,23},{8,24},{9,... | collective-permute-start | bytes 1327112 | tf_op jit(solution)/shard_map/ppermute | solution.py:72
  420.4 37.9 %collective-permute-start.47 = (bf16[2304,256]{1,0:T(8,128)(2,1)S(1)}, bf16[2304,256]{1,0:T(8,128)(2,1)S(1)}, u32[]{:S(2)}, u32[]{:S(2)}) collective-permute-start(bf16[2304,256]{1,0:T(8,128)(2,1)S(1)} %add_convert_fusion.3), channel_id=1, source_target_pairs={{2,4},{3,5},{4,2},{5,3},{10,12},{11,13},{12,10},{13,11},{18,20},{1... | collective-permute-start | bytes 3538952 | tf_op jit(solution)/shard_map/ppermute | solution.py:174
  426.6 82.0 %collective-permute-start.49 = (bf16[2304,256]{1,0:T(8,128)(2,1)S(1)}, bf16[2304,256]{1,0:T(8,128)(2,1)S(1)}, u32[]{:S(2)}, u32[]{:S(2)}) collective-permute-start(bf16[2304,256]{1,0:T(8,128)(2,1)S(1)} %broadcast_select_fusion.2.refs_0_), channel_id=1, source_target_pairs={{0,1},{1,0},{2,3},{3,2},{4,5},{5,4},{6,7},{7,6},{8,9},{9,8},{10,11... | collective-permute-start | bytes 3538952 | tf_op jit(solution)/shard_map/ppermute | solution.py:72
  426.7 42.1 %collective-permute-start.35 = (bf16[1024,1024]{1,0:T(8,128)(2,1)S(1)}, bf16[1024,1024]{1,0:T(8,128)(2,1)S(1)}, u32[]{:S(2)}, u32[]{:S(2)}) collective-permute-start(bf16[1024,1024]{1,0:T(8,128)(2,1)S(1)} %slice.386), channel_id=1, source_target_pairs={{0,1},{1,0},{2,3},{3,2},{4,5},{5,4},{6,7},{7,6},{8,9},{9,8},{10,11... | collective-permute-start | bytes 6291464 | tf_op jit(solution)/shard_map/ppermute | solution.py:72
  433.4 13.3 %collective-permute-start.38 = (bf16[144,1536]{1,0:T(8,128)(2,1)S(1)}, bf16[144,1536]{1,0:T(8,128)(2,1)S(1)}, u32[]{:S(2)}, u32[]{:S(2)}) collective-permute-start(bf16[144,1536]{1,0:T(8,128)(2,1)S(1)} %get-tuple-element.192), channel_id=1, source_target_pairs={{0,2},{1,3},{6,4},{7,5},{8,10},{9,11},{14,12},{15,13},{16,18},{17,... | collective-permute-start | bytes 1327112 | tf_op jit(solution)/shard_map/ppermute | solution.py:174
  439.8 27.2 %collective-permute-start.45 = (bf16[2304,256]{1,0:T(8,128)(2,1)S(1)}, bf16[2304,256]{1,0:T(8,128)(2,1)S(1)}, u32[]{:S(2)}, u32[]{:S(2)}) collective-permute-start(bf16[2304,256]{1,0:T(8,128)(2,1)S(1)} %add_convert_fusion.4), channel_id=1, source_target_pairs={{2,0},{3,1},{4,6},{5,7},{10,8},{11,9},{12,14},{13,15},{18,16},{19,... | collective-permute-start | bytes 3538952 | tf_op jit(solution)/shard_map/ppermute | solution.py:174
  457.5 11.2 %collective-permute-start.39 = (bf16[144,1536]{1,0:T(8,128)(2,1)S(1)}, bf16[144,1536]{1,0:T(8,128)(2,1)S(1)}, u32[]{:S(2)}, u32[]{:S(2)}) collective-permute-start(bf16[144,1536]{1,0:T(8,128)(2,1)S(1)} %add_convert_fusion.33), channel_id=1, source_target_pairs={{2,4},{3,5},{4,2},{5,3},{10,12},{11,13},{12,10},{13,11},{18,20},{1... | collective-permute-start | bytes 1327112 | tf_op jit(solution)/shard_map/ppermute | solution.py:174
  458.3 36.7 %collective-permute-start.42 = (bf16[144,1536]{1,0:T(8,128)(2,1)S(1)}, bf16[144,1536]{1,0:T(8,128)(2,1)S(1)}, u32[]{:S(2)}, u32[]{:S(2)}) collective-permute-start(bf16[144,1536]{1,0:T(8,128)(2,1)S(1)} %add_convert_fusion.29), channel_id=1, source_target_pairs={{2,4},{3,5},{4,2},{5,3},{10,12},{11,13},{12,10},{13,11},{18,20},{1... | collective-permute-start | bytes 1327112 | tf_op jit(solution)/shard_map/ppermute | solution.py:174
  467.0 26.3 %collective-permute-start.48 = (bf16[2304,256]{1,0:T(8,128)(2,1)S(1)}, bf16[2304,256]{1,0:T(8,128)(2,1)S(1)}, u32[]{:S(2)}, u32[]{:S(2)}) collective-permute-start(bf16[2304,256]{1,0:T(8,128)(2,1)S(1)} %add_convert_fusion.2), channel_id=1, source_target_pairs={{2,0},{3,1},{4,6},{5,7},{10,8},{11,9},{12,14},{13,15},{18,16},{19,... | collective-permute-start | bytes 3538952 | tf_op jit(solution)/shard_map/ppermute | solution.py:174
  468.7 39.8 %collective-permute-start.50 = (bf16[2304,256]{1,0:T(8,128)(2,1)S(1)}, bf16[2304,256]{1,0:T(8,128)(2,1)S(1)}, u32[]{:S(2)}, u32[]{:S(2)}) collective-permute-start(bf16[2304,256]{1,0:T(8,128)(2,1)S(1)} %broadcast_select_fusion.1.refs_1_), channel_id=1, source_target_pairs={{0,1},{1,0},{2,3},{3,2},{4,5},{5,4},{6,7},{7,6},{8,9},{9,8},{10,11... | collective-permute-start | bytes 3538952 | tf_op jit(solution)/shard_map/ppermute | solution.py:72
  493.5 16.2 %collective-permute-start.51 = (bf16[2304,256]{1,0:T(8,128)(2,1)S(1)}, bf16[2304,256]{1,0:T(8,128)(2,1)S(1)}, u32[]{:S(2)}, u32[]{:S(2)}) collective-permute-start(bf16[2304,256]{1,0:T(8,128)(2,1)S(1)} %broadcast_select_fusion.refs_2_), channel_id=1, source_target_pairs={{0,1},{1,0},{2,3},{3,2},{4,5},{5,4},{6,7},{7,6},{8,9},{9,8},{10,11... | collective-permute-start | bytes 3538952 | tf_op jit(solution)/shard_map/ppermute | solution.py:72
  493.6 14.9 %collective-permute-start.40 = (bf16[144,1536]{1,0:T(8,128)(2,1)S(1)}, bf16[144,1536]{1,0:T(8,128)(2,1)S(1)}, u32[]{:S(2)}, u32[]{:S(2)}) collective-permute-start(bf16[144,1536]{1,0:T(8,128)(2,1)S(1)} %add_convert_fusion.32), channel_id=1, source_target_pairs={{2,0},{3,1},{4,6},{5,7},{10,8},{11,9},{12,14},{13,15},{18,16},{19,... | collective-permute-start | bytes 1327112 | tf_op jit(solution)/shard_map/ppermute | solution.py:174
  495.1 26.6 %collective-permute-start.43 = (bf16[144,1536]{1,0:T(8,128)(2,1)S(1)}, bf16[144,1536]{1,0:T(8,128)(2,1)S(1)}, u32[]{:S(2)}, u32[]{:S(2)}) collective-permute-start(bf16[144,1536]{1,0:T(8,128)(2,1)S(1)} %add_convert_fusion.28), channel_id=1, source_target_pairs={{2,0},{3,1},{4,6},{5,7},{10,8},{11,9},{12,14},{13,15},{18,16},{19,... | collective-permute-start | bytes 1327112 | tf_op jit(solution)/shard_map/ppermute | solution.py:174
  (72 other events, 635.5 us)
